TPU v7x, 32 devices: a whole 2x2x4 slice. The times are simulated.
32 devices in a mesh: batch: 8 (over z, x), blk: 4 (over y, core).
Axes of the slice: x: 2, y: 2, z: 4, core: 2. Of those that a mesh axis runs over, the one named last changes fastest.
Arguments:
- tokens: bfloat16 [16, 2048, 768], P('batch', 'blk'), may hold values from -6 to 6
- proj_weight: bfloat16 [768, 2304], P('batch', 'blk'), may hold values from -0.3125 to 0.3125
- out_weight: bfloat16 [768, 768], P('batch', 'blk'), may hold values from -0.875 to 0.875
- up_weight: bfloat16 [768, 3072], P('batch', 'blk'), may hold values from -0.21875 to 0.21875
- down_weight: bfloat16 [3072, 768], P('batch', 'blk'), may hold values from -0.109375 to 0.109375
- gain_one: bfloat16 [768], P('blk'), may hold values from 0.25 to 1.75
- bias_one: bfloat16 [768], P('blk'), may hold values from -3 to 3
- gain_two: bfloat16 [768], P('blk'), may hold values from 0.25 to 1.75
- bias_two: bfloat16 [768], P('blk'), may hold values from -3 to 3
- segments: int32 [16, 2048], P('batch', 'blk'), may hold values from 0 to 4, as said below
- present: int32 [16, 2048], P('batch', 'blk'), may hold values from 0 to 1, as said below
- cotangent: bfloat16 [16, 2048, 768], P('batch', 'blk'), may hold values from -6 to 6
Outputs:
- output: bfloat16 [16, 2048, 768], P('batch', 'blk')
- token_grad: bfloat16 [16, 2048, 768], P('batch', 'blk')
- proj_grad: float32 [768, 2304], P('batch', 'blk')
- out_grad: float32 [768, 768], P('batch', 'blk')
- up_grad: float32 [768, 3072], P('batch', 'blk')
- down_grad: float32 [3072, 768], P('batch', 'blk')
- gain_one_grad: float32 [768], P('blk')
- bias_one_grad: float32 [768], P('blk')
- gain_two_grad: float32 [768], P('blk')
- bias_two_grad: float32 [768], P('blk')
Inputs may be any that keep to these rules, and one draw needn't show every extreme that they name: `segments`: in every row the numbers never fall and the last token has 4; the tokens numbered 2 begin within the first half of 512 tokens of the row and end within its last half of 512 tokens. `present`: each row is 1 on a leading run and 0 on the rest, which lies inside clip 4 and holds fewer than a quarter of 512 tokens.
All inputs are finite; a program needn't handle non-finite values.
Results may differ from a plain program's by a relative error of at most 0.02.
Values may be sent and summed in bfloat16 or wider, within the bound.
A program may use at most 192 MiB of HBM per device.

v0:
```python
import jax
import jax.numpy as jnp
from jax import lax
from jax.sharding import PartitionSpec as P

HEADS = 12
HEAD_DIM = 64


epsilon = 1e-05
masked_score = -1e30


def passed_along(value, axis, steps):
    count = lax.axis_size(axis)
    pairs = [(source, (source + steps) % count) for source in range(count)]
    return lax.ppermute(value, axis, pairs)


def from_behind(value, axis, steps):
    count = lax.axis_size(axis)
    initial, last = (max(0, -steps), min(count, count - steps))
    return lax.ppermute(value, axis, [(source, source + steps) for source in range(initial, last)])


def layer_norm(values, gain, shift):
    average = jnp.mean(values, axis=-1, keepdims=True)
    centered = values - average
    variance = jnp.mean(centered * centered, axis=-1, keepdims=True)
    return centered * lax.rsqrt(variance + epsilon) * gain + shift


def gelu_tanh(values):
    return jax.nn.gelu(values, approximate=True)


def contract(left, right, left_dim, right_dim):
    return lax.dot_general(
        left, right, (((left_dim,), (right_dim,)), ((), ())), preferred_element_type=jnp.float32
    )


def visible_mask(query_pos, query_tags, key_start, row_tags, count):
    key_pos = key_start + jnp.arange(count, dtype=jnp.int32)
    key_tags = lax.dynamic_slice_in_dim(row_tags, key_start, count, 1)
    causal = key_pos[None, :] <= query_pos[:, None]
    same = key_tags[:, None, :] == query_tags[:, :, None]
    return jnp.logical_and(causal[None], same)


def attend_block(state, queries, keys_flat, values_flat, visible):
    maxima, totals, accum = state
    rows, count = (keys_flat.shape[0], keys_flat.shape[1])
    keys = keys_flat.reshape(rows, count, HEADS, HEAD_DIM)
    values = values_flat.reshape(rows, count, HEADS, HEAD_DIM)
    scores = jnp.einsum(
        "rqhd,rkhd->rhqk", queries, keys, preferred_element_type=jnp.float32
    ) * HEAD_DIM ** (-0.5)
    scores = jnp.where(visible[:, None], scores, masked_score)
    new_max = jnp.maximum(maxima, jnp.max(scores, axis=-1))
    weights = jnp.where(visible[:, None], jnp.exp(scores - new_max[..., None]), 0.0)
    factor = jnp.exp(maxima - new_max)
    totals = totals * factor + jnp.sum(weights, axis=-1)
    accum = accum * factor[..., None] + jnp.einsum(
        "rhqk,rkhd->rhqd", weights.astype(jnp.bfloat16), values, preferred_element_type=jnp.float32
    )
    return (new_max, totals, accum)


def body(
    tokens,
    proj_weight,
    out_weight,
    up_weight,
    down_weight,
    gain_one,
    bias_one,
    gain_two,
    bias_two,
    segments,
    present,
    cotangent,
):
    rows, block, width = tokens.shape
    span = lax.axis_size("blk")
    index = lax.axis_index("blk")
    scale = HEAD_DIM ** (-0.5)
    query_start = index * block
    query_pos = query_start + jnp.arange(block, dtype=jnp.int32)
    local_tags = jnp.where(present == 1, segments, -1 - query_pos[None, :])
    row_tags = lax.all_gather(local_tags, "blk", axis=1, tiled=True)
    proj_wide, out_wide, up_wide, down_wide, gain_a, bias_a, gain_b, bias_b = (
        lax.all_gather(proj_weight, "blk", axis=1, tiled=True),
        lax.all_gather(out_weight, "blk", axis=1, tiled=True),
        lax.all_gather(up_weight, "blk", axis=1, tiled=True),
        lax.all_gather(down_weight, "blk", axis=1, tiled=True),
        lax.all_gather(gain_one, "blk", axis=0, tiled=True),
        lax.all_gather(bias_one, "blk", axis=0, tiled=True),
        lax.all_gather(gain_two, "blk", axis=0, tiled=True),
        lax.all_gather(bias_two, "blk", axis=0, tiled=True),
    )
    proj_full, out_full, up_full, down_full = (
        lax.all_gather(proj_wide, "batch", axis=0, tiled=True),
        lax.all_gather(out_wide, "batch", axis=0, tiled=True),
        lax.all_gather(up_wide, "batch", axis=0, tiled=True),
        lax.all_gather(down_wide, "batch", axis=0, tiled=True),
    )
    gain_a = gain_a.astype(jnp.float32)
    bias_a = bias_a.astype(jnp.float32)
    gain_b = gain_b.astype(jnp.float32)
    bias_b = bias_b.astype(jnp.float32)
    inputs = tokens.reshape(rows * block, width).astype(jnp.float32)
    normed_low = layer_norm(inputs, gain_a, bias_a).astype(jnp.bfloat16)
    projected = jnp.dot(normed_low, proj_full, preferred_element_type=jnp.float32).astype(
        jnp.bfloat16
    )
    projected = projected.reshape(rows, block, 3 * width)
    queries_flat = projected[:, :, :width]
    keys_flat = projected[:, :, width : 2 * width]
    values_flat = projected[:, :, 2 * width :]
    queries = queries_flat.reshape(rows, block, HEADS, HEAD_DIM)
    initial = (
        jnp.full((rows, HEADS, block), masked_score, jnp.float32),
        jnp.zeros((rows, HEADS, block), jnp.float32),
        jnp.zeros((rows, HEADS, block, HEAD_DIM), jnp.float32),
    )
    key_all = lax.all_gather(keys_flat, "blk", axis=1, tiled=True)
    value_all = lax.all_gather(values_flat, "blk", axis=1, tiled=True)
    steps = key_all.shape[1] // block

    def one(step, inner):
        offset = step * block
        keys_here = lax.dynamic_slice_in_dim(key_all, offset, block, 1)
        values_here = lax.dynamic_slice_in_dim(value_all, offset, block, 1)

        def one_work(current):
            visible = visible_mask(query_pos, local_tags, offset, row_tags, block)
            return attend_block(current, queries, keys_here, values_here, visible)

        return lax.cond(offset <= query_start, one_work, lambda current: current, inner)

    state = lax.fori_loop(0, steps, one, initial)
    maxima, totals, accum = state
    log_total = maxima + jnp.log(totals)
    attended = (accum / totals[..., None]).transpose(0, 2, 1, 3)
    attended_low = attended.reshape(rows * block, width).astype(jnp.bfloat16)
    middle = inputs + jnp.dot(attended_low, out_full, preferred_element_type=jnp.float32)
    normed_two_low = layer_norm(middle, gain_b, bias_b).astype(jnp.bfloat16)
    hidden = jnp.dot(normed_two_low, up_full, preferred_element_type=jnp.float32)
    activated_low = gelu_tanh(hidden).astype(jnp.bfloat16)
    output = middle + jnp.dot(activated_low, down_full, preferred_element_type=jnp.float32)
    proj_back, out_back, up_back, down_back = (
        lax.all_gather(proj_weight, "blk", axis=1, tiled=True),
        lax.all_gather(out_weight, "blk", axis=1, tiled=True),
        lax.all_gather(up_weight, "blk", axis=1, tiled=True),
        lax.all_gather(down_weight, "blk", axis=1, tiled=True),
    )
    proj_use, out_use, up_use, down_use = (
        lax.all_gather(proj_back, "batch", axis=0, tiled=True),
        lax.all_gather(out_back, "batch", axis=0, tiled=True),
        lax.all_gather(up_back, "batch", axis=0, tiled=True),
        lax.all_gather(down_back, "batch", axis=0, tiled=True),
    )
    grad_out = cotangent.reshape(rows * block, width)
    down_grad = contract(activated_low, grad_out, 0, 0)
    grad_act = contract(grad_out, down_use, 1, 1)
    unused_value, gelu_back = jax.vjp(gelu_tanh, hidden)
    grad_hidden = gelu_back(grad_act)[0].astype(jnp.bfloat16)
    up_grad = contract(normed_two_low, grad_hidden, 0, 0)
    grad_normed_two = contract(grad_hidden, up_use, 1, 1)
    unused_norm, norm_two_back = jax.vjp(layer_norm, middle, gain_b, bias_b)
    grad_middle_part, gain_two_grad, bias_two_grad = norm_two_back(grad_normed_two)
    grad_middle = grad_out.astype(jnp.float32) + grad_middle_part
    grad_middle_low = grad_middle.astype(jnp.bfloat16)
    out_grad = contract(attended_low, grad_middle_low, 0, 0)
    grad_attended = contract(grad_middle_low, out_use, 1, 1).astype(jnp.bfloat16)
    grad_heads = grad_attended.reshape(rows, block, HEADS, HEAD_DIM)
    delta = jnp.sum(grad_heads.astype(jnp.float32) * attended, axis=-1).transpose(0, 2, 1)

    def grad_block(held_keys, held_values, visible):
        keys = held_keys.reshape(rows, block, HEADS, HEAD_DIM)
        values = held_values.reshape(rows, block, HEADS, HEAD_DIM)
        scores = (
            jnp.einsum("rqhd,rkhd->rhqk", queries, keys, preferred_element_type=jnp.float32) * scale
        )
        probs = jnp.where(visible[:, None], jnp.exp(scores - log_total[..., None]), 0.0)
        probs_low = probs.astype(jnp.bfloat16)
        value_grad = jnp.einsum(
            "rhqk,rqhd->rkhd", probs_low, grad_heads, preferred_element_type=jnp.float32
        )
        prob_grad = jnp.einsum(
            "rqhd,rkhd->rhqk", grad_heads, values, preferred_element_type=jnp.float32
        )
        score_grad = (probs * (prob_grad - delta[..., None])).astype(jnp.bfloat16)
        query_part = (
            jnp.einsum("rhqk,rkhd->rqhd", score_grad, keys, preferred_element_type=jnp.float32)
            * scale
        )
        key_part = (
            jnp.einsum("rhqk,rqhd->rkhd", score_grad, queries, preferred_element_type=jnp.float32)
            * scale
        )
        term = jnp.concatenate(
            [key_part.reshape(rows, block, width), value_grad.reshape(rows, block, width)], axis=2
        )
        return (query_part, term)

    def visit(step, held_keys, held_values, travel, query_grad):
        anchor = (index - step) % span
        key_start = anchor * block

        def visit_work(inner):
            current_query, current_travel = inner
            visible = visible_mask(query_pos, local_tags, key_start, row_tags, block)
            query_part, term = grad_block(held_keys, held_values, visible)
            return (current_query + query_part, current_travel + term)

        return lax.cond(anchor <= index, visit_work, lambda inner: inner, (query_grad, travel))

    def pass_grads(travel):
        return passed_along(travel.astype(jnp.bfloat16), "blk", 1).astype(travel.dtype)

    travel_zero = jnp.zeros((rows, block, 2 * width), jnp.float32)
    query_zero = jnp.zeros((rows, block, HEADS, HEAD_DIM), jnp.float32)

    def turn(step, carry):
        held_keys, held_values, travel, query_grad = carry
        query_grad, travel = visit(step, held_keys, held_values, travel, query_grad)
        held_keys, held_values = from_behind((held_keys, held_values), "blk", 1)
        return (held_keys, held_values, pass_grads(travel), query_grad)

    held_keys, held_values, travel, query_grad = lax.fori_loop(
        0, span - 1, turn, (keys_flat, values_flat, travel_zero, query_zero)
    )
    query_grad, travel = visit(span - 1, held_keys, held_values, travel, query_grad)
    travel = pass_grads(travel)
    proj_grad_low = jnp.concatenate(
        [query_grad.reshape(rows, block, width), travel], axis=2
    ).astype(jnp.bfloat16)
    proj_grad_low = proj_grad_low.reshape(rows * block, 3 * width)
    proj_grad = contract(normed_low, proj_grad_low, 0, 0)
    grad_normed = contract(proj_grad_low, proj_use, 1, 1)
    unused_first, norm_one_back = jax.vjp(layer_norm, inputs, gain_a, bias_a)
    grad_inputs_part, gain_one_grad, bias_one_grad = norm_one_back(grad_normed)
    token_grad = (grad_middle + grad_inputs_part).astype(jnp.bfloat16)
    proj_part, out_part, up_part, down_part, gain_a_sum, bias_a_sum, gain_b_sum, bias_b_sum = (
        lax.psum_scatter(
            proj_grad.astype(jnp.bfloat16), "blk", scatter_dimension=1, tiled=True
        ).astype(jnp.float32),
        lax.psum_scatter(
            out_grad.astype(jnp.bfloat16), "blk", scatter_dimension=1, tiled=True
        ).astype(jnp.float32),
        lax.psum_scatter(
            up_grad.astype(jnp.bfloat16), "blk", scatter_dimension=1, tiled=True
        ).astype(jnp.float32),
        lax.psum_scatter(
            down_grad.astype(jnp.bfloat16), "blk", scatter_dimension=1, tiled=True
        ).astype(jnp.float32),
        lax.psum_scatter(
            gain_one_grad.astype(jnp.bfloat16), "blk", scatter_dimension=0, tiled=True
        ).astype(jnp.float32),
        lax.psum_scatter(
            bias_one_grad.astype(jnp.bfloat16), "blk", scatter_dimension=0, tiled=True
        ).astype(jnp.float32),
        lax.psum_scatter(
            gain_two_grad.astype(jnp.bfloat16), "blk", scatter_dimension=0, tiled=True
        ).astype(jnp.float32),
        lax.psum_scatter(
            bias_two_grad.astype(jnp.bfloat16), "blk", scatter_dimension=0, tiled=True
        ).astype(jnp.float32),
    )
    proj_sum, out_sum, up_sum, down_sum = (
        lax.psum_scatter(
            proj_part.astype(jnp.bfloat16), "batch", scatter_dimension=0, tiled=True
        ).astype(jnp.float32),
        lax.psum_scatter(
            out_part.astype(jnp.bfloat16), "batch", scatter_dimension=0, tiled=True
        ).astype(jnp.float32),
        lax.psum_scatter(
            up_part.astype(jnp.bfloat16), "batch", scatter_dimension=0, tiled=True
        ).astype(jnp.float32),
        lax.psum_scatter(
            down_part.astype(jnp.bfloat16), "batch", scatter_dimension=0, tiled=True
        ).astype(jnp.float32),
    )
    gain_a_total, bias_a_total, gain_b_total, bias_b_total = lax.psum(
        (gain_a_sum, bias_a_sum, gain_b_sum, bias_b_sum), "batch"
    )
    return (
        output.reshape(rows, block, width).astype(jnp.bfloat16),
        token_grad.reshape(rows, block, width),
        proj_sum,
        out_sum,
        up_sum,
        down_sum,
        gain_a_total,
        bias_a_total,
        gain_b_total,
        bias_b_total,
    )


def solution(mesh):
    in_specs = (
        P("batch", "blk", None),
        P("batch", "blk"),
        P("batch", "blk"),
        P("batch", "blk"),
        P("batch", "blk"),
        P("blk"),
        P("blk"),
        P("blk"),
        P("blk"),
        P("batch", "blk"),
        P("batch", "blk"),
        P("batch", "blk", None),
    )
    out_specs = (
        P("batch", "blk", None),
        P("batch", "blk", None),
        P("batch", "blk"),
        P("batch", "blk"),
        P("batch", "blk"),
        P("batch", "blk"),
        P("blk"),
        P("blk"),
        P("blk"),
        P("blk"),
    )
    return jax.shard_map(body, mesh=mesh, in_specs=in_specs, out_specs=out_specs, check_vma=False)
```

profile of v0, /device:TPU:0, one launch (start us, length us, event | category | flops | bytes accessed | tf_op | source)
XLA Modules:
  0.0 1247.3 jit_solution(3414099360909492144)
XLA Ops:
  7.2 8.8 all-gather
  22.9 6.8 all-reduce.10
  32.5 51.2 %all-gather.8.cloned.1.call-done = bf16[768,2304]{1,0:T(8,128)(2,1)} async-done(((bf16[96,2304]{1,0:T(8,128)(2,1)}), bf16[768,2304]{1,0:T(8,128)(2,1)}) %all-gather.8.cloned.1.call-update) | async-done | bytes 3538960 | tf_op jit(solution)/shard_map/all_gather | solution.py:103
  83.7 6.0 convolution_convert_fusion
  95.7 5.6 all_gather.60
  102.2 11.6 all_gather.64
  113.9 11.6 all_gather.66
  126.8 5.4 all_gather.53
  133.0 12.3 all-gather.12.cloned.1.call-done
  145.2 48.0 %all-gather.10.cloned.1.call-done = bf16[2,2048,768]{1,2,0:T(8,128)(2,1)} async-done(((bf16[2,512,768]{1,2,0:T(8,128)(2,1)}), bf16[2,2048,768]{1,2,0:T(8,128)(2,1)}) %all-gather.10.cloned.1.call-update) | async-done | bytes 6291472 | tf_op jit(solution)/shard_map/all_gather | solution.py:127
  195.3 38.3 %while.42 = (s32[]{:T(128)}, f32[2,12,512]{2,1,0:T(8,128)S(1)}, f32[2,12,512]{2,1,0:T(8,128)S(1)}, f32[2,12,512,64]{2,3,1,0:T(8,128)}, s32[]{:T(128)}, /*index=5...) while((s32[]{:T(128)}, f32[2,12,512]{2,1,0:T(8,128)S(1)}, ...), condition=%wide.region_7.8_spmd.clone.clone, body=%wide.region_2.7_spmd.clone.clone.sunk | while | flops 1695310848 | bytes 121401736 | solution.py:142
  195.3 38.3 %conditional.10 = ((f32[2,12,512]{2,1,0:T(8,128)S(1)}, f32[2,12,512]{2,1,0:T(8,128)S(1)}, f32[2,12,512,64]{2,3,1,0:T(8,128)})) conditional(s32[]{:T(128)} %convert_element_type.308, (f32[2,12,512]{2,1,0:T(8,128)S(1)}, f32[2,12,512]{2,1,0:T(8,128)S(1)}, f32[2,12,512,64]{2,3,1,0:T(8,128)}) %tuple.167, (s32[]{:T(128)}, s32[]{:T(128)}, ...), branch_computations={%region_3.3_spmd, %region_4.6_spmd} | conditional | flops 1695310848 | bytes 121399432 | solution.py:140
  198.2 10.5 fusion.4
  208.7 11.6 fusion.6
  220.4 11.6 multiply_add_fusion
  233.7 7.9 bitcast_convert_fusion
  249.0 68.6 %all-gather.16.cloned.1.call-done = bf16[768,3072]{1,0:T(8,128)(2,1)} async-done(((bf16[96,3072]{1,0:T(8,128)(2,1)}), bf16[768,3072]{1,0:T(8,128)(2,1)}) %all-gather.16.cloned.1.call-update) | async-done | bytes 4718608 | tf_op jit(solution)/shard_map/all_gather | solution.py:105
  317.6 11.1 fusion.56
  328.8 70.0 %all-gather.18.cloned.1.call-done = bf16[3072,768]{0,1:T(8,128)(2,1)} async-done(((bf16[384,768]{0,1:T(8,128)(2,1)}), bf16[3072,768]{0,1:T(8,128)(2,1)}) %all-gather.18.cloned.1.call-update) | async-done | bytes 4718608 | tf_op jit(solution)/shard_map/all_gather | solution.py:106
  398.7 15.0 %fusion.36 = bf16[1024,3072]{1,0:T(8,128)(2,1)S(1)} fusion(f32[1024,3072]{1,0:T(8,128)} %fusion.56, bf16[1024,768]{1,0:T(8,128)(2,1)S(1)} %bitcast.157, bf16[3072,768]{0,1:T(8,128)(2,1)} %all-gather.18.cloned.1.call-done), kind=kOutput, calls=%fused_computation.63 | convolution fusion | flops 4894752768 | bytes 25165824 | tf_op jit(solution)/shard_map/dot_general | solution.py:38
  413.8 6.1 multiply_reduce_fusion
  427.0 10.1 convolution_convert_fusion.1
  437.2 10.6 convolution_convert_fusion.2
  463.8 389.8 %while.41 = (s32[]{:T(128)}, bf16[2,512,768]{1,2,0:T(8,128)(2,1)}, bf16[2,512,768]{1,2,0:T(8,128)(2,1)}, f32[2,512,1536]{1,2,0:T(8,128)}, f32[2,512,12,64]{1,3,2...) while((s32[]{:T(128)}, bf16[2,512,768]{1,2,0:T(8,128)(2,1)}, ...), condition=%wide.region_16.17_spmd.clone, body=%wide.region_13.0_spmd.clone.sunk | while | flops 4100981760 | bytes 302690976 | solution.py:232
  472.1 67.0 %conditional.9 = ((f32[2,512,12,64]{1,3,2,0:T(8,128)}, f32[2,512,1536]{1,2,0:T(8,128)})) conditional(s32[]{:T(128)} %convert_element_type.305, (f32[2,512,12,64]{1,3,2,0:T(8,128)}, f32[2,512,1536]{1,2,0:T(8,128)}) %tuple.164, (s32[]{:T(128)}, s32[]{:T(128)}, s32[2,2048]{1,0:T(2,128)S(1)}, s32[2,512]{1,0:T(2,128)S(1)}, ...), branch_computations={%region_14.14_spmd, %region_15.15_spmd} | conditional | flops 4096263168 | bytes 214608000 | solution.py:218
  472.8 10.2 fusion.62
  483.1 12.2 fusion.16
  495.2 13.2 %multiply_convert_fusion = bf16[2,12,512,512]{3,2,1,0:T(8,128)(2,1)S(1)} fusion(f32[2,12,512,512]{3,2,1,0:T(8,128)} %fusion.62, f32[2,12,512]{2,1,0:T(8,128)S(1)} %get-tuple-element.712, f32[2,12,512]{2,1,0:T(8,128)S(1)} %get-tuple-element.709, pred[2,512,512]{2,1,0:T(8,128)(4,1)S(1)} %compare_and_fusion.1, bf16[2,512,12,64]{1,3,2,0:T(8,128)(2,1)S(1)} %copy-done.18, ...), kind=kOutput, calls=%fused_computation.22 | convolution fusion | flops 843055104 | bytes 41517056 | tf_op jit(solution)/shard_map/while/body/eval_jaxpr/cond/branch_1_fun/rqhd,rkhd->rhqk/dot_general | solution.py:191
  508.5 6.3 copy-done
  518.6 11.7 bitcast_add_fusion
  530.2 8.9 maximum_add_fusion
  550.7 33.7 %collective-permute-done.2 = bf16[2,512,1536]{1,2,0:T(8,128)(2,1)} collective-permute-done((bf16[2,512,1536]{1,2,0:T(8,128)(2,1)}, bf16[2,512,1536]{1,2,0:T(8,128)(2,1)}, u32[]{:S(2)}, u32[]{:S(2)}) %collective-permute-start.2) | collective-permute-done | bytes 3145760 | tf_op jit(solution)/shard_map/while/body/eval_jaxpr/ppermute | solution.py:17
  602.4 90.3 %collective-permute-start.2 = (bf16[2,512,1536]{1,2,0:T(8,128)(2,1)}, bf16[2,512,1536]{1,2,0:T(8,128)(2,1)}, u32[]{:S(2)}, u32[]{:S(2)}) collective-permute-start(bf16[2,512,1536]{1,2,0:T(8,128)(2,1)} %convert_element_type.306), channel_id=1, source_target_pairs={{0,1},{1,2},{2,3},{3,0},{4,5},{5,6},{6,7},{7,4},{8,9},{9,10},{10,1... | collective-permute-start | bytes 9437192 | tf_op jit(solution)/shard_map/while/body/eval_jaxpr/ppermute | solution.py:17
  692.7 5.6 collective-permute-start
  719.0 57.0 %collective-permute-start.2 = (bf16[2,512,1536]{1,2,0:T(8,128)(2,1)}, bf16[2,512,1536]{1,2,0:T(8,128)(2,1)}, u32[]{:S(2)}, u32[]{:S(2)}) collective-permute-start(bf16[2,512,1536]{1,2,0:T(8,128)(2,1)} %convert_element_type.306), channel_id=1, source_target_pairs={{0,1},{1,2},{2,3},{3,0},{4,5},{5,6},{6,7},{7,4},{8,9},{9,10},{10,1... | collective-permute-start | bytes 9437192 | tf_op jit(solution)/shard_map/while/body/eval_jaxpr/ppermute | solution.py:17
  776.0 69.6 %collective-permute-start = (bf16[2,512,768]{1,2,0:T(8,128)(2,1)S(1)}, bf16[2,512,768]{1,2,0:T(8,128)(2,1)}, u32[]{:S(2)}, u32[]{:S(2)}) collective-permute-start(bf16[2,512,768]{1,2,0:T(8,128)(2,1)S(1)} %copy.142), channel_id=1, source_target_pairs={{0,1},{1,2},{2,3},{4,5},{5,6},{6,7},{8,9},{9,10},{10,11},{12,13},{... | collective-permute-start | bytes 4718600 | tf_op jit(solution)/shard_map/while/body/eval_jaxpr/ppermute | solution.py:23
  859.9 5.6 copy.83
  865.5 57.3 %collective-permute-start.3 = (bf16[2,512,1536]{2,1,0:T(8,128)(2,1)}, bf16[2,512,1536]{2,1,0:T(8,128)(2,1)}, u32[]{:S(2)}, u32[]{:S(2)}) collective-permute-start(bf16[2,512,1536]{2,1,0:T(8,128)(2,1)} %copy.83), channel_id=1, source_target_pairs={{0,1},{1,2},{2,3},{3,0},{4,5},{5,6},{6,7},{7,4},{8,9},{9,10},{10,1... | collective-permute-start | bytes 9437192 | tf_op jit(solution)/shard_map/ppermute | solution.py:17
  924.8 42.1 %collective-permute-done.3 = bf16[2,512,1536]{2,1,0:T(8,128)(2,1)} collective-permute-done((bf16[2,512,1536]{2,1,0:T(8,128)(2,1)}, bf16[2,512,1536]{2,1,0:T(8,128)(2,1)}, u32[]{:S(2)}, u32[]{:S(2)}) %collective-permute-start.3) | collective-permute-done | bytes 3145760 | tf_op jit(solution)/shard_map/ppermute | solution.py:17
  966.8 7.5 convolution_convert_fusion.3
  978.1 13.3 %add_convert_fusion.1 = bf16[1024,768]{1,0:T(8,128)(2,1)} fusion(f32[1024,768]{1,0:T(8,128)} %copy-done.8, bf16[3072,768]{0,1:T(8,128)(2,1)} %all-gather.18.cloned.1.call-done, f32[1024,3072]{1,0:T(8,128)} %fusion.56), kind=kOutput, calls=%fused_computation.95 | convolution fusion | flops 4861722624 | bytes 22020096 | tf_op jit(solution)/shard_map/dot_general | solution.py:151
  996.8 40.6 %reduce-scatter.15.cloned.1.call-done = bf16[768,576]{0,1:T(8,128)(2,1)} async-done(((bf16[768,2304]{0,1:T(8,128)(2,1)}), bf16[768,576]{0,1:T(8,128)(2,1)}) %reduce-scatter.15.cloned.1.call-update) | async-done | bytes 884752 | tf_op jit(solution)/shard_map/reduce_scatter | solution.py:247
  1039.7 7.1 fusion.57
  1050.1 5.8 all-reduce.9
  1056.1 22.3 %all-reduce.8 = (f32[192]{0:T(256)}, f32[192]{0:T(256)}, f32[192]{0:T(256)}, f32[192]{0:T(256)}) all-reduce(f32[192]{0:T(256)S(1)} %get-tuple-element.1123, f32[192]{0:T(256)S(1)} %get-tuple-element.1122, f32[192]{0:T(256)S(1)} %get-tuple-element.1121, f32[192]{0:T(256)S(1)} %get-tuple-element.1120), channel_id=1, replica_groups=mesh['batch'=8,'blk'=4] {'batch'}, use_global_device_ids=true, to_apply=%region_31.32 | all-reduce | flops 768 | bytes 6144 | tf_op jit(solution)/shard_map/psum | solution.py:286
  1083.0 22.6 %reduce-scatter.29.cloned.1.call-done = bf16[384,192]{1,0:T(8,128)(2,1)} async-done(((bf16[3072,192]{1,0:T(8,128)(2,1)}), bf16[384,192]{1,0:T(8,128)(2,1)}) %reduce-scatter.29.cloned.1.call-update) | async-done | bytes 147472
  1107.4 65.0 %reduce-scatter.21.cloned.1.call-done = bf16[96,768]{1,0:T(8,128)(2,1)} async-done(((bf16[768,768]{1,0:T(8,128)(2,1)}), bf16[96,768]{1,0:T(8,128)(2,1)}) %reduce-scatter.21.cloned.1.call-update) | async-done | bytes 147472 | tf_op jit(solution)/shard_map/reduce_scatter | solution.py:279
  1174.1 64.4 %reduce-scatter.25.cloned.1.call-done = bf16[96,576]{1,0:T(8,128)(2,1)} async-done(((bf16[768,576]{1,0:T(8,128)(2,1)}), bf16[96,576]{1,0:T(8,128)(2,1)}) %reduce-scatter.25.cloned.1.call-update) | async-done | bytes 110608
  (257 shorter events, 162.3 us)
Async XLA Ops:
  7.2 22.5 %copy-start.2 = (bf16[2,512,768]{2,1,0:T(8,128)(2,1)S(1)}, bf16[2,512,768]{2,1,0:T(8,128)(2,1)}, u32[]{:S(2)}) copy-start(bf16[2,512,768]{2,1,0:T(8,128)(2,1)} %param.22) | copy-start | bytes 4718596
  7.2 76.5 %all-gather.8.cloned.1.call-start = ((), (), s32[]{:S(2)}) async-start(), calls=%async_computation.8 | async-start | bytes 3981312 | tf_op jit(solution)/shard_map/all_gather | solution.py:103
  17.5 127.7 %all-gather.12.cloned.1.call-start = ((), (), s32[]{:S(2)}) async-start(), calls=%async_computation.10 | async-start | bytes 7864320 | tf_op jit(solution)/shard_map/all_gather | solution.py:128
  32.5 57.2 %copy-start.16 = (bf16[1024,768]{1,0:T(8,128)(2,1)}, bf16[1024,768]{1,0:T(8,128)(2,1)S(1)}, u32[]{:S(2)}) copy-start(bf16[1024,768]{1,0:T(8,128)(2,1)S(1)} %fusion.44) | copy-start | bytes 4718596
  93.8 8.4 copy-start.25
  93.8 99.4 %all-gather.10.cloned.1.call-start = ((), (), s32[]{:S(2)}) async-start(), calls=%async_computation.9 | async-start | bytes 7864320 | tf_op jit(solution)/shard_map/all_gather | solution.py:127
  93.9 20.0 %copy-start.26 = (bf16[384,192]{0,1:T(8,128)(2,1)S(1)}, bf16[384,192]{0,1:T(8,128)(2,1)}, u32[]{:S(2)}) copy-start(bf16[384,192]{0,1:T(8,128)(2,1)} %param.26) | copy-start | bytes 442372
  95.5 31.3 %copy-start.40 = (s32[2,512]{1,0:T(2,128)S(1)}, s32[2,512]{1,0:T(2,128)}, u32[]{:S(2)}) copy-start(s32[2,512]{1,0:T(2,128)} %param.31) | copy-start | bytes 12292
  95.5 31.3 %copy-start.41 = (s32[2,512]{1,0:T(2,128)S(1)}, s32[2,512]{1,0:T(2,128)}, u32[]{:S(2)}) copy-start(s32[2,512]{1,0:T(2,128)} %param.32) | copy-start | bytes 12292
  95.5 147.7 %all-gather.14.cloned.1.call-start = ((), (), s32[]{:S(2)}) async-start(), calls=%async_computation.11 | async-start | bytes 1327104 | tf_op jit(solution)/shard_map/all_gather | solution.py:104
  102.1 215.5 %all-gather.16.cloned.1.call-start = ((), (), s32[]{:S(2)}) async-start(), calls=%async_computation.12 | async-start | bytes 5308416 | tf_op jit(solution)/shard_map/all_gather | solution.py:105
  113.9 284.9 %all-gather.18.cloned.1.call-start = ((), (), s32[]{:S(2)}) async-start(), calls=%async_computation.13 | async-start | bytes 5308416 | tf_op jit(solution)/shard_map/all_gather | solution.py:106
  125.6 797.2 %reduce-scatter.17.cloned.1.call-start = ((), (), s32[]{:S(2)}) async-start(), calls=%async_computation.15 | async-start | bytes 1474560 | tf_op jit(solution)/shard_map/reduce_scatter | solution.py:250
  208.7 11.6 copy-start.12
  246.6 71.0 %copy-start.38 = (f32[768]{0:T(1024)S(1)}, f32[768]{0:T(1024)}, u32[]{:S(2)}) copy-start(f32[768]{0:T(1024)} %convert_element_type.195) | copy-start | bytes 9220
  246.7 71.0 %copy-start.42 = (f32[768]{0:T(1024)S(1)}, f32[768]{0:T(1024)}, u32[]{:S(2)}) copy-start(f32[768]{0:T(1024)} %convert_element_type.196) | copy-start | bytes 9220
  249.0 149.7 %copy-start.14 = (bf16[2,512,768]{2,1,0:T(8,128)(2,1)S(1)}, bf16[2,512,768]{2,1,0:T(8,128)(2,1)}, u32[]{:S(2)}) copy-start(bf16[2,512,768]{2,1,0:T(8,128)(2,1)} %param.33) | copy-start | bytes 4718596
  398.7 15.0 %copy-start.9 = (f32[1024,768]{1,0:T(8,128)S(1)}, f32[1024,768]{1,0:T(8,128)}, u32[]{:S(2)}) copy-start(f32[1024,768]{1,0:T(8,128)} %copy-done.8) | copy-start | bytes 9437188
  398.7 15.0 %copy-start.45 = (bf16[768,3072]{1,0:T(8,128)(2,1)S(1)}, bf16[768,3072]{1,0:T(8,128)(2,1)}, u32[]{:S(2)}) copy-start(bf16[768,3072]{1,0:T(8,128)(2,1)} %all-gather.16.cloned.1.call-done) | copy-start | bytes 14155780
  427.0 547.5 %reduce-scatter.23.cloned.1.call-start = ((), (), s32[]{:S(2)}) async-start(), calls=%async_computation.18 | async-start | bytes 5898240 | tf_op jit(solution)/shard_map/reduce_scatter | solution.py:256
  437.1 540.6 %reduce-scatter.19.cloned.1.call-start = ((), (), s32[]{:S(2)}) async-start(), calls=%async_computation.16 | async-start | bytes 5898240 | tf_op jit(solution)/shard_map/reduce_scatter | solution.py:253
  447.8 547.3 %reduce-scatter.27.cloned.1.call-start = ((), (), s32[]{:S(2)}) async-start(), calls=%async_computation.20 | async-start | bytes 442368
  463.8 389.8 %copy-start.24 = (f32[2,512,12]{1,0,2:T(2,128)S(1)}, f32[2,512,12]{1,0,2:T(2,128)}, u32[]{:S(2)}) copy-start(f32[2,512,12]{1,0,2:T(2,128)} %copy-done.23) | copy-start | bytes 147460
  463.8 389.9 %copy-start.39 = (s32[512]{0:T(512)S(1)}, s32[512]{0:T(512)}, u32[]{:S(2)}) copy-start(s32[512]{0:T(512)} %iota_add_fusion.3) | copy-start | bytes 6148
  472.8 10.2 copy-start.18
  544.1 40.3 %collective-permute-start.2 = (bf16[2,512,1536]{1,2,0:T(8,128)(2,1)}, bf16[2,512,1536]{1,2,0:T(8,128)(2,1)}, u32[]{:S(2)}, u32[]{:S(2)}) collective-permute-start(bf16[2,512,1536]{1,2,0:T(8,128)(2,1)} %convert_element_type.306), channel_id=1, source_target_pairs={{0,1},{1,2},{2,3},{3,0},{4,5},{5,6},{6,7},{7,4},{8,9},{9,10},{10,1... | collective-permute-start | bytes 9437192 | tf_op jit(solution)/shard_map/while/body/eval_jaxpr/ppermute | solution.py:17
  544.1 45.7 %collective-permute-start = (bf16[2,512,768]{1,2,0:T(8,128)(2,1)S(1)}, bf16[2,512,768]{1,2,0:T(8,128)(2,1)}, u32[]{:S(2)}, u32[]{:S(2)}) collective-permute-start(bf16[2,512,768]{1,2,0:T(8,128)(2,1)S(1)} %copy.142), channel_id=1, source_target_pairs={{0,1},{1,2},{2,3},{4,5},{5,6},{6,7},{8,9},{9,10},{10,11},{12,13},{... | collective-permute-start | bytes 4718600 | tf_op jit(solution)/shard_map/while/body/eval_jaxpr/ppermute | solution.py:23
  548.2 41.5 %collective-permute-start.1 = (bf16[2,512,768]{1,2,0:T(8,128)(2,1)}, bf16[2,512,768]{1,2,0:T(8,128)(2,1)}, u32[]{:S(2)}, u32[]{:S(2)}) collective-permute-start(bf16[2,512,768]{1,2,0:T(8,128)(2,1)} %copy.143), channel_id=1, source_target_pairs={{0,1},{1,2},{2,3},{4,5},{5,6},{6,7},{8,9},{9,10},{10,11},{12,13},{... | collective-permute-start | bytes 4718600 | tf_op jit(solution)/shard_map/while/body/eval_jaxpr/ppermute | solution.py:23
  602.4 98.6 %collective-permute-start.2 = (bf16[2,512,1536]{1,2,0:T(8,128)(2,1)}, bf16[2,512,1536]{1,2,0:T(8,128)(2,1)}, u32[]{:S(2)}, u32[]{:S(2)}) collective-permute-start(bf16[2,512,1536]{1,2,0:T(8,128)(2,1)} %convert_element_type.306), channel_id=1, source_target_pairs={{0,1},{1,2},{2,3},{3,0},{4,5},{5,6},{6,7},{7,4},{8,9},{9,10},{10,1... | collective-permute-start | bytes 9437192 | tf_op jit(solution)/shard_map/while/body/eval_jaxpr/ppermute | solution.py:17
  692.7 13.7 %collective-permute-start = (bf16[2,512,768]{1,2,0:T(8,128)(2,1)S(1)}, bf16[2,512,768]{1,2,0:T(8,128)(2,1)}, u32[]{:S(2)}, u32[]{:S(2)}) collective-permute-start(bf16[2,512,768]{1,2,0:T(8,128)(2,1)S(1)} %copy.142), channel_id=1, source_target_pairs={{0,1},{1,2},{2,3},{4,5},{5,6},{6,7},{8,9},{9,10},{10,11},{12,13},{... | collective-permute-start | bytes 4718600 | tf_op jit(solution)/shard_map/while/body/eval_jaxpr/ppermute | solution.py:23
  698.3 8.1 collective-permute-start.1
  719.0 129.1 %collective-permute-start.2 = (bf16[2,512,1536]{1,2,0:T(8,128)(2,1)}, bf16[2,512,1536]{1,2,0:T(8,128)(2,1)}, u32[]{:S(2)}, u32[]{:S(2)}) collective-permute-start(bf16[2,512,1536]{1,2,0:T(8,128)(2,1)} %convert_element_type.306), channel_id=1, source_target_pairs={{0,1},{1,2},{2,3},{3,0},{4,5},{5,6},{6,7},{7,4},{8,9},{9,10},{10,1... | collective-permute-start | bytes 9437192 | tf_op jit(solution)/shard_map/while/body/eval_jaxpr/ppermute | solution.py:17
  776.0 77.5 %collective-permute-start = (bf16[2,512,768]{1,2,0:T(8,128)(2,1)S(1)}, bf16[2,512,768]{1,2,0:T(8,128)(2,1)}, u32[]{:S(2)}, u32[]{:S(2)}) collective-permute-start(bf16[2,512,768]{1,2,0:T(8,128)(2,1)S(1)} %copy.142), channel_id=1, source_target_pairs={{0,1},{1,2},{2,3},{4,5},{5,6},{6,7},{8,9},{9,10},{10,11},{12,13},{... | collective-permute-start | bytes 4718600 | tf_op jit(solution)/shard_map/while/body/eval_jaxpr/ppermute | solution.py:23
  845.6 7.9 collective-permute-start.1
  859.9 106.9 %copy-start.17 = (bf16[1024,768]{1,0:T(8,128)(2,1)S(1)}, bf16[1024,768]{1,0:T(8,128)(2,1)}, u32[]{:S(2)}) copy-start(bf16[1024,768]{1,0:T(8,128)(2,1)} %copy-done.16) | copy-start | bytes 4718596
  859.9 106.9 %copy-start.21 = (bf16[1024,768]{1,0:T(8,128)(2,1)S(1)}, bf16[1024,768]{1,0:T(8,128)(2,1)}, u32[]{:S(2)}) copy-start(bf16[1024,768]{1,0:T(8,128)(2,1)} %copy-done.20) | copy-start | bytes 4718596
  865.5 101.3 %collective-permute-start.3 = (bf16[2,512,1536]{2,1,0:T(8,128)(2,1)}, bf16[2,512,1536]{2,1,0:T(8,128)(2,1)}, u32[]{:S(2)}, u32[]{:S(2)}) collective-permute-start(bf16[2,512,1536]{2,1,0:T(8,128)(2,1)} %copy.83), channel_id=1, source_target_pairs={{0,1},{1,2},{2,3},{3,0},{4,5},{5,6},{6,7},{7,4},{8,9},{9,10},{10,1... | collective-permute-start | bytes 9437192 | tf_op jit(solution)/shard_map/ppermute | solution.py:17
  924.7 112.6 %reduce-scatter.15.cloned.1.call-start = ((), (), s32[]{:S(2)}) async-start(), calls=%async_computation.14 | async-start | bytes 4423680 | tf_op jit(solution)/shard_map/reduce_scatter | solution.py:247
  974.4 131.2 %reduce-scatter.29.cloned.1.call-start = ((), (), s32[]{:S(2)}) async-start(), calls=%async_computation.21 | async-start | bytes 1769472
  977.0 195.4 %reduce-scatter.21.cloned.1.call-start = ((), (), s32[]{:S(2)}) async-start(), calls=%async_computation.17 | async-start | bytes 1327104 | tf_op jit(solution)/shard_map/reduce_scatter | solution.py:279
  977.8 61.8 %copy-start.4 = (bf16[2,512,768]{2,1,0:T(8,128)(2,1)S(1)}, bf16[2,512,768]{2,1,0:T(8,128)(2,1)}, u32[]{:S(2)}) copy-start(bf16[2,512,768]{2,1,0:T(8,128)(2,1)} %param.22) | copy-start | bytes 4718596
  977.8 61.8 %copy-start.28 = (f32[768]{0:T(1024)S(1)}, f32[768]{0:T(1024)}, u32[]{:S(2)}) copy-start(f32[768]{0:T(1024)} %copy-done.27) | copy-start | bytes 9220
  977.8 61.8 %copy-start.30 = (f32[1,4,2,128]{3,1,2,0:T(4,128)S(1)}, f32[1,4,2,128]{3,1,2,0:T(4,128)}, u32[]{:S(2)}) copy-start(f32[1,4,2,128]{3,1,2,0:T(4,128)} %copy-done.29) | copy-start | bytes 12292
  977.8 260.7 %reduce-scatter.25.cloned.1.call-start = ((), (), s32[]{:S(2)}) async-start(), calls=%async_computation.19 | async-start | bytes 1105920
  1039.6 7.1 copy-start.35
  1039.6 8.7 copy-start.32
  1046.7 31.7 %copy-start.15 = (bf16[2,512,768]{2,1,0:T(8,128)(2,1)S(1)}, bf16[2,512,768]{2,1,0:T(8,128)(2,1)}, u32[]{:S(2)}) copy-start(bf16[2,512,768]{2,1,0:T(8,128)(2,1)} %param.33) | copy-start | bytes 4718596
  1046.8 31.7 %copy-start.37 = (f32[1024]{0:T(1024)S(1)}, f32[1024]{0:T(1024)}, u32[]{:S(2)}) copy-start(f32[1024]{0:T(1024)} %copy-done.36) | copy-start | bytes 12292
  (24 other events, 61.9 us)
Sparse Core Ops, SparseCore 0:
  17.6 66.0 all-gather.7
  93.9 51.2 all-gather.11
  146.8 46.3 all-gather.9
  195.8 41.0 all-gather.13
  238.9 78.6 all-gather.15
  319.6 79.1 all-gather.17
  427.1 23.9 reduce-scatter.16
  453.8 47.8 reduce-scatter.22
  504.2 49.6 reduce-scatter.18
  924.9 70.2 reduce-scatter.26
  997.9 39.4 reduce-scatter.14
  1040.6 64.9 reduce-scatter.28
  1109.4 63.0 reduce-scatter.20
  1176.0 62.4 reduce-scatter.24
where the time goes:
time: 1250 us
  waiting for transfers between devices  523 us (42%)
  starting transfers between devices  292 us (23%)
  matrix products  169 us (14%)
  other arithmetic  89.6 us (7%)
  local copies, waits for them, and re-layouts  78.3 us (6%)
  blocking collectives  78.1 us (6%)
  between operations  16.4 us (1%)
    ppermute x4, starting transfers between devices, passed_along(): return lax.ppermute(value, axis, pairs)  205 us
    unnamed x17, waiting for transfers between devices  91 us
    ppermute x6, starting transfers between devices, from_behind(): lax.ppermute(value, axis, [(source, source + steps) for source in range(i...  86.7 us
    ppermute x4, waiting for transfers between devices, passed_along(): return lax.ppermute(value, axis, pairs)  76 us
    all_gather x1, waiting for transfers between devices, body(): lax.all_gather(down_wide, 'batch', axis=0, tiled=True)  70 us
    all_gather x1, waiting for transfers between devices, body(): lax.all_gather(up_wide, 'batch', axis=0, tiled=True)  68.6 us
    reduce_scatter x1, waiting for transfers between devices, body(): lax.psum_scatter(up_part.astype(jnp.bfloat16), 'batch', scatter_dimension...  65 us
    dot_general x8, matrix products, contract(): lax.dot_general(left, right, (((left_dim,), (right_dim,)), ((), ())), pre...  62.1 us
  transfers between devices with their start and end apart: 24, of which 13 were waited for; matrix products, arithmetic and copies ran while one was open for 22% of the time, Pallas kernels for 0%

commit v1 on v0

v1 whole, which is shorter than its diff:
```python
import functools

import jax
import jax.numpy as jnp
from jax import lax
from jax.experimental import pallas as pl
from jax.experimental.pallas import tpu as pltpu
from jax.sharding import PartitionSpec as P

HEADS = 12
HEAD_DIM = 64
CORES = 2
LANE_X = 2
MESH = pl.DeviceIdType.MESH
LOG2E = 1.4426950408889634
epsilon = 1e-05
masked = -1e30
bf16 = jnp.bfloat16
f32 = jnp.float32


def dot(left, right, left_dim, right_dim):
    return lax.dot_general(
        left, right, (((left_dim,), (right_dim,)), ((), ())), preferred_element_type=f32
    )


class Place:
    def __init__(self, sizes):
        self.batch, self.blk = sizes
        self.Z, self.X = self.batch // LANE_X, LANE_X
        self.Y, self.C = self.blk // CORES, CORES

    def here(self):
        b, d = lax.axis_index("batch"), lax.axis_index("blk")
        return b // self.X, b % self.X, d // self.C, d % self.C

    def device(self, z, x, p, c):
        return (z * self.X + x, p * self.C + c)


def split_rows(count):
    return 16 * ((count // 2) // 16)


class Sends:
    def __init__(self, send_sem, recv_sem):
        self.send_sem, self.recv_sem, self.count = send_sem, recv_sem, 0

    def start(self, src, dst, device):
        copy = pltpu.make_async_remote_copy(
            src_ref=src,
            dst_ref=dst,
            send_sem=self.send_sem.at[self.count],
            recv_sem=self.recv_sem.at[self.count],
            device_id=device,
            device_id_type=MESH,
        )
        self.count += 1
        copy.start()
        return copy


def greet(place, partners):
    barrier = pltpu.get_barrier_semaphore()
    for partner in partners:
        pl.semaphore_signal(barrier, inc=1, device_id=partner, device_id_type=MESH)
    pl.semaphore_wait(barrier, len(partners))


def partners_of(place):
    z, x, p, c = place.here()
    found = [place.device((z + k) % place.Z, x, p, c) for k in range(1, place.Z)]
    found += [place.device(z, 1 - x, p, c)]
    found += [place.device(z, x, (p + k) % place.Y, c) for k in range(1, place.Y)]
    found += [place.device(z, x, p, 1 - c)]
    return found


def gather_kernel(place, matrices, *refs):
    n = len(matrices)
    mats, (tok, cot, tag, vec) = refs[:n], refs[n : n + 4]
    outs, (tok_g, cot_g, tag_g, vec_g) = refs[n + 4 : 2 * n + 4], refs[2 * n + 4 : 2 * n + 8]
    send_sem, recv_sem, local_sem = refs[2 * n + 8 :]
    z, x, p, c = place.here()
    Z, X, Y = place.Z, place.X, place.Y
    greet(place, partners_of(place))
    sends = Sends(send_sem, recv_sem)
    started = []

    def go(src, dst, device):
        copy = sends.start(src, dst, device)
        started.append(copy)
        return copy

    local = []

    def keep(src, dst):
        copy = pltpu.make_async_copy(src, dst, local_sem.at[len(local)])
        copy.start()
        local.append(copy)
        return copy

    row_copies, cot_copies = [], []
    for k in range(1, Y):
        to = (p + k) % Y
        device = place.device(z, x, to, c)
        row_copies.append(go(tok.at[to], tok_g.at[p, c], device))
        row_copies.append(go(tag.at[to], tag_g.at[p, c], device))
        row_copies.append(go(vec, vec_g.at[p, c], device))
    own = [
        keep(tok.at[p], tok_g.at[p, c]),
        keep(tag.at[p], tag_g.at[p, c]),
        keep(vec, vec_g.at[p, c]),
        keep(cot.at[p], cot_g.at[p]),
    ]
    first = []
    for m in range(n):
        place_here = outs[m].at[p, c, z, x]
        keep(mats[m], place_here)
        first.append(
            [
                go(mats[m], place_here, place.device((z + k) % Z, x, p, c))
                for k in range(1, Z)
            ]
        )
    for k in range(1, Y):
        to = (p + k) % Y
        cot_copies.append(go(cot.at[to], cot_g.at[p], place.device(z, x, to, c)))
    for copy in local:
        copy.wait()
    second = []
    for m in range(n):
        for copy in first[m]:
            copy.wait_recv()
        h = split_rows(mats[m].shape[0])
        r = mats[m].shape[0]
        low = outs[m].at[p, c, :, x, 0:h]
        high = outs[m].at[p, c, :, x, h:r]
        second.append(
            (
                [go(low, low, place.device(z, 1 - x, p, c))],
                [go(high, high, place.device(z, x, (p + k) % Y, c)) for k in range(1, Y)],
            )
        )
    third = []
    for m in range(n):
        h = split_rows(mats[m].shape[0])
        r = mats[m].shape[0]
        for copy in second[m][0]:
            copy.wait_recv()
        low = outs[m].at[p, c, :, :, 0:h]
        a = [go(low, low, place.device(z, x, (p + k) % Y, c)) for k in range(1, Y)]
        for copy in second[m][1]:
            copy.wait_recv()
        high = outs[m].at[:, c, :, x, h:r]
        b = [go(high, high, place.device(z, 1 - x, p, c))]
        third.append(a + b)
    for copy in row_copies:
        copy.wait_recv()
    sibling = place.device(z, x, p, 1 - c)
    last = []
    for ref in (tok_g, tag_g, vec_g):
        last.append(go(ref.at[:, c], ref.at[:, c], sibling))
    for m in range(n):
        for copy in third[m]:
            copy.wait_recv()
        last.append(go(outs[m].at[:, c], outs[m].at[:, c], sibling))
    for copy in last + cot_copies:
        copy.wait_recv()
    for copy in started:
        copy.wait_send()


def gather_all(place, mats, tok, cot, tag, vec):
    n = len(mats)
    Z, X, Y, C = place.Z, place.X, place.Y, place.C
    out = [jax.ShapeDtypeStruct((Y, C, Z, X) + m.shape, m.dtype) for m in mats]
    out += [
        jax.ShapeDtypeStruct((Y, C) + tok.shape[1:], tok.dtype),
        jax.ShapeDtypeStruct((Y,) + cot.shape[1:], cot.dtype),
        jax.ShapeDtypeStruct((Y, C) + tag.shape[1:], tag.dtype),
        jax.ShapeDtypeStruct((Y, C) + vec.shape, vec.dtype),
    ]
    copies = 4 * (Y - 1) + n * ((Z - 1) + 1 + (Y - 1) + (Y - 1) + 1) + 3 + n
    anywhere = pl.BlockSpec(memory_space=pl.ANY)
    return pl.pallas_call(
        functools.partial(gather_kernel, place, tuple(m.shape for m in mats)),
        out_shape=out,
        in_specs=[anywhere] * (n + 4),
        out_specs=[anywhere] * (n + 4),
        scratch_shapes=[
            pltpu.SemaphoreType.DMA((copies,)),
            pltpu.SemaphoreType.DMA((copies,)),
            pltpu.SemaphoreType.DMA((n + 4,)),
        ],
        compiler_params=pltpu.CompilerParams(collective_id=0, has_side_effects=True),
        name="gather_all",
    )(*mats, tok, cot, tag, vec)


def swap_kernel(place, src, dst, send_sem, recv_sem):
    z, x, p, c = place.here()
    sibling = place.device(z, x, p, 1 - c)
    greet(place, [sibling])
    copy = pltpu.make_async_remote_copy(
        src_ref=src.at[1 - c],
        dst_ref=dst,
        send_sem=send_sem,
        recv_sem=recv_sem,
        device_id=sibling,
        device_id_type=MESH,
    )
    copy.start()
    copy.wait()


def swap(place, value, number):
    anywhere = pl.BlockSpec(memory_space=pl.ANY)
    return pl.pallas_call(
        functools.partial(swap_kernel, place),
        out_shape=jax.ShapeDtypeStruct(value.shape[1:], value.dtype),
        in_specs=[anywhere],
        out_specs=anywhere,
        scratch_shapes=[pltpu.SemaphoreType.DMA, pltpu.SemaphoreType.DMA],
        compiler_params=pltpu.CompilerParams(collective_id=number, has_side_effects=True),
        name=f"swap_{number}",
    )(value)


def head_masked(value, h, axis):
    index = lax.broadcasted_iota(jnp.int32, value.shape, axis)
    return jnp.where((index // HEAD_DIM) == h, value, jnp.zeros_like(value))


def attention_forward_kernel(BQ, start_ref, q_ref, k_ref, v_ref, o_ref, oT_ref, lt_ref, qT, vT):
    L = q_ref.shape[0]
    nq = L // BQ
    scale = HEAD_DIM ** (-0.5) * LOG2E
    qT[...] = q_ref[...].T
    vT[...] = v_ref[...].T
    for qi in range(nq):
        qs = slice(qi * BQ, (qi + 1) * BQ)
        begin = start_ref[:, qs]
        d0 = qi * BQ
        if qi == nq - 1:
            cuts = [(0, d0, 1)] if d0 else []
        elif d0 > 256:
            cuts = [(0, 256, 1), (256, d0, 0)]
        else:
            cuts = [(0, d0, 1)] if d0 else []
        cuts.append((d0, d0 + BQ, 2))
        for h in range(2):
            query = head_masked(qT[:, qs], h, 0)
            parts = []
            for a, b, mode in cuts:
                s = dot(k_ref[a:b, :], query, 1, 0) * scale
                if mode:
                    key_pos = lax.broadcasted_iota(jnp.int32, (b - a, BQ), 0) + a
                    visible = key_pos >= begin
                    if mode == 2:
                        query_pos = lax.broadcasted_iota(jnp.int32, (b - a, BQ), 1) + d0
                        visible = jnp.logical_and(visible, key_pos <= query_pos)
                    s = jnp.where(visible, s, masked)
                parts.append(s)
            top = functools.reduce(
                jnp.maximum, [jnp.max(s, axis=0, keepdims=True) for s in parts]
            )
            total, accum = 0.0, 0.0
            for (a, b, mode), s in zip(cuts, parts):
                e = jnp.exp2(s - top)
                total = total + jnp.sum(e, axis=0, keepdims=True)
                accum = accum + dot(
                    vT[h * HEAD_DIM : (h + 1) * HEAD_DIM, a:b], e.astype(bf16), 1, 0
                )
            oT_ref[h * HEAD_DIM : (h + 1) * HEAD_DIM, qs] = accum / total
            lt_ref[0, h : h + 1, qs] = top + jnp.log2(total)
        o_ref[qs, :] = oT_ref[:, qs].astype(bf16).T


def attention_forward(projected, begin):
    L = projected.shape[0]
    pairs = projected.shape[1] // 3 // 128
    return pl.pallas_call(
        functools.partial(attention_forward_kernel, 512),
        grid=(pairs,),
        in_specs=[
            pl.BlockSpec((1, L), lambda i: (0, 0)),
            pl.BlockSpec((L, 128), lambda i: (0, i)),
            pl.BlockSpec((L, 128), lambda i: (0, pairs + i)),
            pl.BlockSpec((L, 128), lambda i: (0, 2 * pairs + i)),
        ],
        out_specs=[
            pl.BlockSpec((L, 128), lambda i: (0, i)),
            pl.BlockSpec((128, L), lambda i: (i, 0)),
            pl.BlockSpec((1, 2, L), lambda i: (i, 0, 0)),
        ],
        out_shape=[
            jax.ShapeDtypeStruct((L, pairs * 128), bf16),
            jax.ShapeDtypeStruct((pairs * 128, L), f32),
            jax.ShapeDtypeStruct((pairs, 2, L), f32),
        ],
        scratch_shapes=[pltpu.VMEM((128, L), bf16), pltpu.VMEM((128, L), bf16)],
        compiler_params=pltpu.CompilerParams(vmem_limit_bytes=50 << 20),
        name="attention_forward",
    )(begin, projected, projected, projected)


def attention_backward_kernel(
    BQ, start_ref, q_ref, k_ref, v_ref, do_ref, oT_ref, lt_ref,
    dq_ref, dk_ref, dv_ref, qT, kT, doT, dk, dv, dqT,
):
    L = q_ref.shape[0]
    nq = L // BQ
    scale = HEAD_DIM ** (-0.5) * LOG2E
    qT[...] = q_ref[...].T
    kT[...] = k_ref[...].T
    doT[...] = do_ref[...].T
    dk[...] = jnp.zeros_like(dk)
    dv[...] = jnp.zeros_like(dv)

    def tile(h, qi, kj, query, grad, deltas, dq, mode):
        qs = pl.ds(pl.multiple_of(qi * BQ, BQ), BQ)
        ks = pl.ds(pl.multiple_of(kj * BQ, BQ), BQ)
        s = dot(k_ref[ks, :], query, 1, 0) * scale
        prob = jnp.exp2(s - lt_ref[0, h : h + 1, qs])
        if mode:
            key_pos = lax.broadcasted_iota(jnp.int32, (BQ, BQ), 0)
            visible = key_pos >= (start_ref[:, qs] - kj * BQ)
            if mode == 2:
                query_pos = lax.broadcasted_iota(jnp.int32, (BQ, BQ), 1)
                visible = jnp.logical_and(visible, key_pos <= query_pos)
            prob = jnp.where(visible, prob, 0.0)
        dp = dot(v_ref[ks, :], grad, 1, 0)
        ds = (prob * (dp - deltas)).astype(bf16)
        dv[ks, :] += dot(prob.astype(bf16), head_masked(do_ref[qs, :], h, 1), 1, 0)
        dk[ks, :] += dot(ds, head_masked(q_ref[qs, :], h, 1), 1, 0)
        return dq + dot(kT[h * HEAD_DIM : (h + 1) * HEAD_DIM, ks], ds, 1, 0)

    def one_query(i, nothing):
        qi = nq - 1 - i
        qs = pl.ds(pl.multiple_of(qi * BQ, BQ), BQ)
        for h in range(2):
            rows = slice(h * HEAD_DIM, (h + 1) * HEAD_DIM)
            deltas = jnp.sum(
                doT[rows, qs].astype(f32) * oT_ref[rows, qs], axis=0, keepdims=True
            )
            query, grad = head_masked(qT[:, qs], h, 0), head_masked(doT[:, qs], h, 0)
            step = functools.partial(tile, h, qi)

            def run(kj, dq, mode):
                return tile(h, qi, kj, query, grad, deltas, dq, mode)

            dq = run(qi, jnp.zeros((HEAD_DIM, BQ), f32), 2)

            def last(dq):
                return lax.fori_loop(0, qi, lambda kj, d: run(kj, d, 1), dq)

            def others(dq):
                dq = lax.cond(qi > 0, lambda d: run(0, d, 1), lambda d: d, dq)
                return lax.fori_loop(1, qi, lambda kj, d: run(kj, d, 0), dq)

            dq = lax.cond(qi == nq - 1, last, others, dq)
            dqT[rows, qs] = dq
        return nothing

    lax.fori_loop(0, nq, one_query, 0)
    scale_back = HEAD_DIM ** (-0.5)
    dq_ref[...] = (dqT[...] * scale_back).astype(bf16).T
    dk_ref[...] = (dk[...] * scale_back).astype(bf16)
    dv_ref[...] = dv[...].astype(bf16)


def attention_backward(projected, grads, oT, lt, begin):
    L = projected.shape[0]
    pairs = projected.shape[1] // 3 // 128
    wide = pl.BlockSpec((L, 128), lambda i: (0, i))
    return pl.pallas_call(
        functools.partial(attention_backward_kernel, 512),
        grid=(pairs,),
        in_specs=[
            pl.BlockSpec((1, L), lambda i: (0, 0)),
            wide,
            pl.BlockSpec((L, 128), lambda i: (0, pairs + i)),
            pl.BlockSpec((L, 128), lambda i: (0, 2 * pairs + i)),
            wide,
            pl.BlockSpec((128, L), lambda i: (i, 0)),
            pl.BlockSpec((1, 2, L), lambda i: (i, 0, 0)),
        ],
        out_specs=[wide] * 3,
        out_shape=[jax.ShapeDtypeStruct((L, pairs * 128), bf16)] * 3,
        scratch_shapes=[pltpu.VMEM((128, L), bf16)] * 3
        + [pltpu.VMEM((L, 128), f32)] * 2
        + [pltpu.VMEM((128, L), f32)],
        compiler_params=pltpu.CompilerParams(vmem_limit_bytes=50 << 20),
        name="attention_backward",
    )(begin, projected, projected, projected, grads, oT, lt)


def reduce_kernel(place, n, *refs):
    parts, (vec, out_in, tg_in) = refs[:n], refs[n : n + 3]
    sums, (vec_out, out_out, tg_out) = refs[n + 3 : 2 * n + 3], refs[2 * n + 3 : 2 * n + 6]
    scratch = refs[2 * n + 6 :]
    per = 7
    stage = [scratch[per * m : per * (m + 1)] for m in range(n)]
    vec_core, vec_y, vec_x, vec_z, vec_acc = scratch[per * n : per * n + 5]
    send_sem, recv_sem, local_sem = scratch[per * n + 5 :]
    z, x, p, c = place.here()
    Z, X, Y = place.Z, place.X, place.Y
    greet(place, partners_of(place))
    sends = Sends(send_sem, recv_sem)
    started = []
    sibling = place.device(z, x, p, 1 - c)
    beside = place.device(z, 1 - x, p, c)

    def go(src, dst, device):
        copy = sends.start(src, dst, device)
        started.append(copy)
        return copy

    def add(target, sources, count):
        def one(i, nothing):
            total = sources[0](i).astype(f32)
            for source in sources[1:]:
                total = total + source(i).astype(f32)
            target(i, total)
            return nothing

        lax.fori_loop(0, count, one, 0)

    core = [go(parts[m].at[:, 1 - c], stage[m][0], sibling) for m in range(n)]
    vec_copy = go(vec.at[:, 1 - c], vec_core, sibling)
    home = []
    for k in range(1, Y):
        to = (p + k) % Y
        device = place.device(z, x, to, c)
        home.append(go(tg_in.at[to], tg_out.at[p], device))
        home.append(go(out_in.at[to], out_out.at[p], device))
    kept = [
        pltpu.make_async_copy(tg_in.at[p], tg_out.at[p], local_sem.at[0]),
        pltpu.make_async_copy(out_in.at[p], out_out.at[p], local_sem.at[1]),
    ]
    for copy in kept:
        copy.start()
    second = []
    for m in range(n):
        recv0, acc, xa, yb, ya, xb, zz = stage[m]
        rows = acc.shape[3]
        h = split_rows(rows)
        core[m].wait_recv()

        def read_part(i):
            return parts[m][i // (Z * X), c, (i // X) % Z, i % X]

        def read_recv(i):
            return recv0[i // (Z * X), (i // X) % Z, i % X]

        def write_acc(i, value):
            acc[i // (Z * X), (i // X) % Z, i % X] = value.astype(bf16)

        add(write_acc, [read_part, read_recv], Y * Z * X)
        second.append(
            (
                go(acc.at[:, :, 1 - x, 0:h], xa, beside),
                [
                    go(
                        acc.at[(p + k) % Y, :, :, h:rows],
                        yb.at[k - 1],
                        place.device(z, x, (p + k) % Y, c),
                    )
                    for k in range(1, Y)
                ],
            )
        )
    vec_copy.wait_recv()
    vec_acc[...] = vec[:, c] + vec_core[...]
    vec_copies = [
        go(vec_acc.at[(p + k) % Y], vec_y.at[k - 1], place.device(z, x, (p + k) % Y, c))
        for k in range(1, Y)
    ]
    third = []
    for m in range(n):
        recv0, acc, xa, yb, ya, xb, zz = stage[m]
        rows = acc.shape[3]
        h = split_rows(rows)
        second[m][0].wait_recv()

        def write_a(i, value):
            acc[i // Z, i % Z, x, 0:h] = value.astype(bf16)

        add(
            write_a,
            [lambda i: acc[i // Z, i % Z, x, 0:h], lambda i: xa[i // Z, i % Z]],
            Y * Z,
        )
        a = [
            go(acc.at[(p + k) % Y, :, x, 0:h], ya.at[k - 1], place.device(z, x, (p + k) % Y, c))
            for k in range(1, Y)
        ]
        for copy in second[m][1]:
            copy.wait_recv()

        def write_b(i, value):
            acc[p, i // X, i % X, h:rows] = value.astype(bf16)

        add(
            write_b,
            [lambda i: acc[p, i // X, i % X, h:rows]]
            + [lambda i, k=k: yb[k, i // X, i % X] for k in range(Y - 1)],
            Z * X,
        )
        b = go(acc.at[p, :, 1 - x, h:rows], xb, beside)
        third.append((a, b))
    for copy in vec_copies:
        copy.wait_recv()
    vec_acc[p] = vec_acc[p] + sum(vec_y[k] for k in range(Y - 1))
    vec_next = go(vec_acc.at[p], vec_x, beside)
    fourth = []
    for m in range(n):
        recv0, acc, xa, yb, ya, xb, zz = stage[m]
        rows = acc.shape[3]
        h = split_rows(rows)
        for copy in third[m][0]:
            copy.wait_recv()

        def write_a2(i, value):
            acc[p, i, x, 0:h] = value.astype(bf16)

        add(
            write_a2,
            [lambda i: acc[p, i, x, 0:h]] + [lambda i, k=k: ya[k, i] for k in range(Y - 1)],
            Z,
        )
        third[m][1].wait_recv()

        def write_b2(i, value):
            acc[p, i, x, h:rows] = value.astype(bf16)

        add(write_b2, [lambda i: acc[p, i, x, h:rows], lambda i: xb[i]], Z)
        fourth.append(
            [
                go(acc.at[p, (z + k) % Z, x], zz.at[k - 1], place.device((z + k) % Z, x, p, c))
                for k in range(1, Z)
            ]
        )
    vec_next.wait_recv()
    vec_next.wait_send()
    vec_acc[p] = vec_acc[p] + vec_x[...]
    vec_last = [
        go(vec_acc.at[p], vec_z.at[k - 1], place.device((z + k) % Z, x, p, c))
        for k in range(1, Z)
    ]
    for m in range(n):
        recv0, acc, xa, yb, ya, xb, zz = stage[m]
        for copy in fourth[m]:
            copy.wait_recv()
        total = acc[p, z, x].astype(f32)
        for k in range(Z - 1):
            total = total + zz[k].astype(f32)
        sums[m][...] = total
    for copy in vec_last:
        copy.wait_recv()
    total = vec_acc[p]
    for k in range(Z - 1):
        total = total + vec_z[k]
    vec_out[...] = total
    for copy in home:
        copy.wait_recv()
    for copy in kept:
        copy.wait()
    for copy in started:
        if copy is not vec_next:
            copy.wait_send()


def reduce_all(place, parts, vec, out_in, tg_in):
    n = len(parts)
    Z, X, Y, C = place.Z, place.X, place.Y, place.C
    inside = pl.BlockSpec(memory_space=pltpu.VMEM)
    anywhere = pl.BlockSpec(memory_space=pl.ANY)
    scratch = []
    for part in parts:
        r, w = part.shape[4:]
        h = split_rows(r)
        scratch += [
            pltpu.VMEM((Y, Z, X, r, w), bf16),
            pltpu.VMEM((Y, Z, X, r, w), bf16),
            pltpu.VMEM((Y, Z, h, w), bf16),
            pltpu.VMEM((Y - 1, Z, X, r - h, w), bf16),
            pltpu.VMEM((Y - 1, Z, h, w), bf16),
            pltpu.VMEM((Z, r - h, w), bf16),
            pltpu.VMEM((Z - 1, r, w), bf16),
        ]
    vs = vec.shape[2:]
    scratch += [
        pltpu.VMEM((Y,) + vs, f32),
        pltpu.VMEM((Y - 1,) + vs, f32),
        pltpu.VMEM(vs, f32),
        pltpu.VMEM((Z - 1,) + vs, f32),
        pltpu.VMEM((Y,) + vs, f32),
    ]
    copies = n * (1 + 1 + (Y - 1) + (Y - 1) + 1 + (Z - 1)) + 1 + (Y - 1) + 1 + (Z - 1) + 2 * (Y - 1)
    scratch += [
        pltpu.SemaphoreType.DMA((copies,)),
        pltpu.SemaphoreType.DMA((copies,)),
        pltpu.SemaphoreType.DMA((2,)),
    ]
    out_shape = [jax.ShapeDtypeStruct(part.shape[4:], f32) for part in parts]
    out_shape += [
        jax.ShapeDtypeStruct(vs, f32),
        jax.ShapeDtypeStruct(out_in.shape, out_in.dtype),
        jax.ShapeDtypeStruct(tg_in.shape, tg_in.dtype),
    ]
    return pl.pallas_call(
        functools.partial(reduce_kernel, place, n),
        out_shape=out_shape,
        in_specs=[inside] * (n + 1) + [anywhere] * 2,
        out_specs=[inside] * (n + 1) + [anywhere] * 2,
        scratch_shapes=scratch,
        compiler_params=pltpu.CompilerParams(
            collective_id=1, has_side_effects=True, vmem_limit_bytes=60 << 20
        ),
        name="reduce_all",
    )(*parts, vec, out_in, tg_in)


def normed(values):
    average = jnp.mean(values, axis=-1, keepdims=True)
    centered = values - average
    variance = jnp.mean(centered * centered, axis=-1, keepdims=True)
    factor = lax.rsqrt(variance + epsilon)
    return centered * factor, factor


def norm_back(grad, gain, unit, factor):
    e = grad * gain
    return factor * (
        e - jnp.mean(e, axis=-1, keepdims=True) - unit * jnp.mean(e * unit, axis=-1, keepdims=True)
    )


def gelu_tanh(values):
    return jax.nn.gelu(values, approximate=True)


def joined(gathered, axis):
    Y, C, Z, X, r, w = gathered.shape
    if axis == 0:
        return gathered.reshape(Y * C, Z * X * r, w).transpose(1, 0, 2).reshape(Z * X * r, -1)
    return gathered.reshape(Y * C, Z * X, r, w).transpose(0, 2, 1, 3).reshape(Y * C * r, -1)


def parted(whole, place, axis):
    Y, C, Z, X = place.Y, place.C, place.Z, place.X
    rows, columns = whole.shape
    if axis == 0:
        value = whole.reshape(Z * X, rows // (Z * X), Y * C, columns // (Y * C))
        value = value.transpose(2, 0, 1, 3)
    else:
        value = whole.reshape(Y * C, rows // (Y * C), Z * X, columns // (Z * X))
        value = value.transpose(0, 2, 1, 3)
    return value.reshape((Y, C, Z, X) + value.shape[2:])


def chosen(pair, c):
    return jnp.where(c == 0, pair[0], pair[1])


def body(
    place,
    tokens,
    proj_weight,
    out_weight,
    up_weight,
    down_weight,
    gain_one,
    bias_one,
    gain_two,
    bias_two,
    segments,
    present,
    cotangent,
):
    rows, block, width = tokens.shape
    Y, C = place.Y, place.C
    length = place.blk * block
    index = lax.axis_index("blk")
    c = index % C
    half = width // C
    query_pos = index * block + jnp.arange(block, dtype=jnp.int32)
    local_tags = jnp.where(present == 1, segments, -1 - query_pos[None, :])
    tag_in = jnp.broadcast_to(local_tags[:, None, :], (rows, 8, block))
    vec_in = jnp.stack([gain_one, bias_one, gain_two, bias_two])
    vec_in = jnp.pad(vec_in, ((0, 12), (0, 0)))
    proj_g, out_g, up_g, down_g, tok_g, cot_g, tag_g, vec_g = gather_all(
        place,
        [proj_weight, out_weight, up_weight, down_weight.T],
        tokens,
        cotangent,
        tag_in,
        vec_in,
    )
    proj_full, out_full, up_full = joined(proj_g, 0), joined(out_g, 0), joined(up_g, 0)
    down_full_t = joined(down_g, 1)
    gain_a, bias_a, gain_b, bias_b = (
        vec_g.reshape(place.blk, 16, -1)[:, :4].transpose(1, 0, 2).reshape(4, width).astype(f32)
    )
    proj_own = lax.dynamic_index_in_dim(
        proj_full.reshape(width, 3, C, half), c, 2, keepdims=False
    ).reshape(width, 3 * half)
    row_tags = tag_g[:, :, 0].reshape(length)
    row_pos = jnp.arange(length, dtype=jnp.int32)
    begin = sum(
        jnp.where(row_tags > s, jnp.sum((row_tags == s).astype(jnp.int32)), 0) for s in range(4)
    )
    begin = jnp.where(row_tags < 0, row_pos, begin)[None]
    inputs = tok_g.reshape(length, width).astype(f32)
    unit, factor = normed(inputs)
    normed_low = (unit * gain_a + bias_a).astype(bf16)
    projected = dot(normed_low, proj_own, 1, 0).astype(bf16)
    attended, attended_t, log_total = attention_forward(projected, begin)
    by_core = attended.reshape(Y, C, block, half).transpose(1, 0, 2, 3)
    other = swap(place, by_core, 2).reshape(Y * block, half)
    mine = lax.dynamic_index_in_dim(by_core, c, 0, keepdims=False).reshape(Y * block, half)
    attended_low = jnp.concatenate(
        [chosen((mine, other), c), chosen((other, mine), c)], axis=1
    )
    inputs_mine = (
        lax.dynamic_index_in_dim(tok_g, c, 1, keepdims=False)
        .reshape(Y * block, width)
        .astype(f32)
    )
    middle = inputs_mine + dot(attended_low, out_full, 1, 0)
    unit_two, factor_two = normed(middle)
    normed_two_low = (unit_two * gain_b + bias_b).astype(bf16)
    hidden = dot(normed_two_low, up_full, 1, 0)
    activated_low = gelu_tanh(hidden).astype(bf16)
    output = (middle + dot(activated_low, down_full_t, 1, 1)).astype(bf16)
    grad_out = cot_g.reshape(Y * block, width)
    down_grad_t = dot(grad_out, activated_low, 0, 0).astype(bf16)
    grad_act = dot(grad_out, down_full_t, 1, 0)
    unused_value, gelu_back = jax.vjp(gelu_tanh, hidden)
    grad_hidden = gelu_back(grad_act)[0].astype(bf16)
    up_grad = dot(normed_two_low, grad_hidden, 0, 0).astype(bf16)
    grad_normed_two = dot(grad_hidden, up_full, 1, 1)
    gain_two_grad = jnp.sum(grad_normed_two * unit_two, axis=0)
    bias_two_grad = jnp.sum(grad_normed_two, axis=0)
    grad_middle = grad_out.astype(f32) + norm_back(grad_normed_two, gain_b, unit_two, factor_two)
    grad_middle_low = grad_middle.astype(bf16)
    out_grad = dot(attended_low, grad_middle_low, 0, 0).astype(bf16)
    grad_attended = dot(grad_middle_low, out_full, 1, 1).astype(bf16)
    grad_by_core = grad_attended.reshape(Y, block, C, half).transpose(2, 0, 1, 3)
    grad_other = swap(place, grad_by_core, 3)
    grad_mine = lax.dynamic_index_in_dim(grad_by_core, c, 0, keepdims=False)
    grad_heads = jnp.stack(
        [chosen((grad_mine, grad_other), c), chosen((grad_other, grad_mine), c)], axis=1
    ).reshape(length, half)
    dq, dk, dv = attention_backward(projected, grad_heads, attended_t, log_total, begin)
    projected_grad = jnp.concatenate([dq, dk, dv], axis=1)
    proj_grad_own = dot(normed_low, projected_grad, 0, 0).astype(bf16)
    spread = jnp.zeros((width, 3, C, half), bf16)
    proj_grad = lax.dynamic_update_slice(
        spread, proj_grad_own.reshape(width, 3, 1, half), (0, 0, c, 0)
    ).reshape(width, 3 * width)
    g_part = dot(projected_grad, proj_own, 1, 1)
    g_by_core = g_part.astype(bf16).reshape(Y, C, block, width).transpose(1, 0, 2, 3)
    g_other = swap(place, g_by_core, 4).reshape(Y * block, width)
    g_mine = lax.dynamic_index_in_dim(
        g_part.reshape(Y, C, block, width), c, 1, keepdims=False
    ).reshape(Y * block, width)
    grad_normed = g_mine + g_other.astype(f32)
    unit_mine, factor_mine = normed(inputs_mine)
    gain_one_grad = jnp.sum(grad_normed * unit_mine, axis=0)
    bias_one_grad = jnp.sum(grad_normed, axis=0)
    token_grad = (
        grad_middle + norm_back(grad_normed, gain_a, unit_mine, factor_mine)
    ).astype(bf16)
    vec = jnp.stack([gain_one_grad, bias_one_grad, gain_two_grad, bias_two_grad])
    vec = jnp.pad(vec, ((0, 4), (0, 0)))
    vec = vec.reshape(8, Y, C, width // place.blk).transpose(1, 2, 0, 3)
    proj_sum, out_sum, up_sum, down_sum, vec_sum, output, token_grad = reduce_all(
        place,
        [
            parted(proj_grad, place, 0),
            parted(out_grad, place, 0),
            parted(up_grad, place, 0),
            parted(down_grad_t, place, 1),
        ],
        vec,
        output.reshape(Y, block, width),
        token_grad.reshape(Y, block, width),
    )
    return (
        output,
        token_grad,
        proj_sum,
        out_sum,
        up_sum,
        down_sum.T,
        vec_sum[0],
        vec_sum[1],
        vec_sum[2],
        vec_sum[3],
    )


def solution(mesh):
    place = Place((mesh.shape["batch"], mesh.shape["blk"]))
    weight, vector = P("batch", "blk"), P("blk")
    row = P("batch", "blk", None)
    in_specs = (row,) + (weight,) * 4 + (vector,) * 4 + (weight,) * 2 + (row,)
    out_specs = (row, row) + (weight,) * 4 + (vector,) * 4
    return jax.shard_map(
        functools.partial(body, place),
        mesh=mesh,
        in_specs=in_specs,
        out_specs=out_specs,
        check_vma=False,
    )
```

time: 1250 us -> 659 us (0.53)
  waiting for transfers between devices: 523 us -> 0 us
  Pallas kernels: 0 us -> 367 us
  starting transfers between devices: 292 us -> 0 us
  local copies, waits for them, and re-layouts: 78.3 us -> 162 us
  blocking collectives: 78.1 us -> 0 us
  matrix products: 169 us -> 92 us
  other arithmetic: 89.6 us -> 24.4 us
  between operations: 16.4 us -> 1.5 us
    pallas_call x0 -> x7, Pallas kernels: none -> 367 us  [the longest x1 136 us: gather_all(): pl.pallas_call(functools.partial(gather_kernel, place, tuple((m.shape for...]
    ppermute x10 -> x0, starting transfers between devices: 291 us -> none  [the longest x4 205 us: passed_along(): return lax.ppermute(value, axis, pairs)]
    all_gather x6 -> x0, waiting for transfers between devices: 250 us -> none  [the longest x1 70 us: body(): lax.all_gather(down_wide, 'batch', axis=0, tiled=True)]
    reduce_scatter x5 -> x0, waiting for transfers between devices: 106 us -> none  [the longest x1 65 us: body(): lax.psum_scatter(up_part.astype(jnp.bfloat16), 'batch', scatter_dimension...]
    unnamed x17 -> x0, waiting for transfers between devices: 91 us -> none
    dot_general x19 -> x12, matrix products: 169 us -> 92 us  [dot(): lax.dot_general(left, right, (((left_dim,), (right_dim,)), ((), ())), pre...]
    ppermute x10 -> x0, waiting for transfers between devices: 76 us -> none  [the longest x4 76 us: passed_along(): return lax.ppermute(value, axis, pairs)]
    dynamic_update_slice x0 -> x1, local copies, waits for them, and re-layouts: none -> 56.4 us  [body(): lax.dynamic_update_slice(spread, proj_grad_own.reshape(width, 3, 1, half)...]
  transfers between devices with their start and end apart: 24 -> 0, of which waited for: 13 -> 0; matrix products, arithmetic and copies ran while one was open for 22% -> 0% of each run, Pallas kernels for 0% -> 0%
where the time goes in v1:
time: 659 us; the launch traced here: 647 us
  Pallas kernels  367 us (56%)
  local copies, waits for them, and re-layouts  162 us (25%)
  matrix products  92 us (14%)
  other arithmetic  24.4 us (4%)
    pallas_call x1, Pallas kernels, gather_all(): pl.pallas_call(functools.partial(gather_kernel, place, tuple((m.shape for...  136 us
    pallas_call x1, Pallas kernels, reduce_all(): pl.pallas_call(functools.partial(reduce_kernel, place, n), out_shape=out_...  133 us
    dot_general x12, matrix products, dot(): lax.dot_general(left, right, (((left_dim,), (right_dim,)), ((), ())), pre...  92 us
    pallas_call x1, Pallas kernels, attention_backward(): pl.pallas_call(functools.partial(attention_backward_kernel, 512), grid=(p...  60.4 us
    dynamic_update_slice x1, local copies, waits for them, and re-layouts, body(): lax.dynamic_update_slice(spread, proj_grad_own.reshape(width, 3, 1, half)...  56.4 us
    pallas_call x1, Pallas kernels, attention_forward(): pl.pallas_call(functools.partial(attention_forward_kernel, 512), grid=(pa...  28.5 us
    reshape x4, local copies, waits for them, and re-layouts, parted(): value = whole.reshape(Z * X, rows // (Z * X), Y * C, columns // (Y * C))  22.6 us
    reshape x3, local copies, waits for them, and re-layouts, joined(): gathered.reshape(Y * C, Z * X * r, w).transpose(1, 0, 2)  14.7 us

profile of v1, /device:TPU:0, one launch (start us, length us, event | category | flops | bytes accessed | tf_op | source)
XLA Modules:
  0.0 647.0 jit_solution(17541024644663709863)
XLA Ops:
  5.2 136.2 %gather_all.1 = (bf16[2,2,4,2,96,576]{5,4,3,2,1,0:T(8,128)(2,1)}, bf16[2,2,4,2,96,192]{5,4,3,2,1,0:T(8,128)(2,1)}, bf16[2,2,4,2,96,768]{5,4,3,2,1,0:T(8,128)(2,1...) custom-call(bf16[96,576]{1,0:T(8,128)(2,1)} %refs_0_.1, ...), custom_call_target="tpu_custom_call" | custom-call | tf_op jit(solution)/shard_map/gather_all/pallas_call | solution.py:187
  141.5 6.2 copy.44
  147.7 3.0 constant_dynamic-slice_fusion.4
  154.7 5.9 convolution_convert_fusion.q_ref.k_ref.v_ref
  160.6 1.5 fusion.40
  162.2 3.5 fusion.41
  166.5 28.5 %attention_forward.1 = (bf16[2048,384]{1,0:T(8,128)(2,1)S(1)}, f32[384,2048]{1,0:T(8,128)}, f32[3,2,2048]{2,1,0:T(2,128)S(1)}) custom-call(s32[1,2048]{1,0:T(1,128)S(1)} %iota_select_fusion.start_ref, bf16[2048,1152]{1,0:T(8,128)(2,1)} %convolution_convert_fusion.q_ref.k_ref.v_ref, bf16[2048,1152]{1,0:T(8,128)(2,1)} %convolution_convert_fusion.q_ref.k_ref.v_ref, ...), custom_call_target="tpu_custom_call" | custom-call | tf_op jit(solution)/shard_map/attention_forward/pallas_call | solution.py:284
  196.3 2.7 swap_2.1
  199.2 2.6 bitcast_select_fusion.3
  203.0 1.5 copy.47
  204.4 3.8 fusion.53
  209.0 7.0 %copy.49 = bf16[4,768,768]{1,2,0:T(8,128)(2,1)} copy(bf16[4,768,768]{2,1,0:T(8,128)(2,1)} %bitcast.193) | data formatting | bytes 9437184 | tf_op jit(solution)/shard_map/reshape | solution.py:649
  216.0 11.0 %fusion.51 = f32[1024,3072]{1,0:T(8,128)} fusion(bf16[768,3072]{0,1:T(8,128)(2,1)} %bitcast.194, f32[1024,768]{1,0:T(8,128)S(1)} %get-tuple-element.86, f32[768]{0:T(1024)S(1)} %add.167, f32[768]{0:T(1024)S(1)} %mul.197, f32[1024]{0:T(1024)S(1)} %add_rsqrt_fusion.2, f32[1024]{0:T(1024)S(1)} %broadcast_multiply_fusion.4), kind=kOutput, calls=%fused_computation.129 | convolution fusion | flops 4835770368 | bytes 20461568 | tf_op jit(solution)/shard_map/dot_general | solution.py:23
  227.0 2.8 copy.48
  231.3 15.5 %fusion.6 = bf16[1024,3072]{1,0:T(8,128)(2,1)S(1)} fusion(f32[1024,3072]{1,0:T(8,128)} %fusion.51, bf16[1024,768]{1,0:T(8,128)(2,1)S(1)} %bitcast.205, bf16[768,3072]{1,0:T(8,128)(2,1)S(1)} %bitcast.188), kind=kOutput, calls=%fused_computation.8 | convolution fusion | flops 4894752768 | bytes 25165824 | tf_op jit(solution)/shard_map/dot_general | solution.py:23
  246.8 5.9 multiply_reduce_fusion.1
  252.8 1.4 multiply_add_fusion
  254.2 1.6 copy-done.6
  255.9 1.4 convolution_convert_fusion.4
  257.7 1.3 copy.88
  259.0 2.6 swap_3.1
  261.7 1.6 constant_dynamic-slice_fusion.1
  263.7 1.3 copy.51
  265.0 60.4 %attention_backward.1 = (bf16[2048,384]{1,0:T(8,128)(2,1)S(1)}, bf16[2048,384]{1,0:T(8,128)(2,1)S(1)}, bf16[2048,384]{1,0:T(8,128)(2,1)}) custom-call(s32[1,2048]{1,0:T(1,128)S(1)} %iota_select_fusion.start_ref, bf16[2048,1152]{1,0:T(8,128)(2,1)} %convolution_convert_fusion.q_ref.k_ref.v_ref, bf16[2048,1152]{1,0:T(8,128)(2,1)} %convolution_convert_fusion.q_ref.k_ref.v_ref, ...), custom_call_target="tpu_custom_call" | custom-call | tf_op jit(solution)/shard_map/attention_backward/pallas_call | solution.py:378
  327.4 6.0 fusion.54
  333.5 1.8 copy.87
  335.3 3.8 swap_4.1
  340.5 3.6 fusion.22
  344.1 2.8 fusion.16
  347.7 10.5 %convolution_convert_fusion.2 = bf16[768,3072]{1,0:T(8,128)(2,1)} fusion(bf16[1024,3072]{1,0:T(8,128)(2,1)} %copy-done.26, f32[1024,768]{1,0:T(8,128)} %copy-done.4, f32[768]{0:T(1024)S(1)} %add.167, f32[768]{0:T(1024)S(1)} %mul.197, f32[1024]{0:T(1024)S(1)} %add_rsqrt_fusion.2, f32[1024]{0:T(1024)S(1)} %broadcast_multiply_fusion.4), kind=kOutput, calls=%fused_computation.20 | convolution fusion | flops 4838129664 | bytes 14170112 | tf_op jit(solution)/shard_map/dot_general | solution.py:23
  358.2 9.7 %reshape.437 = bf16[8,96,4,768]{3,2,1,0:T(4,128)(2,1)} reshape(bf16[768,3072]{1,0:T(8,128)(2,1)} %convolution_convert_fusion.2) | data formatting | bytes 9437184 | tf_op jit(solution)/shard_map/reshape | solution.py:657
  368.0 5.5 copy.56
  373.5 12.8 %add_convert_fusion.1 = bf16[1024,768]{1,0:T(8,128)(2,1)} fusion(f32[1024,768]{1,0:T(8,128)S(1)} %copy-done.5, bf16[768,3072]{1,0:T(8,128)(2,1)} %bitcast.189, f32[1024,3072]{1,0:T(8,128)} %fusion.51), kind=kOutput, calls=%fused_computation.44 | convolution fusion | flops 4861722624 | bytes 22020096 | tf_op jit(solution)/shard_map/dot_general | solution.py:23
  386.3 2.5 convolution_convert_fusion.5
  388.8 4.6 reshape.435
  393.4 2.8 copy.55
  397.5 7.9 %convolution_convert_fusion.3 = bf16[768,1152]{1,0:T(8,128)(2,1)} fusion(bf16[2048,768]{1,0:T(8,128)(2,1)S(1)} %fusion.10, bf16[2048,1152]{1,0:T(8,128)(2,1)} %copy-done.21), kind=kOutput, calls=%fused_computation.21 | convolution fusion | flops 3624763392 | bytes 9633792 | tf_op jit(solution)/shard_map/dot_general | solution.py:23
  405.3 2.6 copy.52
  408.0 8.3 %copy.53 = bf16[768,3,1,384]{3,2,1,0:T(2,128)(2,1)} copy(bf16[768,3,1,384]{0,3,1,2:T(8,128)(2,1)S(1)} %bitcast.182) | data formatting | bytes 3538944 | tf_op jit(solution)/shard_map/reshape | solution.py:763
  416.2 3.6 broadcast_in_dim.47
  419.9 56.4 %dynamic_update_slice.3 = bf16[768,3,2,384]{3,2,1,0:T(2,128)(2,1)} dynamic-update-slice(bf16[768,3,2,384]{3,2,1,0:T(2,128)(2,1)} %broadcast_in_dim.47, bf16[768,3,1,384]{3,2,1,0:T(2,128)(2,1)} %copy.53, s32[]{:T(128)} %constant.71.clone.1, s32[]{:T(128)} %constant.71.clone.1, s32[]{:T(128)S(6)} %select_n.113, s32[]{:T(128)} %constant.71.clone.1) | dynamic-update-slice | bytes 3538948 | tf_op jit(solution)/shard_map/dynamic_update_slice | solution.py:762
  476.2 11.6 %reshape_reshape.7 = bf16[8,96,4,576]{3,2,1,0:T(4,128)(2,1)} reshape(bf16[768,3,2,384]{3,2,1,0:T(2,128)(2,1)} %dynamic_update_slice.3) | data formatting | bytes 7077888 | tf_op jit(solution)/shard_map/reshape;reshape | solution.py:657
  487.8 4.7 copy.54
  492.6 8.8 %convolution_convert_fusion.1 = bf16[768,3072]{1,0:T(8,128)(2,1)S(1)} fusion(bf16[1024,768]{1,0:T(8,128)(2,1)S(1)} %bitcast.206, f32[1024,3072]{1,0:T(8,128)} %fusion.51), kind=kOutput, calls=%fused_computation.19 | convolution fusion | flops 4862509056 | bytes 18874368 | tf_op jit(solution)/shard_map/dot_general | solution.py:23
  502.5 3.0 copy.57
  505.6 133.1 %reduce_all.1 = (f32[96,576]{1,0:T(8,128)}, f32[96,192]{1,0:T(8,128)}, f32[96,768]{1,0:T(8,128)}, f32[192,384]{1,0:T(8,128)}, f32[8,192]{1,0:T(8,128)}, /*index=...) custom-call(bf16[2,2,4,2,96,576]{5,4,3,2,1,0:T(8,128)(2,1)} %bitcast.179, bf16[2,2,4,2,96,192]{5,4,3,2,1,0:T(8,128)(2,1)} %bitcast.184, ...), custom_call_target="tpu_custom_call" | custom-call | tf_op jit(solution)/shard_map/reduce_all/pallas_call | solution.py:614
  638.6 1.4 fusion.52
  640.1 2.7 copy.100
  (124 shorter events, 25.5 us)
Async XLA Ops:
  147.7 3.0 copy-start
  153.2 1.5 copy-start.11
  199.1 2.6 copy-start.1
  199.1 3.8 copy-start.17
  208.3 44.5 %copy-start.4 = (f32[1024,768]{1,0:T(8,128)}, f32[1024,768]{1,0:T(8,128)S(1)}, u32[]{:S(2)}) copy-start(f32[1024,768]{1,0:T(8,128)S(1)} %get-tuple-element.86) | copy-start | bytes 9437188
  216.0 11.0 %slice-start = ((s8[4718592]{0:T(1024)(128)(4,1)}), s8[4194304]{0:T(1024)(128)(4,1)S(1)}, s32[]{:S(2)}) async-start(s8[4718592]{0:T(1024)(128)(4,1)} %bitcast.190), calls=%async_computation | async-start | bytes 8388608
  216.0 11.0 %slice-start.1 = ((s8[4718592]{0:T(1024)(128)(4,1)}), s8[524288]{0:T(1024)(128)(4,1)S(1)}, s32[]{:S(2)}) async-start(s8[4718592]{0:T(1024)(128)(4,1)} %bitcast.190), calls=%async_computation.1 | async-start | bytes 1048576
  229.9 1.4 copy-start.13
  229.9 17.0 %slice-start.2 = ((s8[4718592]{0:T(1024)(128)(4,1)}), s8[4194304]{0:T(1024)(128)(4,1)S(1)}, s32[]{:S(2)}) async-start(s8[4718592]{0:T(1024)(128)(4,1)} %bitcast.195), calls=%async_computation.2 | async-start | bytes 8388608
  231.0 15.8 %copy-start.9 = (bf16[96,8,8,384]{3,1,2,0:T(8,128)(2,1)}, bf16[96,8,8,384]{3,1,2,0:T(8,128)(2,1)S(1)}, u32[]{:S(2)}) copy-start(bf16[96,8,8,384]{3,1,2,0:T(8,128)(2,1)S(1)} %copy.65) | copy-start | bytes 14155780
  231.3 15.6 %slice-start.3 = ((s8[4718592]{0:T(1024)(128)(4,1)}), s8[524288]{0:T(1024)(128)(4,1)S(1)}, s32[]{:S(2)}) async-start(s8[4718592]{0:T(1024)(128)(4,1)} %bitcast.195), calls=%async_computation.3 | async-start | bytes 1048576
  246.8 5.9 copy-start.26
  252.8 3.1 copy-start.18
  254.2 1.6 copy-start.6
  261.7 1.6 copy-start.10
  325.4 1.4 copy-start.16
  325.6 1.8 copy-start.12
  327.4 6.0 copy-start.21
  335.3 3.8 copy-start.2
  339.1 1.4 copy-start.3
  340.5 3.6 copy-start.7
  368.0 5.5 copy-start.5
  373.4 12.9 %copy-start.8 = (f32[1024,768]{1,0:T(8,128)S(1)}, f32[1024,768]{1,0:T(8,128)}, u32[]{:S(2)}) copy-start(f32[1024,768]{1,0:T(8,128)} %copy-done.6) | copy-start | bytes 9437188
  373.4 12.9 %copy-start.19 = (bf16[1024,384]{1,0:T(8,128)(2,1)S(1)}, bf16[1024,384]{1,0:T(8,128)(2,1)}, u32[]{:S(2)}) copy-start(bf16[1024,384]{1,0:T(8,128)(2,1)} %get-tuple-element.71) | copy-start | bytes 2359300
  373.4 12.9 %copy-start.20 = (bf16[1024,384]{1,0:T(8,128)(2,1)S(1)}, bf16[1024,384]{1,0:T(8,128)(2,1)}, u32[]{:S(2)}) copy-start(bf16[1024,384]{1,0:T(8,128)(2,1)} %get-tuple-element.72) | copy-start | bytes 2359300
  487.8 4.7 copy-start.14
  638.6 4.2 copy-start.15
  640.1 3.9 copy-start.24
  640.1 4.6 copy-start.25
  640.1 5.2 copy-start.23
  640.1 5.9 copy-start.22

commit v2 on v1

v2 whole, which is shorter than its diff:
```python
import functools

import jax
import jax.numpy as jnp
from jax import lax
from jax.experimental import pallas as pl
from jax.experimental.pallas import tpu as pltpu
from jax.sharding import PartitionSpec as P

HEADS = 12
HEAD_DIM = 64
CORES = 2
LANE_X = 2
MESH = pl.DeviceIdType.MESH
LOG2E = 1.4426950408889634
epsilon = 1e-05
masked = -1e30
bf16 = jnp.bfloat16
f32 = jnp.float32


def dot(left, right, left_dim, right_dim):
    return lax.dot_general(
        left, right, (((left_dim,), (right_dim,)), ((), ())), preferred_element_type=f32
    )


class Place:
    def __init__(self, sizes):
        self.batch, self.blk = sizes
        self.Z, self.X = self.batch // LANE_X, LANE_X
        self.Y, self.C = self.blk // CORES, CORES

    def here(self):
        b, d = lax.axis_index("batch"), lax.axis_index("blk")
        return b // self.X, b % self.X, d // self.C, d % self.C

    def device(self, z, x, p, c):
        return (z * self.X + x, p * self.C + c)


def split_rows(count):
    return 16 * ((count // 2) // 16)


class Sends:
    def __init__(self, send_sem, recv_sem):
        self.send_sem, self.recv_sem, self.count = send_sem, recv_sem, 0

    def start(self, src, dst, device):
        copy = pltpu.make_async_remote_copy(
            src_ref=src,
            dst_ref=dst,
            send_sem=self.send_sem.at[self.count],
            recv_sem=self.recv_sem.at[self.count],
            device_id=device,
            device_id_type=MESH,
        )
        self.count += 1
        copy.start()
        return copy


def greet(place, partners):
    barrier = pltpu.get_barrier_semaphore()
    for partner in partners:
        pl.semaphore_signal(barrier, inc=1, device_id=partner, device_id_type=MESH)
    pl.semaphore_wait(barrier, len(partners))


def partners_of(place):
    z, x, p, c = place.here()
    found = [place.device((z + k) % place.Z, x, p, c) for k in range(1, place.Z)]
    found += [place.device(z, 1 - x, p, c)]
    found += [place.device(z, x, (p + k) % place.Y, c) for k in range(1, place.Y)]
    found += [place.device(z, x, p, 1 - c)]
    return found


def gather_kernel(place, matrices, *refs):
    n = len(matrices)
    mats, (tok, cot, tag, vec) = refs[:n], refs[n : n + 4]
    outs, (tok_g, cot_g, tag_g, vec_g) = refs[n + 4 : 2 * n + 4], refs[2 * n + 4 : 2 * n + 8]
    send_sem, recv_sem, local_sem = refs[2 * n + 8 :]
    z, x, p, c = place.here()
    Z, X, Y = place.Z, place.X, place.Y
    greet(place, partners_of(place))
    sends = Sends(send_sem, recv_sem)
    started = []

    def go(src, dst, device):
        copy = sends.start(src, dst, device)
        started.append(copy)
        return copy

    local = []

    def keep(src, dst):
        copy = pltpu.make_async_copy(src, dst, local_sem.at[len(local)])
        copy.start()
        local.append(copy)
        return copy

    row_copies, cot_copies = [], []
    for k in range(1, Y):
        to = (p + k) % Y
        device = place.device(z, x, to, c)
        row_copies.append(go(tok.at[to], tok_g.at[p, c], device))
        row_copies.append(go(tag.at[to], tag_g.at[p, c], device))
        row_copies.append(go(vec, vec_g.at[p, c], device))
    own = [
        keep(tok.at[p], tok_g.at[p, c]),
        keep(tag.at[p], tag_g.at[p, c]),
        keep(vec, vec_g.at[p, c]),
        keep(cot.at[p], cot_g.at[p]),
    ]
    first = []
    for m in range(n):
        place_here = outs[m].at[p, c, z, x]
        keep(mats[m], place_here)
        first.append(
            [
                go(mats[m], place_here, place.device((z + k) % Z, x, p, c))
                for k in range(1, Z)
            ]
        )
    for k in range(1, Y):
        to = (p + k) % Y
        cot_copies.append(go(cot.at[to], cot_g.at[p], place.device(z, x, to, c)))
    for copy in local:
        copy.wait()
    second = []
    for m in range(n):
        for copy in first[m]:
            copy.wait_recv()
        h = split_rows(mats[m].shape[0])
        r = mats[m].shape[0]
        low = outs[m].at[p, c, :, x, 0:h]
        high = outs[m].at[p, c, :, x, h:r]
        second.append(
            (
                [go(low, low, place.device(z, 1 - x, p, c))],
                [go(high, high, place.device(z, x, (p + k) % Y, c)) for k in range(1, Y)],
            )
        )
    third = []
    for m in range(n):
        h = split_rows(mats[m].shape[0])
        r = mats[m].shape[0]
        for copy in second[m][0]:
            copy.wait_recv()
        low = outs[m].at[p, c, :, :, 0:h]
        a = [go(low, low, place.device(z, x, (p + k) % Y, c)) for k in range(1, Y)]
        for copy in second[m][1]:
            copy.wait_recv()
        high = outs[m].at[:, c, :, x, h:r]
        b = [go(high, high, place.device(z, 1 - x, p, c))]
        third.append(a + b)
    for copy in row_copies:
        copy.wait_recv()
    sibling = place.device(z, x, p, 1 - c)
    last = []
    for ref in (tok_g, tag_g, vec_g):
        last.append(go(ref.at[:, c], ref.at[:, c], sibling))
    for m in range(n):
        for copy in third[m]:
            copy.wait_recv()
        last.append(go(outs[m].at[:, c], outs[m].at[:, c], sibling))
    for copy in last + cot_copies:
        copy.wait_recv()
    for copy in started:
        copy.wait_send()


def gather_all(place, mats, tok, cot, tag, vec):
    n = len(mats)
    Z, X, Y, C = place.Z, place.X, place.Y, place.C
    out = [jax.ShapeDtypeStruct((Y, C, Z, X) + m.shape, m.dtype) for m in mats]
    out += [
        jax.ShapeDtypeStruct((Y, C) + tok.shape[1:], tok.dtype),
        jax.ShapeDtypeStruct((Y,) + cot.shape[1:], cot.dtype),
        jax.ShapeDtypeStruct((Y, C) + tag.shape[1:], tag.dtype),
        jax.ShapeDtypeStruct((Y, C) + vec.shape, vec.dtype),
    ]
    copies = 4 * (Y - 1) + n * ((Z - 1) + 1 + (Y - 1) + (Y - 1) + 1) + 3 + n
    anywhere = pl.BlockSpec(memory_space=pl.ANY)
    return pl.pallas_call(
        functools.partial(gather_kernel, place, tuple(m.shape for m in mats)),
        out_shape=out,
        in_specs=[anywhere] * (n + 4),
        out_specs=[anywhere] * (n + 4),
        scratch_shapes=[
            pltpu.SemaphoreType.DMA((copies,)),
            pltpu.SemaphoreType.DMA((copies,)),
            pltpu.SemaphoreType.DMA((n + 4,)),
        ],
        compiler_params=pltpu.CompilerParams(collective_id=0, has_side_effects=True),
        name="gather_all",
    )(*mats, tok, cot, tag, vec)


def swap_kernel(place, src, dst, send_sem, recv_sem):
    z, x, p, c = place.here()
    sibling = place.device(z, x, p, 1 - c)
    greet(place, [sibling])
    copy = pltpu.make_async_remote_copy(
        src_ref=src.at[1 - c],
        dst_ref=dst,
        send_sem=send_sem,
        recv_sem=recv_sem,
        device_id=sibling,
        device_id_type=MESH,
    )
    copy.start()
    copy.wait()


def swap(place, value, number):
    anywhere = pl.BlockSpec(memory_space=pl.ANY)
    return pl.pallas_call(
        functools.partial(swap_kernel, place),
        out_shape=jax.ShapeDtypeStruct(value.shape[1:], value.dtype),
        in_specs=[anywhere],
        out_specs=anywhere,
        scratch_shapes=[pltpu.SemaphoreType.DMA, pltpu.SemaphoreType.DMA],
        compiler_params=pltpu.CompilerParams(collective_id=number, has_side_effects=True),
        name=f"swap_{number}",
    )(value)


def head_masked(value, h, axis):
    index = lax.broadcasted_iota(jnp.int32, value.shape, axis)
    return jnp.where((index // HEAD_DIM) == h, value, jnp.zeros_like(value))


def attention_forward_kernel(BQ, start_ref, q_ref, k_ref, v_ref, o_ref, oT_ref, lt_ref, qT, vT):
    L = q_ref.shape[0]
    nq = L // BQ
    scale = HEAD_DIM ** (-0.5) * LOG2E
    qT[...] = q_ref[...].T
    vT[...] = v_ref[...].T
    for qi in range(nq):
        qs = slice(qi * BQ, (qi + 1) * BQ)
        begin = start_ref[:, qs]
        d0 = qi * BQ
        if qi == nq - 1:
            cuts = [(0, d0, 1)] if d0 else []
        elif d0 > 256:
            cuts = [(0, 256, 1), (256, d0, 0)]
        else:
            cuts = [(0, d0, 1)] if d0 else []
        cuts.append((d0, d0 + BQ, 2))
        for h in range(2):
            query = head_masked(qT[:, qs], h, 0)
            parts = []
            for a, b, mode in cuts:
                s = dot(k_ref[a:b, :], query, 1, 0) * scale
                if mode:
                    key_pos = lax.broadcasted_iota(jnp.int32, (b - a, BQ), 0) + a
                    visible = key_pos >= begin
                    if mode == 2:
                        query_pos = lax.broadcasted_iota(jnp.int32, (b - a, BQ), 1) + d0
                        visible = jnp.logical_and(visible, key_pos <= query_pos)
                    s = jnp.where(visible, s, masked)
                parts.append(s)
            top = functools.reduce(
                jnp.maximum, [jnp.max(s, axis=0, keepdims=True) for s in parts]
            )
            total, accum = 0.0, 0.0
            for (a, b, mode), s in zip(cuts, parts):
                e = jnp.exp2(s - top)
                total = total + jnp.sum(e, axis=0, keepdims=True)
                accum = accum + dot(
                    vT[h * HEAD_DIM : (h + 1) * HEAD_DIM, a:b], e.astype(bf16), 1, 0
                )
            oT_ref[h * HEAD_DIM : (h + 1) * HEAD_DIM, qs] = accum / total
            lt_ref[0, h : h + 1, qs] = top + jnp.log2(total)
        o_ref[qs, :] = oT_ref[:, qs].astype(bf16).T


def attention_forward(projected, begin):
    L = projected.shape[0]
    pairs = projected.shape[1] // 3 // 128
    return pl.pallas_call(
        functools.partial(attention_forward_kernel, 512),
        grid=(pairs,),
        in_specs=[
            pl.BlockSpec((1, L), lambda i: (0, 0)),
            pl.BlockSpec((L, 128), lambda i: (0, i)),
            pl.BlockSpec((L, 128), lambda i: (0, pairs + i)),
            pl.BlockSpec((L, 128), lambda i: (0, 2 * pairs + i)),
        ],
        out_specs=[
            pl.BlockSpec((L, 128), lambda i: (0, i)),
            pl.BlockSpec((128, L), lambda i: (i, 0)),
            pl.BlockSpec((1, 2, L), lambda i: (i, 0, 0)),
        ],
        out_shape=[
            jax.ShapeDtypeStruct((L, pairs * 128), bf16),
            jax.ShapeDtypeStruct((pairs * 128, L), f32),
            jax.ShapeDtypeStruct((pairs, 2, L), f32),
        ],
        scratch_shapes=[pltpu.VMEM((128, L), bf16), pltpu.VMEM((128, L), bf16)],
        compiler_params=pltpu.CompilerParams(vmem_limit_bytes=50 << 20),
        name="attention_forward",
    )(begin, projected, projected, projected)


class Wire:
    def __init__(self, send_sem, recv_sem):
        self.send_sem, self.recv_sem, self.names = send_sem, recv_sem, {}

    def copy(self, name, src, dst, device):
        i = self.names.setdefault(name, len(self.names))
        return pltpu.make_async_remote_copy(
            src_ref=src,
            dst_ref=dst,
            send_sem=self.send_sem.at[i],
            recv_sem=self.recv_sem.at[i],
            device_id=device,
            device_id_type=MESH,
        )


def start_all(copies):
    for copy in copies:
        copy.start()


def arrive_all(copies):
    for copy in copies:
        copy.wait_recv()


def leave_all(copies):
    for copy in copies:
        copy.wait_send()


def first_rows(rows, sixths):
    return min(rows - 16, 16 * ((rows * sixths // 6) // 16)) if rows > 16 else 0


class Summing:
    def __init__(self, place, wire, name, spots, acc, xa, yb, ya, xb, zz):
        self.place, self.wire, self.name, self.spots = place, wire, name, spots
        self.acc, self.xa, self.yb, self.ya, self.xb, self.zz = acc, xa, yb, ya, xb, zz
        self.rows = acc.shape[3]
        self.h = xa.shape[2]

    def one(self):
        z, x, p, c = self.spots
        place, h, r = self.place, self.h, self.rows
        side = place.device(z, 1 - x, p, c)
        found = [
            self.wire.copy((self.name, "xa"), self.acc.at[:, :, 1 - x, 0:h], self.xa, side)
        ]
        for k in range(1, place.Y):
            to = (p + k) % place.Y
            found.append(
                self.wire.copy(
                    (self.name, "yb", k),
                    self.acc.at[to, :, :, h:r],
                    self.yb.at[k - 1],
                    place.device(z, x, to, c),
                )
            )
        return found

    def two(self):
        z, x, p, c = self.spots
        place, h, r = self.place, self.h, self.rows
        found = []
        for k in range(1, place.Y):
            to = (p + k) % place.Y
            found.append(
                self.wire.copy(
                    (self.name, "ya", k),
                    self.acc.at[to, :, x, 0:h],
                    self.ya.at[k - 1],
                    place.device(z, x, to, c),
                )
            )
        side = place.device(z, 1 - x, p, c)
        found.append(
            self.wire.copy((self.name, "xb"), self.acc.at[p, :, 1 - x, h:r], self.xb, side)
        )
        return found

    def three(self):
        z, x, p, c = self.spots
        place = self.place
        found = []
        for k in range(1, place.Z):
            to = (z + k) % place.Z
            found.append(
                self.wire.copy(
                    (self.name, "z", k),
                    self.acc.at[p, to, x],
                    self.zz.at[k - 1],
                    place.device(to, x, p, c),
                )
            )
        return found

    def add_one(self):
        z, x, p, c = self.spots
        place, h, r, acc = self.place, self.h, self.rows, self.acc
        ones = self.one()
        ones[0].wait_recv()

        def low(i, nothing):
            a, b = i // place.Z, i % place.Z
            total = acc[a, b, x, 0:h].astype(f32) + self.xa[a, b].astype(f32)
            acc[a, b, x, 0:h] = total.astype(bf16)
            return nothing

        lax.fori_loop(0, place.Y * place.Z, low, 0)
        twos = self.two()
        start_all(twos[:-1])
        arrive_all(ones[1:])

        def high(i, nothing):
            a, b = i // place.X, i % place.X
            total = acc[p, a, b, h:r].astype(f32)
            for k in range(place.Y - 1):
                total = total + self.yb[k, a, b].astype(f32)
            acc[p, a, b, h:r] = total.astype(bf16)
            return nothing

        lax.fori_loop(0, place.Z * place.X, high, 0)
        twos[-1].start()

    def add_two(self):
        z, x, p, c = self.spots
        place, h, r, acc = self.place, self.h, self.rows, self.acc
        arrive_all(self.two())

        def both(i, nothing):
            total = acc[p, i, x, 0:h].astype(f32)
            for k in range(place.Y - 1):
                total = total + self.ya[k, i].astype(f32)
            acc[p, i, x, 0:h] = total.astype(bf16)
            total = acc[p, i, x, h:r].astype(f32) + self.xb[i].astype(f32)
            acc[p, i, x, h:r] = total.astype(bf16)
            return nothing

        lax.fori_loop(0, place.Z, both, 0)
        start_all(self.three())

    def finish(self, target):
        z, x, p, c = self.spots
        arrive_all(self.three())
        total = self.acc[p, z, x].astype(f32)
        for k in range(self.place.Z - 1):
            total = total + self.zz[k].astype(f32)
        target[...] = total

    def leave(self):
        leave_all(self.one())
        leave_all(self.two())
        leave_all(self.three())


def backward_kernel(place, n, BQ, *refs):
    (begin, proj, ga, oT_in, lt, normedT, w_in, tok, gm, out_in, vec, vec_two) = refs[:12]
    parts = refs[12 : 12 + n]
    outs = refs[12 + n :]
    sums, (vec_out, out_home, tg_home) = outs[: n + 1], outs[n + 1 : n + 4]
    landing = outs[n + 4 : 2 * n + 4]
    rest = outs[2 * n + 4 :]
    (
        pv, do, oT, wv, kT, dk, dv, nT, pacc, p_recv,
        keep, g_send, g_recv, tok_v, gm_v, grads, v0, v1, v2, v3, vc, vy, vx, vz,
    ) = rest[:24]
    buffers = rest[24 : 24 + 6 * (n + 1)]
    send_sem, recv_sem, local_sem = rest[24 + 6 * (n + 1) :]
    tg_v = g_recv
    spots = place.here()
    z, x, p, c = spots
    Z, X, Y, C = place.Z, place.X, place.Y, place.C
    L, W3 = pv.shape
    H = W3 // 3
    D = wv.shape[0]
    T = L // (Y * C)
    pairs = H // 128
    nq = L // BQ
    scale = HEAD_DIM ** (-0.5) * LOG2E
    scale_back = HEAD_DIM ** (-0.5)
    wire = Wire(send_sem, recv_sem)
    sibling = place.device(z, x, p, 1 - c)
    beside = place.device(z, 1 - x, p, c)
    adds = [
        Summing(place, wire, m, spots, *buffers[6 * m : 6 * m + 6]) for m in range(n + 1)
    ]

    def local(i, src, dst):
        return pltpu.make_async_copy(src, dst, local_sem.at[i])

    def lane(offset, size):
        return pl.ds(pl.multiple_of(offset, 128), size)

    def line(offset, size):
        return pl.ds(pl.multiple_of(offset, 16), size)

    def grad_swap():
        return [
            wire.copy(
                ("ga", q),
                ga.at[q * T : (q + 1) * T, lane((1 - c) * H, H)],
                do.at[line((2 * q + c) * T, T), :],
                sibling,
            )
            for q in range(Y)
        ]

    def core_sends(m):
        return [wire.copy(("core", m), parts[m].at[:, 1 - c], landing[m], sibling)]

    def out_sends():
        found = []
        for k in range(1, Y):
            to = (p + k) % Y
            found.append(
                wire.copy(
                    ("out", k), out_in.at[line(to * T, T)], out_home.at[p], place.device(z, x, to, c)
                )
            )
        return found

    greet(place, partners_of(place))
    start_all(grad_swap())
    own = [
        local(q, ga.at[q * T : (q + 1) * T, lane(c * H, H)], do.at[line((2 * q + c) * T, T), :])
        for q in range(Y)
    ]
    def out_fetch(qi):
        return local(Y + 1, oT_in.at[:, lane(qi * BQ, BQ)], oT)

    loads = [local(Y, proj, pv), local(Y + 2, w_in, wv)]
    out_fetch(nq - 1).start()
    out_own = local(Y + 3, out_in.at[line(p * T, T)], out_home.at[p])
    acc_own = [
        local(Y + 4 + m, parts[m].at[:, c], adds[m + 1].acc) for m in range(n)
    ]
    start_all(own + loads)
    for m in range(n):
        start_all(core_sends(m))
    start_all(out_sends())
    start_all(acc_own + [out_own])
    row_sem = Y + 4 + n

    def core_add(m):
        arrive_all(core_sends(m))
        acc_own[m].wait()
        acc, other = adds[m + 1].acc, landing[m]

        def one(i, nothing):
            a, b, d = i // (Z * X), (i // X) % Z, i % X
            total = acc[a, b, d].astype(f32) + other[a, b, d].astype(f32)
            acc[a, b, d] = total.astype(bf16)
            return nothing

        lax.fori_loop(0, Y * Z * X, one, 0)
        start_all(adds[m + 1].one())

    for copy in loads:
        copy.wait()
    kT[...] = pv[:, H : 2 * H].T
    dk[...] = jnp.zeros_like(dk)
    dv[...] = jnp.zeros_like(dv)
    pacc[...] = jnp.zeros_like(pacc)
    grads[...] = jnp.zeros_like(grads)
    for copy in own:
        copy.wait()
    arrive_all(grad_swap())

    U = BQ // T
    gain = vec[0:1, :]

    def sub_blocks(qi):
        found = []
        for u in range(U):
            block = qi * U + u
            found.append((u, block // C, block % C))
        return found

    reserved = send_sem.shape[0] - 3 * Y

    def g_wire(q):
        return pltpu.make_async_remote_copy(
            src_ref=g_send.at[q],
            dst_ref=g_recv.at[q],
            send_sem=send_sem.at[reserved + q],
            recv_sem=recv_sem.at[reserved + q],
            device_id=sibling,
            device_id_type=MESH,
        )

    def home_from(k):
        q = (p + k) % Y
        return pltpu.make_async_remote_copy(
            src_ref=tg_v.at[p],
            dst_ref=tg_home.at[q],
            send_sem=send_sem.at[reserved + Y + q],
            recv_sem=recv_sem.at[reserved + 2 * Y + q],
            device_id=place.device(z, x, q, c),
            device_id_type=MESH,
        )

    def home_to(q):
        return pltpu.make_async_remote_copy(
            src_ref=tg_v.at[q],
            dst_ref=tg_home.at[p],
            send_sem=send_sem.at[reserved + Y + q],
            recv_sem=recv_sem.at[reserved + 2 * Y + p],
            device_id=place.device(z, x, q, c),
            device_id_type=MESH,
        )

    def block_done(qi):
        qs = line(qi * BQ, BQ)
        fetch = local(row_sem, normedT.at[:, lane(qi * BQ, BQ)], nT)
        fetch.start()
        pv[qs, H : 2 * H] = (dk[qs, :] * scale_back).astype(bf16)
        pv[qs, 2 * H :] = dv[qs, :].astype(bf16)
        g = dot(pv[qs, :], wv[...], 1, 1)
        for u, q, owner in sub_blocks(qi):
            rows = slice(u * T, (u + 1) * T)

            @pl.when(owner == c)
            def _():
                keep[u // C] = g[rows, :]

            @pl.when(owner != c)
            def _():
                g_send[q] = g[rows, :].astype(bf16)
                g_wire(q).start()

        fetch.wait()
        pacc[...] += dot(nT[...], pv[qs, :], 1, 0)

    def token_rows(qi):
        for u, q, owner in sub_blocks(qi):

            @pl.when(owner == c)
            def _():
                a = local(row_sem, tok.at[line(q * T, T)], tok_v)
                b = local(row_sem + 1, gm.at[line(q * T, T)], gm_v)
                a.start()
                b.start()
                g_wire(q).wait_recv()
                grad = keep[u // C] + g_recv[q].astype(f32)
                a.wait()
                unit, factor = normed(tok_v[...].astype(f32))
                grads[0:1, :] += jnp.sum(grad * unit, axis=0, keepdims=True)
                grads[1:2, :] += jnp.sum(grad, axis=0, keepdims=True)
                b.wait()
                tg_v[q] = (gm_v[...] + norm_back(grad, gain, unit, factor)).astype(bf16)

                @pl.when(q == p)
                def _():
                    local(row_sem + 2, tg_v.at[q], tg_home.at[p]).start()

                @pl.when(q != p)
                def _():
                    home_to(q).start()

    def step(s, nothing):
        qi = nq - 1 - s // pairs
        pair = s % pairs
        qs = line(qi * BQ, BQ)
        ql = lane(qi * BQ, BQ)
        cols = lane(pair * 128, 128)
        k_cols, v_cols = lane(H + pair * 128, 128), lane(2 * H + pair * 128, 128)
        q_val, do_val = pv[qs, cols], do[qs, cols]
        qT_val, doT_val = q_val.T, do_val.T
        heads = []

        @pl.when(pair == 0)
        def _():
            out_fetch(qi).wait()

        for h in range(2):
            rows = slice(h * HEAD_DIM, (h + 1) * HEAD_DIM)
            head_rows = pl.ds(pl.multiple_of(pair * 128 + h * HEAD_DIM, HEAD_DIM), HEAD_DIM)
            delta = jnp.sum(
                doT_val[rows, :].astype(f32) * oT[head_rows, :], axis=0, keepdims=True
            )
            heads.append(
                (
                    head_masked(qT_val, h, 0),
                    head_masked(doT_val, h, 0),
                    head_masked(q_val, h, 1),
                    head_masked(do_val, h, 1),
                    delta,
                    lt[pair, h : h + 1, ql],
                    head_rows,
                )
            )

        @pl.when(jnp.logical_and(pair == pairs - 1, qi > 0))
        def _():
            out_fetch(qi - 1).start()

        def tile(kj, dqs, mode):
            ks = line(kj * BQ, BQ)
            kl = lane(kj * BQ, BQ)
            if mode:
                key_pos = lax.broadcasted_iota(jnp.int32, (BQ, BQ), 0)
                visible = key_pos >= (begin[:, ql] - kj * BQ)
                if mode == 2:
                    query_pos = lax.broadcasted_iota(jnp.int32, (BQ, BQ), 1)
                    visible = jnp.logical_and(visible, key_pos <= query_pos)
            more_dv, more_dk, found = 0.0, 0.0, []
            for h in range(2):
                query, grad, q_nat, do_nat, delta, log_total, head_rows = heads[h]
                sc = dot(pv[ks, k_cols], query, 1, 0) * scale
                prob = jnp.exp2(sc - log_total)
                if mode:
                    prob = jnp.where(visible, prob, 0.0)
                dp = dot(pv[ks, v_cols], grad, 1, 0)
                ds = (prob * (dp - delta)).astype(bf16)
                more_dv = more_dv + dot(prob.astype(bf16), do_nat, 1, 0)
                more_dk = more_dk + dot(ds, q_nat, 1, 0)
                found.append(dqs[h] + dot(kT[head_rows, kl], ds, 1, 0))
            dv[ks, cols] += more_dv
            dk[ks, cols] += more_dk
            return tuple(found)

        zero = jnp.zeros((HEAD_DIM, BQ), f32)
        dqs = tile(qi, (zero, zero), 2)

        def last(d):
            return lax.fori_loop(0, qi, lambda kj, e: tile(kj, e, 1), d)

        def others(d):
            d = lax.cond(qi > 0, lambda e: tile(0, e, 1), lambda e: e, d)
            return lax.fori_loop(1, qi, lambda kj, e: tile(kj, e, 0), d)

        dqs = lax.cond(qi == nq - 1, last, others, dqs)
        dq = jnp.concatenate(dqs, axis=0) * scale_back
        pv[qs, cols] = dq.astype(bf16).T

        def at(number, *events):
            @pl.when(s == number)
            def _():
                for event in events:
                    event()

        @pl.when(pair == pairs - 1)
        def _():
            block_done(qi)

        @pl.when(jnp.logical_and(pair == 0, qi < nq - 1))
        def _():
            token_rows(qi + 1)

        def do_it(f, *args):
            return lambda: f(*args)

        out_m, up_m, down_m = 0, 1, 2
        at(0, do_it(core_add, down_m))
        at(1, do_it(core_add, out_m))
        at(3, adds[up_m + 1].add_one)
        at(7, adds[up_m + 1].add_two)
        at(8, adds[down_m + 1].add_one)
        at(9, adds[out_m + 1].add_one)
        return nothing

    core_add(1)
    lax.fori_loop(0, nq * pairs, step, 0)
    p_send = pv.at[0:D, :]
    p_send[...] = pacc[...].astype(bf16)
    p_swap = wire.copy("p", p_send, p_recv, sibling)
    p_swap.start()
    adds[3].add_two()
    token_rows(0)
    p_swap.wait_recv()
    acc = adds[0].acc
    r, w = acc.shape[3:]
    for mine in range(C):

        @pl.when(c == mine)
        def _():
            for q in range(Y):
                low_col = w * (C * q + mine)
                for third in range(3):
                    for half in range(C):
                        base = third * D + half * H
                        a, b = max(base, low_col), min(base + H, low_col + w)
                        if a >= b:
                            continue
                        source = p_send if half == mine else p_recv
                        off = third * H - base
                        for i in range(Z * X):
                            acc[q, i // X, i % X, :, a - low_col : b - low_col] = source[
                                i * r : (i + 1) * r, a + off : b + off
                            ]

    start_all(adds[0].one())
    grads[2:4, :] = vec_two[...]
    v0[0:4, :] = grads[0:4, 0:H]
    v0[4:8, :] = grads[0:4, H:]
    v_core = wire.copy("vc", v0, vc, sibling)
    v_core.start()
    adds[1].add_two()
    v_core.wait_recv()
    v1[...] = v0[...] + vc[...]
    v_y = [
        wire.copy(("vy", k), v1, vy.at[k - 1], place.device(z, x, (p + k) % Y, c))
        for k in range(1, Y)
    ]
    start_all(v_y)
    adds[2].finish(sums[2])
    adds[0].add_one()
    arrive_all(v_y)
    total = v1[...]
    for k in range(Y - 1):
        total = total + vy[k]
    v2[...] = total
    v_x = wire.copy("vx", v2, vx, beside)
    v_x.start()
    adds[3].finish(sums[3])
    adds[0].add_two()
    v_x.wait_recv()
    v3[...] = v2[...] + vx[...]
    v_z = [
        wire.copy(("vz", k), v3, vz.at[k - 1], place.device((z + k) % Z, x, p, c))
        for k in range(1, Z)
    ]
    start_all(v_z)
    adds[1].finish(sums[1])
    adds[0].finish(sums[0])
    arrive_all(v_z)
    total = v3[...]
    for k in range(Z - 1):
        total = total + vz[k]
    vec_out[...] = total
    for k in range(1, Y):
        home_from(k).wait_recv()
        home_to((p + k) % Y).wait_send()
    local(row_sem + 2, tg_v.at[p], tg_home.at[p]).wait()
    out_own.wait()
    arrive_all(out_sends())
    leave_all(out_sends())
    leave_all(grad_swap())
    for q in range(Y):
        g_wire(q).wait_send()
    for m in range(n):
        leave_all(core_sends(m))
    p_swap.wait_send()
    v_core.wait_send()
    leave_all(v_y)
    v_x.wait_send()
    leave_all(v_z)
    for summing in adds:
        summing.leave()


def backward(place, parts, proj_shape, begin, proj, ga, oT, lt, normedT, w_own, tok, gm, out, vec, vec_two):
    n = len(parts)
    Z, X, Y, C = place.Z, place.X, place.Y, place.C
    L, W3 = proj.shape
    H = W3 // 3
    D = w_own.shape[0]
    T = L // (Y * C)
    BQ = 512
    inside = pl.BlockSpec(memory_space=pltpu.VMEM)
    anywhere = pl.BlockSpec(memory_space=pl.ANY)
    shapes = [proj_shape] + [part.shape[4:] for part in parts]
    sixths = [3, 4, 5, 5]
    out_shape = [jax.ShapeDtypeStruct(shape, f32) for shape in shapes]
    out_shape += [
        jax.ShapeDtypeStruct((8, H), f32),
        jax.ShapeDtypeStruct((Y, T, D), bf16),
        jax.ShapeDtypeStruct((Y, T, D), bf16),
    ]
    scratch = [pltpu.VMEM((Y, Z, X) + shape, bf16) for shape in shapes[1:]]
    scratch += [
        pltpu.VMEM((L, W3), bf16),
        pltpu.VMEM((L, H), bf16),
        pltpu.VMEM((H, BQ), f32),
        pltpu.VMEM((D, W3), bf16),
        pltpu.VMEM((H, L), bf16),
        pltpu.VMEM((L, H), f32),
        pltpu.VMEM((L, H), f32),
        pltpu.VMEM((D, BQ), bf16),
        pltpu.VMEM((D, W3), f32),
        pltpu.VMEM((D, W3), bf16),
        pltpu.VMEM((max(1, BQ // T // C), T, D), f32),
        pltpu.VMEM((Y, T, D), bf16),
        pltpu.VMEM((Y, T, D), bf16),
        pltpu.VMEM((T, D), bf16),
        pltpu.VMEM((T, D), f32),
    ]
    scratch += [pltpu.VMEM((8, D), f32)] + [pltpu.VMEM((8, H), f32)] * 5
    scratch += [
        pltpu.VMEM((Y - 1, 8, H), f32),
        pltpu.VMEM((8, H), f32),
        pltpu.VMEM((Z - 1, 8, H), f32),
    ]
    for shape, part in zip(shapes, sixths):
        r, w = shape
        h = first_rows(r, part)
        scratch += [
            pltpu.VMEM((Y, Z, X, r, w), bf16),
            pltpu.VMEM((Y, Z, h, w), bf16),
            pltpu.VMEM((Y - 1, Z, X, r - h, w), bf16),
            pltpu.VMEM((Y - 1, Z, h, w), bf16),
            pltpu.VMEM((Z, r - h, w), bf16),
            pltpu.VMEM((Z - 1, r, w), bf16),
        ]
    each = 1 + (Y - 1) + (Y - 1) + 1 + (Z - 1)
    copies = Y + n + (Y - 1) + (n + 1) * each + 2 + (Y - 1) + 1 + (Z - 1) + 3 * Y
    scratch += [
        pltpu.SemaphoreType.DMA((copies,)),
        pltpu.SemaphoreType.DMA((copies,)),
        pltpu.SemaphoreType.DMA((Y + 4 + n + 3,)),
    ]
    return pl.pallas_call(
        functools.partial(backward_kernel, place, n, BQ),
        out_shape=out_shape,
        in_specs=[inside] + [anywhere] * 3 + [inside] + [anywhere] * 5 + [inside] * 2 + [anywhere] * n,
        out_specs=[inside] * (n + 2) + [anywhere] * 2,
        scratch_shapes=scratch,
        compiler_params=pltpu.CompilerParams(
            collective_id=1, has_side_effects=True, vmem_limit_bytes=63 << 20
        ),
        name="backward",
    )(begin, proj, ga, oT, lt, normedT, w_own, tok, gm, out, vec, vec_two, *parts)


def gelu_both(u):
    k = 0.7978845608028654
    square = u * u
    t = jnp.tanh(k * u * (1.0 + 0.044715 * square))
    half = 0.5 * (1.0 + t)
    slope = half + 0.5 * k * u * (1.0 - t * t) * (1.0 + 3 * 0.044715 * square)
    return u * half, slope


def dense_kernel(
    place, aligned, att, tok, cot, out_w, up_w, down_w, vec,
    output, gm_out, ga_out, up_p, down_p, out_p, vec_out,
    att_v, tok_v, cot_v, out_v, up_v, down_v, out_full, mid, n2, act, gh, n2T, cotT, g2,
    wide, stage, load_sem, store_sem,
):
    S, nb = place.blk, place.batch
    M, D = att_v.shape
    FF = up_v.shape[1]
    J = FF // D
    loads = []

    def load(src, dst):
        copy = pltpu.make_async_copy(src, dst, load_sem.at[len(loads)])
        copy.start()
        loads.append(copy)
        return copy

    first = [load(att, att_v), load(tok, tok_v), load(out_w, out_v)]
    first.append(load(cot, cot_v))
    if aligned:
        w = up_w.shape[2]
        weights = [load(up_w.at[d], up_v.at[:, d * w : (d + 1) * w]) for d in range(S)]
        r, w = down_w.shape[2:]
        for d in range(S):
            for b in range(nb):
                weights.append(
                    load(
                        down_w.at[d, b],
                        down_v.at[d * r : (d + 1) * r, b * w : (b + 1) * w],
                    )
                )
    else:
        weights = [load(up_w, up_v), load(down_w, down_v)]
    for copy in first:
        copy.wait()
    w = out_v.shape[2]
    for d in range(S):
        out_full[:, d * w : (d + 1) * w] = out_v[d]
    gain, shift = vec[2:3, :], vec[3:4, :]
    T = M // 2
    for t in range(2):
        ts = slice(t * T, (t + 1) * T)
        middle = tok_v[ts, :].astype(f32) + dot(att_v[ts, :], out_full[...], 1, 0)
        unit, factor = normed(middle)
        mid[ts, :] = middle
        n2[ts, :] = (unit * gain + shift).astype(bf16)
    for copy in weights:
        copy.wait()
    n2T[...] = n2[...].T
    cotT[...] = cot_v[...].T
    gain_sum = jnp.zeros((1, D), f32)
    shift_sum = jnp.zeros((1, D), f32)
    stores = [None, None]
    for t in range(2):
        ts = slice(t * T, (t + 1) * T)

        def chunk(j, nothing):
            js = pl.ds(pl.multiple_of(j * D, D), D)
            h = dot(n2[ts, :], up_v[:, js], 1, 0)
            g = dot(cot_v[ts, :], down_v[:, js], 1, 0)
            a, slope = gelu_both(h)
            a = a.astype(bf16)
            b = (g * slope).astype(bf16)
            act[ts, js] = a
            gh[ts, js] = b
            more_out = dot(a, down_v[:, js], 1, 1)
            more_g2 = dot(b, up_v[:, js], 1, 1)
            mid[ts, :] += more_out

            @pl.when(j == 0)
            def _():
                g2[...] = more_g2

            @pl.when(j > 0)
            def _():
                g2[...] += more_g2

            return nothing

        middle = mid[ts, :]
        unit, factor = normed(middle)
        lax.fori_loop(0, J, chunk, 0)
        middle_unit, middle_factor = unit, factor
        wide[...] = middle_unit
        if stores[0] is not None:
            for copy in stores:
                copy.wait()
        stage[0, 0:T, :] = mid[ts, :].astype(bf16)
        copy = pltpu.make_async_copy(stage.at[0, 0:T], output.at[ts], store_sem.at[0])
        copy.start()
        stores[0] = copy
        grad = g2[...]
        n = wide[...]
        gain_sum = gain_sum + jnp.sum(grad * n, axis=0, keepdims=True)
        shift_sum = shift_sum + jnp.sum(grad, axis=0, keepdims=True)
        gm = cot_v[ts, :].astype(f32) + norm_back(grad, gain, n, middle_factor)
        mid[ts, :] = gm
        low = gm.astype(bf16)
        n2[ts, :] = low
        stage[1, 0:T, :] = dot(low, out_full[...], 1, 1).astype(bf16)
        copy = pltpu.make_async_copy(stage.at[1, 0:T], ga_out.at[ts], store_sem.at[1])
        copy.start()
        stores[1] = copy
    for copy in stores:
        copy.wait()
    save = pltpu.make_async_copy(mid, gm_out, store_sem.at[2])
    save.start()
    vec_out[0:1, :] = gain_sum
    vec_out[1:2, :] = shift_sum
    pending = [[], []]
    turn = 0

    def put(value, pieces):
        nonlocal turn
        slot = turn % 2
        turn += 1
        for copy in pending[slot]:
            copy.wait()
        stage[slot, 0 : value.shape[0], :] = value
        pending[slot] = []
        for i, (rows, columns, dst) in enumerate(pieces):
            copy = pltpu.make_async_copy(
                stage.at[slot, rows, columns], dst, store_sem.at[3 + slot * 64 + i]
            )
            copy.start()
            pending[slot].append(copy)

    every = slice(0, D)
    for j in range(J):
        js = slice(j * D, (j + 1) * D)
        value = dot(n2T[...], gh[:, js], 1, 0).astype(bf16)
        if aligned:
            w = up_p.shape[2]
            pieces = [
                (every, slice(i * w, (i + 1) * w), up_p.at[j * D // w + i]) for i in range(D // w)
            ]
        else:
            pieces = [(every, every, up_p.at[:, js])]
        put(value, pieces)
        value = dot(cotT[...], act[:, js], 1, 0).astype(bf16)
        if aligned:
            r, w = down_p.shape[2:]
            pieces = [
                (
                    slice(d * r, (d + 1) * r),
                    slice(i * w, (i + 1) * w),
                    down_p.at[d, j * D // w + i],
                )
                for d in range(S)
                for i in range(D // w)
            ]
        else:
            pieces = [(every, every, down_p.at[:, js])]
        put(value, pieces)
    value = dot(att_v[...], n2[...], 0, 0).astype(bf16)
    for copy in pending[turn % 2]:
        copy.wait()
    pending[turn % 2] = []
    stage[turn % 2, 0:D, :] = value
    w = out_v.shape[2]
    for d in range(S):
        out_v[d] = stage[turn % 2, 0:D, d * w : (d + 1) * w]
    copy = pltpu.make_async_copy(out_v, out_p, store_sem.at[3])
    for group in pending:
        for other in group:
            other.wait()
    copy.start()
    copy.wait()
    save.wait()


def dense(place, att, tok, cot, out_g, up_g, down_g, vec):
    M, D = att.shape
    S, nb = place.blk, place.batch
    aligned = up_g.shape[-1] % 128 == 0 and down_g.shape[-1] % 128 == 0
    out_w = out_g.reshape(S, D, -1)
    FF = S * up_g.shape[-1]
    if aligned:
        up_w = up_g.reshape(S, D, -1)
        down_w = down_g.reshape((S, nb) + down_g.shape[-2:])
    else:
        up_w, down_w = joined(up_g, 0), joined(down_g, 1)
    anywhere = pl.BlockSpec(memory_space=pl.ANY)
    inside = pl.BlockSpec(memory_space=pltpu.VMEM)
    loads = 8 + S + S * nb
    results = pl.pallas_call(
        functools.partial(dense_kernel, place, aligned),
        out_shape=[
            jax.ShapeDtypeStruct((M, D), bf16),
            jax.ShapeDtypeStruct((M, D), f32),
            jax.ShapeDtypeStruct((M, D), bf16),
            jax.ShapeDtypeStruct(up_w.shape, bf16),
            jax.ShapeDtypeStruct(down_w.shape, bf16),
            jax.ShapeDtypeStruct(out_w.shape, bf16),
            jax.ShapeDtypeStruct((2, D), f32),
        ],
        in_specs=[anywhere] * 6 + [inside],
        out_specs=[anywhere] * 6 + [inside],
        scratch_shapes=[
            pltpu.VMEM((M, D), bf16),
            pltpu.VMEM((M, D), bf16),
            pltpu.VMEM((M, D), bf16),
            pltpu.VMEM(out_w.shape, bf16),
            pltpu.VMEM((D, FF), bf16),
            pltpu.VMEM((D, FF), bf16),
            pltpu.VMEM((D, D), bf16),
            pltpu.VMEM((M, D), f32),
            pltpu.VMEM((M, D), bf16),
            pltpu.VMEM((M, FF), bf16),
            pltpu.VMEM((M, FF), bf16),
            pltpu.VMEM((D, M), bf16),
            pltpu.VMEM((D, M), bf16),
            pltpu.VMEM((M // 2, D), f32),
            pltpu.VMEM((M // 2, D), f32),
            pltpu.VMEM((2, max(D, M // 2), D), bf16),
            pltpu.SemaphoreType.DMA((loads,)),
            pltpu.SemaphoreType.DMA((3 + 128,)),
        ],
        compiler_params=pltpu.CompilerParams(vmem_limit_bytes=62 << 20),
        name="dense",
    )(att, tok, cot, out_w, up_w, down_w, vec)
    output, gm, ga, up_p, down_p, out_p, vec_grads = results
    out_p = out_p.reshape(out_g.shape)
    if aligned:
        up_p, down_p = up_p.reshape(up_g.shape), down_p.reshape(down_g.shape)
    else:
        up_p, down_p = parted(up_p, place, 0), parted(down_p, place, 1)
    return output, gm, ga, up_p, down_p, out_p, vec_grads


def normed(values):
    average = jnp.mean(values, axis=-1, keepdims=True)
    centered = values - average
    variance = jnp.mean(centered * centered, axis=-1, keepdims=True)
    factor = lax.rsqrt(variance + epsilon)
    return centered * factor, factor


def norm_back(grad, gain, unit, factor):
    e = grad * gain
    return factor * (
        e - jnp.mean(e, axis=-1, keepdims=True) - unit * jnp.mean(e * unit, axis=-1, keepdims=True)
    )


def joined(gathered, axis):
    Y, C, Z, X, r, w = gathered.shape
    if axis == 0:
        return gathered.reshape(Y * C, Z * X * r, w).transpose(1, 0, 2).reshape(Z * X * r, -1)
    return gathered.reshape(Y * C, Z * X, r, w).transpose(0, 2, 1, 3).reshape(Y * C * r, -1)


def parted(whole, place, axis):
    Y, C, Z, X = place.Y, place.C, place.Z, place.X
    rows, columns = whole.shape
    if axis == 0:
        value = whole.reshape(Z * X, rows // (Z * X), Y * C, columns // (Y * C))
        value = value.transpose(2, 0, 1, 3)
    else:
        value = whole.reshape(Y * C, rows // (Y * C), Z * X, columns // (Z * X))
        value = value.transpose(0, 2, 1, 3)
    return value.reshape((Y, C, Z, X) + value.shape[2:])


def chosen(pair, c):
    return jnp.where(c == 0, pair[0], pair[1])


def body(
    place,
    tokens,
    proj_weight,
    out_weight,
    up_weight,
    down_weight,
    gain_one,
    bias_one,
    gain_two,
    bias_two,
    segments,
    present,
    cotangent,
):
    rows, block, width = tokens.shape
    Y, C = place.Y, place.C
    length = place.blk * block
    index = lax.axis_index("blk")
    c = index % C
    half = width // C
    query_pos = index * block + jnp.arange(block, dtype=jnp.int32)
    local_tags = jnp.where(present == 1, segments, -1 - query_pos[None, :])
    tag_in = jnp.broadcast_to(local_tags[:, None, :], (rows, 8, block))
    vec_in = jnp.stack([gain_one, bias_one, gain_two, bias_two])
    vec_in = jnp.pad(vec_in, ((0, 12), (0, 0)))
    proj_g, out_g, up_g, down_g, tok_g, cot_g, tag_g, vec_g = gather_all(
        place,
        [proj_weight, out_weight, up_weight, down_weight.T],
        tokens,
        cotangent,
        tag_in,
        vec_in,
    )
    proj_full = joined(proj_g, 0)
    vec = vec_g.reshape(place.blk, 16, -1)[:, :8].transpose(1, 0, 2).reshape(8, width).astype(f32)
    gain_a, bias_a = vec[0], vec[1]
    proj_own = lax.dynamic_index_in_dim(
        proj_full.reshape(width, 3, C, half), c, 2, keepdims=False
    ).reshape(width, 3 * half)
    row_tags = tag_g[:, :, 0].reshape(length)
    row_pos = jnp.arange(length, dtype=jnp.int32)
    begin = sum(
        jnp.where(row_tags > s, jnp.sum((row_tags == s).astype(jnp.int32)), 0) for s in range(4)
    )
    begin = jnp.where(row_tags < 0, row_pos, begin)[None]
    inputs = tok_g.reshape(length, width).astype(f32)
    unit, factor = normed(inputs)
    normed_low = (unit * gain_a + bias_a).astype(bf16)
    projected = dot(normed_low, proj_own, 1, 0).astype(bf16)
    attended, attended_t, log_total = attention_forward(projected, begin)
    by_core = attended.reshape(Y, C, block, half).transpose(1, 0, 2, 3)
    other = swap(place, by_core, 2).reshape(Y * block, half)
    mine = lax.dynamic_index_in_dim(by_core, c, 0, keepdims=False).reshape(Y * block, half)
    attended_low = jnp.concatenate(
        [chosen((mine, other), c), chosen((other, mine), c)], axis=1
    )
    inputs_mine = (
        lax.dynamic_index_in_dim(tok_g, c, 1, keepdims=False)
        .reshape(Y * block, width)
        .astype(f32)
    )
    output, grad_middle, grad_attended, up_p, down_p, out_p, vec_two = dense(
        place,
        attended_low,
        lax.dynamic_index_in_dim(tok_g, c, 1, keepdims=False).reshape(Y * block, width),
        cot_g.reshape(Y * block, width),
        out_g,
        up_g,
        down_g,
        vec,
    )
    inputs_mine = lax.dynamic_index_in_dim(tok_g, c, 1, keepdims=False)
    proj_sum, out_sum, up_sum, down_sum, vec_sum, output, token_grad = backward(
        place,
        [out_p, up_p, down_p],
        proj_weight.shape,
        begin,
        projected,
        grad_attended,
        attended_t,
        log_total,
        normed_low.T,
        proj_own,
        inputs_mine.reshape(Y * block, width),
        grad_middle,
        output,
        vec,
        vec_two,
    )
    share = width // place.blk
    vec_sum = jnp.concatenate([vec_sum[:4], vec_sum[4:]], axis=1)
    vec_sum = lax.dynamic_slice(vec_sum, (0, index * share), (4, share))
    return (
        output,
        token_grad,
        proj_sum,
        out_sum,
        up_sum,
        down_sum.T,
        vec_sum[0],
        vec_sum[1],
        vec_sum[2],
        vec_sum[3],
    )


def solution(mesh):
    place = Place((mesh.shape["batch"], mesh.shape["blk"]))
    weight, vector = P("batch", "blk"), P("blk")
    row = P("batch", "blk", None)
    in_specs = (row,) + (weight,) * 4 + (vector,) * 4 + (weight,) * 2 + (row,)
    out_specs = (row, row) + (weight,) * 4 + (vector,) * 4
    return jax.shard_map(
        functools.partial(body, place),
        mesh=mesh,
        in_specs=in_specs,
        out_specs=out_specs,
        check_vma=False,
    )
```

time: 659 us -> 437 us (0.66)
  local copies, waits for them, and re-layouts: 162 us -> 33.5 us
  matrix products: 92 us -> 5.91 us
    dot_general x12 -> x1, matrix products: 92 us -> 5.91 us  [dot(): lax.dot_general(left, right, (((left_dim,), (right_dim,)), ((), ())), pre...]
    dynamic_update_slice x1 -> x0, local copies, waits for them, and re-layouts: 56.4 us -> none  [body(): lax.dynamic_update_slice(spread, proj_grad_own.reshape(width, 3, 1, half)...]
    reshape x12 -> x1, local copies, waits for them, and re-layouts: 41.1 us -> 3.91 us  [body(): proj_own = lax.dynamic_index_in_dim(proj_full.reshape(width, 3, C, half),...]
    another operation x9 -> x1, local copies, waits for them, and re-layouts: 14.7 us -> 0.08 us  [the longest x1 11.6 us: parted(): value = whole.reshape(Z * X, rows // (Z * X), Y * C, columns // (Y * C))]
    pallas_call x2, Pallas kernels: 193 us -> 205 us  [the longest x1 134 us: backward(): pl.pallas_call(functools.partial(backward_kernel, place, n, BQ), out_shap...]
    reshape x3 -> x1, local copies, waits for them, and re-layouts: 14.7 us -> 6.16 us  [joined(): gathered.reshape(Y * C, Z * X * r, w).transpose(1, 0, 2)]
    unnamed x78 -> x27, local copies, waits for them, and re-layouts: 13.2 us -> 6.87 us
where the time goes in v2:
time: 437 us; the launch traced here: 431 us
  Pallas kernels  372 us (85%)
  local copies, waits for them, and re-layouts  33.5 us (8%)
  other arithmetic  18.9 us (4%)
  matrix products  5.91 us (1%)
    pallas_call x1, Pallas kernels, gather_all(): pl.pallas_call(functools.partial(gather_kernel, place, tuple((m.shape for...  136 us
    pallas_call x1, Pallas kernels, backward(): pl.pallas_call(functools.partial(backward_kernel, place, n, BQ), out_shap...  134 us
    pallas_call x1, Pallas kernels, dense(): pl.pallas_call(functools.partial(dense_kernel, place, aligned), out_shape...  70.4 us
    pallas_call x1, Pallas kernels, attention_forward(): pl.pallas_call(functools.partial(attention_forward_kernel, 512), grid=(pa...  28.2 us

profile of v2, /device:TPU:0, one launch (start us, length us, event | category | flops | bytes accessed | tf_op | source)
XLA Modules:
  0.0 431.5 jit_solution(5502360857012245439)
XLA Ops:
  0.7 0.7 stack.15
  1.3 0.7 stack.16
  2.0 0.7 stack.17
  2.6 0.7 stack.18
  3.3 0.7 compare_select_fusion.4
  4.0 0.6 fusion.7.refs_7_
  4.6 0.6 broadcast_in_dim.37.refs_6_
  5.2 136.2 %gather_all.1 = (bf16[2,2,4,2,96,576]{5,4,3,2,1,0:T(8,128)(2,1)}, bf16[2,2,4,2,96,192]{5,4,3,2,1,0:T(8,128)(2,1)}, bf16[2,2,4,2,96,768]{5,4,3,2,1,0:T(8,128)(2,1...) custom-call(bf16[96,576]{1,0:T(8,128)(2,1)} %refs_0_.1, ...), custom_call_target="tpu_custom_call" | custom-call | tf_op jit(solution)/shard_map/gather_all/pallas_call | solution.py:187
  141.5 0.7 slice_convert_fusion
  142.2 6.2 %copy.25 = bf16[4,768,576]{1,2,0:T(8,128)(2,1)} copy(bf16[4,768,576]{2,1,0:T(8,128)(2,1)} %bitcast.61) | data formatting | bytes 7077888 | tf_op jit(solution)/shard_map/reshape | solution.py:1192
  148.4 3.0 constant_dynamic-slice_fusion.2
  151.4 1.5 fusion.10
  152.9 3.5 fusion.11
  156.4 0.9 broadcast_compare_fusion
  157.3 0.0 copy-done.2
  157.3 0.0 copy-start
  157.3 0.5 convert_reduce_fusion
  157.8 1.1 multiply_reduce_fusion
  158.9 0.7 convert_element_type.57.vec.refs_10_
  159.6 0.1 mul.42
  159.7 0.1 add.98
  159.8 1.2 constant_dynamic-slice_fusion
  161.0 3.9 copy.28.refs_6_
  164.9 1.3 add_convert_fusion.1
  166.2 0.2 copy-done.3
  166.4 5.9 %convolution_convert_fusion.q_ref.k_ref.v_ref.refs_1_ = bf16[2048,1152]{1,0:T(8,128)(2,1)} fusion(bf16[2048,768]{1,0:T(8,128)(2,1)S(1)} %bitcast.62, bf16[768,1152]{0,1:T(8,128)(2,1)S(1)} %bitcast.55), kind=kOutput, calls=%fused_computation | convolution fusion | flops 3626237952 | bytes 9633792 | tf_op jit(solution)/shard_map/dot_general | solution.py:23
  172.3 28.2 %attention_forward.1 = (bf16[2048,384]{1,0:T(8,128)(2,1)S(1)}, f32[384,2048]{1,0:T(8,128)}, f32[3,2,2048]{2,1,0:T(2,128)S(1)}) custom-call(s32[1,2048]{1,0:T(1,128)S(1)} %iota_select_fusion.start_ref.refs_0_, bf16[2048,1152]{1,0:T(8,128)(2,1)} %convolution_convert_fusion.q_ref.k_ref.v_ref.refs_1_, ...), custom_call_target="tpu_custom_call" | custom-call | tf_op jit(solution)/shard_map/attention_forward/pallas_call | solution.py:284
  200.5 0.1 constant_dynamic-slice_fusion.1
  200.6 1.3 copy.36
  201.9 2.7 swap_2.1
  204.6 1.3 bitcast_select_fusion.1
  205.9 1.3 pad_maximum_fusion.att
  207.2 70.4 %dense.1 = (bf16[1024,768]{1,0:T(8,128)(2,1)}, f32[1024,768]{1,0:T(8,128)}, bf16[1024,768]{1,0:T(8,128)(2,1)}, bf16[4,768,768]{2,1,0:T(8,128)(2,1)}, bf16[4,8,19...) custom-call(bf16[1024,768]{1,0:T(8,128)(2,1)} %pad_maximum_fusion.att, ...), custom_call_target="tpu_custom_call" | custom-call | tf_op jit(solution)/shard_map/dense/pallas_call | solution.py:1129
  277.6 5.4 %copy.29 = f32[2048,768]{0,1:T(8,128)} copy(bf16[2048,768]{1,0:T(8,128)(2,1)} %bitcast.50) | data formatting | bytes 9437184 | tf_op jit(solution)/shard_map/convert_element_type | solution.py:1258
  283.0 5.5 %fusion.refs_5_ = bf16[768,2048]{1,0:T(8,128)(2,1)} fusion(f32[2048,768]{0,1:T(8,128)} %copy.29, f32[768]{0:T(1024)S(1)} %add.98, f32[768]{0:T(1024)S(1)} %mul.42, f32[2048]{0:T(1024)S(1)} %bitcast.73, f32[2048]{0:T(1024)S(1)} %bitcast.72), kind=kLoop, calls=%fused_computation.5 | loop fusion | flops 7864320 | bytes 9459712 | tf_op jit(solution)/shard_map/transpose | solution.py:1294
  288.5 134.5 %backward.1 = (f32[96,576]{1,0:T(8,128)}, f32[96,192]{1,0:T(8,128)}, f32[96,768]{1,0:T(8,128)}, f32[192,384]{1,0:T(8,128)}, f32[8,384]{1,0:T(8,128)}, /*index=5*...) custom-call(s32[1,2048]{1,0:T(1,128)} %copy-done, bf16[2048,1152]{1,0:T(8,128)(2,1)} %convolution_convert_fusion.q_ref.k_ref.v_ref.refs_1_, ...), custom_call_target="tpu_custom_call" | custom-call | tf_op jit(solution)/shard_map/backward/pallas_call | solution.py:921
  422.9 0.0 copy-start.4
  422.9 0.8 fusion.19
  423.8 0.1 fusion.15
  423.9 0.6 fusion.20
  424.4 0.0 copy-start.5
  424.5 2.7 copy.44
  427.2 0.0 copy-done.4
  427.2 1.1 copy.45
  428.3 0.7 copy.46
  429.0 0.6 copy.47
  429.7 0.7 copy.48
  430.4 0.7 copy.49
  (20 shorter events, 0.1 us)
Async XLA Ops:
  148.4 8.9 %copy-start.2 = (bf16[2,2,512,768]{3,2,1,0:T(8,128)(2,1)S(1)}, bf16[2,2,512,768]{3,2,1,0:T(8,128)(2,1)}, u32[]{:S(2)}) copy-start(bf16[2,2,512,768]{3,2,1,0:T(8,128)(2,1)} %get-tuple-element.36) | copy-start | bytes 9437188
  157.3 15.0 %copy-start = (s32[1,2048]{1,0:T(1,128)}, s32[1,2048]{1,0:T(1,128)S(1)}, u32[]{:S(2)}) copy-start(s32[1,2048]{1,0:T(1,128)S(1)} %iota_select_fusion.start_ref.refs_0_) | copy-start | bytes 24580
  164.9 1.5 copy-start.3
  200.5 1.4 copy-start.1
  422.9 4.3 copy-start.4
  424.4 3.9 copy-start.7
  424.4 4.6 %copy-start.8 = (f32[96,192]{1,0:T(8,128)S(1)}, f32[96,192]{1,0:T(8,128)}, u32[]{:S(2)}) copy-start(f32[96,192]{1,0:T(8,128)} %get-tuple-element.91) | copy-start | bytes 221188
  424.4 5.2 %copy-start.6 = (f32[96,768]{1,0:T(8,128)S(1)}, f32[96,768]{1,0:T(8,128)}, u32[]{:S(2)}) copy-start(f32[96,768]{1,0:T(8,128)} %get-tuple-element.92) | copy-start | bytes 884740
  424.4 5.9 %copy-start.5 = (f32[192,384]{1,0:T(8,128)S(1)}, f32[192,384]{1,0:T(8,128)}, u32[]{:S(2)}) copy-start(f32[192,384]{1,0:T(8,128)} %get-tuple-element.58) | copy-start | bytes 884740

commit v3 on v2

--- a/solution.py
+++ b/solution.py
@@ -39,273 +39,6 @@
         return (z * self.X + x, p * self.C + c)
 
 
-def split_rows(count):
-    return 16 * ((count // 2) // 16)
-
-
-class Sends:
-    def __init__(self, send_sem, recv_sem):
-        self.send_sem, self.recv_sem, self.count = send_sem, recv_sem, 0
-
-    def start(self, src, dst, device):
-        copy = pltpu.make_async_remote_copy(
-            src_ref=src,
-            dst_ref=dst,
-            send_sem=self.send_sem.at[self.count],
-            recv_sem=self.recv_sem.at[self.count],
-            device_id=device,
-            device_id_type=MESH,
-        )
-        self.count += 1
-        copy.start()
-        return copy
-
-
-def greet(place, partners):
-    barrier = pltpu.get_barrier_semaphore()
-    for partner in partners:
-        pl.semaphore_signal(barrier, inc=1, device_id=partner, device_id_type=MESH)
-    pl.semaphore_wait(barrier, len(partners))
-
-
-def partners_of(place):
-    z, x, p, c = place.here()
-    found = [place.device((z + k) % place.Z, x, p, c) for k in range(1, place.Z)]
-    found += [place.device(z, 1 - x, p, c)]
-    found += [place.device(z, x, (p + k) % place.Y, c) for k in range(1, place.Y)]
-    found += [place.device(z, x, p, 1 - c)]
-    return found
-
-
-def gather_kernel(place, matrices, *refs):
-    n = len(matrices)
-    mats, (tok, cot, tag, vec) = refs[:n], refs[n : n + 4]
-    outs, (tok_g, cot_g, tag_g, vec_g) = refs[n + 4 : 2 * n + 4], refs[2 * n + 4 : 2 * n + 8]
-    send_sem, recv_sem, local_sem = refs[2 * n + 8 :]
-    z, x, p, c = place.here()
-    Z, X, Y = place.Z, place.X, place.Y
-    greet(place, partners_of(place))
-    sends = Sends(send_sem, recv_sem)
-    started = []
-
-    def go(src, dst, device):
-        copy = sends.start(src, dst, device)
-        started.append(copy)
-        return copy
-
-    local = []
-
-    def keep(src, dst):
-        copy = pltpu.make_async_copy(src, dst, local_sem.at[len(local)])
-        copy.start()
-        local.append(copy)
-        return copy
-
-    row_copies, cot_copies = [], []
-    for k in range(1, Y):
-        to = (p + k) % Y
-        device = place.device(z, x, to, c)
-        row_copies.append(go(tok.at[to], tok_g.at[p, c], device))
-        row_copies.append(go(tag.at[to], tag_g.at[p, c], device))
-        row_copies.append(go(vec, vec_g.at[p, c], device))
-    own = [
-        keep(tok.at[p], tok_g.at[p, c]),
-        keep(tag.at[p], tag_g.at[p, c]),
-        keep(vec, vec_g.at[p, c]),
-        keep(cot.at[p], cot_g.at[p]),
-    ]
-    first = []
-    for m in range(n):
-        place_here = outs[m].at[p, c, z, x]
-        keep(mats[m], place_here)
-        first.append(
-            [
-                go(mats[m], place_here, place.device((z + k) % Z, x, p, c))
-                for k in range(1, Z)
-            ]
-        )
-    for k in range(1, Y):
-        to = (p + k) % Y
-        cot_copies.append(go(cot.at[to], cot_g.at[p], place.device(z, x, to, c)))
-    for copy in local:
-        copy.wait()
-    second = []
-    for m in range(n):
-        for copy in first[m]:
-            copy.wait_recv()
-        h = split_rows(mats[m].shape[0])
-        r = mats[m].shape[0]
-        low = outs[m].at[p, c, :, x, 0:h]
-        high = outs[m].at[p, c, :, x, h:r]
-        second.append(
-            (
-                [go(low, low, place.device(z, 1 - x, p, c))],
-                [go(high, high, place.device(z, x, (p + k) % Y, c)) for k in range(1, Y)],
-            )
-        )
-    third = []
-    for m in range(n):
-        h = split_rows(mats[m].shape[0])
-        r = mats[m].shape[0]
-        for copy in second[m][0]:
-            copy.wait_recv()
-        low = outs[m].at[p, c, :, :, 0:h]
-        a = [go(low, low, place.device(z, x, (p + k) % Y, c)) for k in range(1, Y)]
-        for copy in second[m][1]:
-            copy.wait_recv()
-        high = outs[m].at[:, c, :, x, h:r]
-        b = [go(high, high, place.device(z, 1 - x, p, c))]
-        third.append(a + b)
-    for copy in row_copies:
-        copy.wait_recv()
-    sibling = place.device(z, x, p, 1 - c)
-    last = []
-    for ref in (tok_g, tag_g, vec_g):
-        last.append(go(ref.at[:, c], ref.at[:, c], sibling))
-    for m in range(n):
-        for copy in third[m]:
-            copy.wait_recv()
-        last.append(go(outs[m].at[:, c], outs[m].at[:, c], sibling))
-    for copy in last + cot_copies:
-        copy.wait_recv()
-    for copy in started:
-        copy.wait_send()
-
-
-def gather_all(place, mats, tok, cot, tag, vec):
-    n = len(mats)
-    Z, X, Y, C = place.Z, place.X, place.Y, place.C
-    out = [jax.ShapeDtypeStruct((Y, C, Z, X) + m.shape, m.dtype) for m in mats]
-    out += [
-        jax.ShapeDtypeStruct((Y, C) + tok.shape[1:], tok.dtype),
-        jax.ShapeDtypeStruct((Y,) + cot.shape[1:], cot.dtype),
-        jax.ShapeDtypeStruct((Y, C) + tag.shape[1:], tag.dtype),
-        jax.ShapeDtypeStruct((Y, C) + vec.shape, vec.dtype),
-    ]
-    copies = 4 * (Y - 1) + n * ((Z - 1) + 1 + (Y - 1) + (Y - 1) + 1) + 3 + n
-    anywhere = pl.BlockSpec(memory_space=pl.ANY)
-    return pl.pallas_call(
-        functools.partial(gather_kernel, place, tuple(m.shape for m in mats)),
-        out_shape=out,
-        in_specs=[anywhere] * (n + 4),
-        out_specs=[anywhere] * (n + 4),
-        scratch_shapes=[
-            pltpu.SemaphoreType.DMA((copies,)),
-            pltpu.SemaphoreType.DMA((copies,)),
-            pltpu.SemaphoreType.DMA((n + 4,)),
-        ],
-        compiler_params=pltpu.CompilerParams(collective_id=0, has_side_effects=True),
-        name="gather_all",
-    )(*mats, tok, cot, tag, vec)
-
-
-def swap_kernel(place, src, dst, send_sem, recv_sem):
-    z, x, p, c = place.here()
-    sibling = place.device(z, x, p, 1 - c)
-    greet(place, [sibling])
-    copy = pltpu.make_async_remote_copy(
-        src_ref=src.at[1 - c],
-        dst_ref=dst,
-        send_sem=send_sem,
-        recv_sem=recv_sem,
-        device_id=sibling,
-        device_id_type=MESH,
-    )
-    copy.start()
-    copy.wait()
-
-
-def swap(place, value, number):
-    anywhere = pl.BlockSpec(memory_space=pl.ANY)
-    return pl.pallas_call(
-        functools.partial(swap_kernel, place),
-        out_shape=jax.ShapeDtypeStruct(value.shape[1:], value.dtype),
-        in_specs=[anywhere],
-        out_specs=anywhere,
-        scratch_shapes=[pltpu.SemaphoreType.DMA, pltpu.SemaphoreType.DMA],
-        compiler_params=pltpu.CompilerParams(collective_id=number, has_side_effects=True),
-        name=f"swap_{number}",
-    )(value)
-
-
-def head_masked(value, h, axis):
-    index = lax.broadcasted_iota(jnp.int32, value.shape, axis)
-    return jnp.where((index // HEAD_DIM) == h, value, jnp.zeros_like(value))
-
-
-def attention_forward_kernel(BQ, start_ref, q_ref, k_ref, v_ref, o_ref, oT_ref, lt_ref, qT, vT):
-    L = q_ref.shape[0]
-    nq = L // BQ
-    scale = HEAD_DIM ** (-0.5) * LOG2E
-    qT[...] = q_ref[...].T
-    vT[...] = v_ref[...].T
-    for qi in range(nq):
-        qs = slice(qi * BQ, (qi + 1) * BQ)
-        begin = start_ref[:, qs]
-        d0 = qi * BQ
-        if qi == nq - 1:
-            cuts = [(0, d0, 1)] if d0 else []
-        elif d0 > 256:
-            cuts = [(0, 256, 1), (256, d0, 0)]
-        else:
-            cuts = [(0, d0, 1)] if d0 else []
-        cuts.append((d0, d0 + BQ, 2))
-        for h in range(2):
-            query = head_masked(qT[:, qs], h, 0)
-            parts = []
-            for a, b, mode in cuts:
-                s = dot(k_ref[a:b, :], query, 1, 0) * scale
-                if mode:
-                    key_pos = lax.broadcasted_iota(jnp.int32, (b - a, BQ), 0) + a
-                    visible = key_pos >= begin
-                    if mode == 2:
-                        query_pos = lax.broadcasted_iota(jnp.int32, (b - a, BQ), 1) + d0
-                        visible = jnp.logical_and(visible, key_pos <= query_pos)
-                    s = jnp.where(visible, s, masked)
-                parts.append(s)
-            top = functools.reduce(
-                jnp.maximum, [jnp.max(s, axis=0, keepdims=True) for s in parts]
-            )
-            total, accum = 0.0, 0.0
-            for (a, b, mode), s in zip(cuts, parts):
-                e = jnp.exp2(s - top)
-                total = total + jnp.sum(e, axis=0, keepdims=True)
-                accum = accum + dot(
-                    vT[h * HEAD_DIM : (h + 1) * HEAD_DIM, a:b], e.astype(bf16), 1, 0
-                )
-            oT_ref[h * HEAD_DIM : (h + 1) * HEAD_DIM, qs] = accum / total
-            lt_ref[0, h : h + 1, qs] = top + jnp.log2(total)
-        o_ref[qs, :] = oT_ref[:, qs].astype(bf16).T
-
-
-def attention_forward(projected, begin):
-    L = projected.shape[0]
-    pairs = projected.shape[1] // 3 // 128
-    return pl.pallas_call(
-        functools.partial(attention_forward_kernel, 512),
-        grid=(pairs,),
-        in_specs=[
-            pl.BlockSpec((1, L), lambda i: (0, 0)),
-            pl.BlockSpec((L, 128), lambda i: (0, i)),
-            pl.BlockSpec((L, 128), lambda i: (0, pairs + i)),
-            pl.BlockSpec((L, 128), lambda i: (0, 2 * pairs + i)),
-        ],
-        out_specs=[
-            pl.BlockSpec((L, 128), lambda i: (0, i)),
-            pl.BlockSpec((128, L), lambda i: (i, 0)),
-            pl.BlockSpec((1, 2, L), lambda i: (i, 0, 0)),
-        ],
-        out_shape=[
-            jax.ShapeDtypeStruct((L, pairs * 128), bf16),
-            jax.ShapeDtypeStruct((pairs * 128, L), f32),
-            jax.ShapeDtypeStruct((pairs, 2, L), f32),
-        ],
-        scratch_shapes=[pltpu.VMEM((128, L), bf16), pltpu.VMEM((128, L), bf16)],
-        compiler_params=pltpu.CompilerParams(vmem_limit_bytes=50 << 20),
-        name="attention_forward",
-    )(begin, projected, projected, projected)
-
-
 class Wire:
     def __init__(self, send_sem, recv_sem):
         self.send_sem, self.recv_sem, self.names = send_sem, recv_sem, {}
@@ -339,6 +72,439 @@
 
 def first_rows(rows, sixths):
     return min(rows - 16, 16 * ((rows * sixths // 6) // 16)) if rows > 16 else 0
+
+
+def greet(place, partners):
+    barrier = pltpu.get_barrier_semaphore()
+    for partner in partners:
+        pl.semaphore_signal(barrier, inc=1, device_id=partner, device_id_type=MESH)
+    pl.semaphore_wait(barrier, len(partners))
+
+
+def partners_of(place):
+    z, x, p, c = place.here()
+    found = [place.device((z + k) % place.Z, x, p, c) for k in range(1, place.Z)]
+    found += [place.device(z, 1 - x, p, c)]
+    found += [place.device(z, x, (p + k) % place.Y, c) for k in range(1, place.Y)]
+    found += [place.device(z, x, p, 1 - c)]
+    return found
+
+
+def head_masked(value, h, axis):
+    index = lax.broadcasted_iota(jnp.int32, value.shape, axis)
+    return jnp.where((index // HEAD_DIM) == h, value, jnp.zeros_like(value))
+
+
+class Spreading:
+    def __init__(self, place, wire, name, spots, shard, whole, sixths):
+        self.place, self.wire, self.name, self.spots = place, wire, name, spots
+        self.shard, self.whole = shard, whole
+        self.rows = shard.shape[0]
+        self.h = first_rows(self.rows, sixths)
+
+    def zero(self):
+        z, x, p, c = self.spots
+        place = self.place
+        found = []
+        for k in range(1, place.Z):
+            found.append(
+                self.wire.copy(
+                    (self.name, "z", k),
+                    self.shard,
+                    self.whole.at[p, c, z, x],
+                    place.device((z + k) % place.Z, x, p, c),
+                )
+            )
+        return found
+
+    def one(self):
+        z, x, p, c = self.spots
+        place, h, r = self.place, self.h, self.rows
+        low = self.whole.at[p, c, :, x, 0:h]
+        found = [self.wire.copy((self.name, "xa"), low, low, place.device(z, 1 - x, p, c))]
+        high = self.whole.at[p, c, :, x, h:r]
+        for k in range(1, place.Y):
+            found.append(
+                self.wire.copy(
+                    (self.name, "yb", k), high, high, place.device(z, x, (p + k) % place.Y, c)
+                )
+            )
+        return found
+
+    def two(self):
+        z, x, p, c = self.spots
+        place, h, r = self.place, self.h, self.rows
+        low = self.whole.at[p, c, :, :, 0:h]
+        found = [
+            self.wire.copy(
+                (self.name, "ya", k), low, low, place.device(z, x, (p + k) % place.Y, c)
+            )
+            for k in range(1, place.Y)
+        ]
+        high = self.whole.at[:, c, :, x, h:r]
+        found.append(
+            self.wire.copy((self.name, "xb"), high, high, place.device(z, 1 - x, p, c))
+        )
+        return found
+
+    def three(self):
+        z, x, p, c = self.spots
+        plane = self.whole.at[:, c]
+        return [self.wire.copy((self.name, "core"), plane, plane, self.place.device(z, x, p, 1 - c))]
+
+    def go_one(self):
+        arrive_all(self.zero())
+        start_all(self.one())
+
+    def go_two(self):
+        arrive_all(self.one())
+        start_all(self.two())
+
+    def go_three(self):
+        arrive_all(self.two())
+        start_all(self.three())
+
+    def leave(self):
+        for copies in (self.zero(), self.one(), self.two(), self.three()):
+            leave_all(copies)
+
+
+def forward_kernel(place, n, BQ, *refs):
+    shards, (tok, cot, tag, vec_in) = refs[: n + 1], refs[n + 1 : n + 5]
+    outs = refs[n + 5 :]
+    wholes = outs[:n]
+    (tok_out, cot_out, vec_out, begin, proj_out, w_out, normedT_out, att_out, oT_out, lt) = outs[
+        n : n + 10
+    ]
+    (
+        proj_v, tok_v, tag_v, vec_v, n_v, nT, wv, pv, vT, att, oT,
+        send_sem, recv_sem, local_sem,
+    ) = outs[n + 10 :]
+    spots = place.here()
+    z, x, p, c = spots
+    Z, X, Y, C = place.Z, place.X, place.Y, place.C
+    D, W3 = wv.shape
+    H = W3 // 3
+    L = pv.shape[0]
+    T = L // (Y * C)
+    U = BQ // T
+    pairs = H // 128
+    nq = L // BQ
+    wire = Wire(send_sem, recv_sem)
+    sibling = place.device(z, x, p, 1 - c)
+    flows = [
+        Spreading(place, wire, m, spots, shards[m], proj_v if m == 0 else wholes[m - 1], 3)
+        for m in range(n + 1)
+    ]
+
+    def local(i, src, dst):
+        return pltpu.make_async_copy(src, dst, local_sem.at[i])
+
+    def lane(offset, size):
+        return pl.ds(pl.multiple_of(offset, 128), size)
+
+    def line(offset, size):
+        return pl.ds(pl.multiple_of(offset, 16), size)
+
+    row_parts = (("vec", vec_in, vec_v), ("tag", tag, tag_v), ("tok", tok, tok_v))
+
+    def along_y(what, src, dst):
+        found = []
+        for k in range(1, Y):
+            to = (p + k) % Y
+            piece = src if what == "vec" else src.at[to]
+            found.append(
+                wire.copy((what, "y", k), piece, dst.at[p, c], place.device(z, x, to, c))
+            )
+        return found
+
+    def to_sibling_own(what, src, dst):
+        piece = src if what == "vec" else src.at[p]
+        return wire.copy((what, "own"), piece, dst.at[p, c], sibling)
+
+    def to_sibling(what, dst):
+        found = []
+        for k in range(1, Y):
+            q = (p + k) % Y
+            found.append(wire.copy((what, "pass", k), dst.at[q, c], dst.at[q, c], sibling))
+        return found
+
+    def cot_sends():
+        return [
+            wire.copy(
+                ("cot", k), cot.at[(p + k) % Y], cot_out.at[p], place.device(z, x, (p + k) % Y, c)
+            )
+            for k in range(1, Y)
+        ]
+
+    greet(place, partners_of(place))
+    for part in row_parts:
+        start_all(along_y(*part))
+    for part in row_parts:
+        to_sibling_own(*part).start()
+    for flow in flows:
+        start_all(flow.zero())
+    kept = [local(m, shards[m], flows[m].whole.at[p, c, z, x]) for m in range(n + 1)]
+    kept += [
+        local(n + 1, vec_in, vec_v.at[p, c]),
+        local(n + 2, tag.at[p], tag_v.at[p, c]),
+        local(n + 3, tok.at[p], tok_v.at[p, c]),
+        local(n + 4, cot.at[p], cot_out.at[p]),
+    ]
+    start_all(kept)
+    arrive_all(along_y(*row_parts[0]))
+    start_all(to_sibling("vec", vec_v))
+    for copy in kept[:-1]:
+        copy.wait()
+    flows[0].go_one()
+    to_sibling_own(*row_parts[0]).wait_recv()
+    arrive_all(to_sibling("vec", vec_v))
+    share = vec_v.shape[3]
+    for q in range(Y):
+        for i in range(C):
+            lo = (q * C + i) * share
+            vec_out[:, lo : lo + share] = vec_v[q, i, 0:8, :].astype(f32)
+    gain, shift = vec_out[0:1, :], vec_out[1:2, :]
+
+    def norm_block(q, i):
+        unit, factor = normed(tok_v[q, i].astype(f32))
+        low = (unit * gain + shift).astype(bf16)
+        rows = line((q * C + i) * T, T)
+        n_v[rows, :] = low
+        nT[:, lane((q * C + i) * T, T)] = low.T
+
+    norm_block(p, c)
+    to_sibling_own(*row_parts[2]).wait_recv()
+    norm_block(p, 1 - c)
+    arrive_all(flows[0].one()[:1])
+    start_all(flows[0].two()[:-1])
+    for what, src, dst in row_parts[1:]:
+        arrive_all(along_y(what, src, dst))
+        start_all(to_sibling(what, dst))
+    for k in range(1, Y):
+        norm_block((p + k) % Y, c)
+    arrive_all(to_sibling("tok", tok_v))
+    for k in range(1, Y):
+        norm_block((p + k) % Y, 1 - c)
+    arrive_all(flows[0].one()[1:])
+    start_all(flows[0].two()[-1:])
+    flows[1].go_one()
+    flows[2].go_one()
+    saves = [
+        local(n + 5, nT, normedT_out),
+        local(n + 6, tok_v.at[:, c], tok_out),
+    ]
+    start_all(saves)
+    to_sibling_own(*row_parts[1]).wait_recv()
+    arrive_all(to_sibling("tag", tag_v))
+    tags = [tag_v[q, i, 0:1, :] for q in range(Y) for i in range(C)]
+    counts = []
+    for s in range(4):
+        hits = sum((t == s).astype(f32) for t in tags)
+        counts.append(jnp.sum(hits, axis=1, keepdims=True).astype(jnp.int32))
+    for b, t in enumerate(tags):
+        first = sum(jnp.where(t > s, counts[s], 0) for s in range(4))
+        position = lax.broadcasted_iota(jnp.int32, (1, T), 1) + b * T
+        begin[:, b * T : (b + 1) * T] = jnp.where(t < 0, position, first)
+    flows[0].go_three()
+    arrive_all(flows[0].three())
+    r, w = proj_v.shape[4:]
+    for mine in range(C):
+
+        @pl.when(c == mine)
+        def _():
+            for third in range(3):
+                base = third * D + mine * H
+                for d in range(Y * C):
+                    a, b = max(base, d * w), min(base + H, (d + 1) * w)
+                    if a >= b:
+                        continue
+                    to = third * H + a - base
+                    for i in range(Z * X):
+                        wv[i * r : (i + 1) * r, to : to + b - a] = proj_v[
+                            d // C, d % C, i // X, i % X, :, a - d * w : b - d * w
+                        ]
+
+    def project(i, nothing):
+        rows = line(i * BQ, BQ)
+        pv[rows, :] = dot(n_v[rows, :], wv[...], 1, 0).astype(bf16)
+        return nothing
+
+    lax.fori_loop(0, nq, project, 0)
+    vT[...] = pv[:, 2 * H :].T
+    saves += [local(n + 7, pv, proj_out), local(n + 8, wv, w_out)]
+    start_all(saves[2:])
+    flows[1].go_two()
+    flows[2].go_two()
+    scale = HEAD_DIM ** (-0.5) * LOG2E
+
+    def block_copies(qi):
+        found = []
+        for u in range(U):
+            b = qi * U + u
+            q, owner = b // C, b % C
+            src = att.at[b * T : (b + 1) * T, :]
+            dst = att_out.at[q * T : (q + 1) * T, lane(c * H, H)]
+            found.append(
+                (owner, local(n + 9 + q, src, dst), wire.copy(("att", q), src, dst, sibling))
+            )
+        return found
+
+    def event(pair, number, *events):
+        @pl.when(pair == number)
+        def _():
+            for e in events:
+                e()
+
+    for qi in range(nq):
+        qs = slice(qi * BQ, (qi + 1) * BQ)
+        d0 = qi * BQ
+        if qi == nq - 1:
+            cuts = [(0, d0, 1)] if d0 else []
+        elif d0 > 256:
+            cuts = [(0, 256, 1), (256, d0, 0)]
+        else:
+            cuts = [(0, d0, 1)] if d0 else []
+        cuts.append((d0, d0 + BQ, 2))
+
+        def one_pair(pair, nothing):
+            cols = lane(pair * 128, 128)
+            k_cols = lane(H + pair * 128, 128)
+            qT = pv[qs, cols].T
+            found = []
+            for h in range(2):
+                query = head_masked(qT, h, 0)
+                rows = pl.ds(pl.multiple_of(pair * 128 + h * HEAD_DIM, HEAD_DIM), HEAD_DIM)
+                parts = []
+                for a, b, mode in cuts:
+                    s = dot(pv[a:b, k_cols], query, 1, 0) * scale
+                    if mode:
+                        key_pos = lax.broadcasted_iota(jnp.int32, (b - a, BQ), 0) + a
+                        visible = key_pos >= begin[:, qs]
+                        if mode == 2:
+                            query_pos = lax.broadcasted_iota(jnp.int32, (b - a, BQ), 1) + d0
+                            visible = jnp.logical_and(visible, key_pos <= query_pos)
+                        s = jnp.where(visible, s, masked)
+                    parts.append(s)
+                top = functools.reduce(
+                    jnp.maximum, [jnp.max(s, axis=0, keepdims=True) for s in parts]
+                )
+                total, accum = 0.0, 0.0
+                for (a, b, mode), s in zip(cuts, parts):
+                    e = jnp.exp2(s - top)
+                    total = total + jnp.sum(e, axis=0, keepdims=True)
+                    accum = accum + dot(vT[rows, a:b], e.astype(bf16), 1, 0)
+                result = accum / total
+                oT[rows, qs] = result
+                found.append(result)
+                lt[pair, h : h + 1, qs] = top + jnp.log2(total)
+            att[qs, cols] = jnp.concatenate(found, axis=0).astype(bf16).T
+            if qi == nq - 1:
+                event(pair, 0, flows[3].go_two)
+            return nothing
+
+        lax.fori_loop(0, pairs, one_pair, 0)
+        for owner, keep, send in block_copies(qi):
+
+            @pl.when(owner == c)
+            def _():
+                keep.start()
+
+            @pl.when(owner != c)
+            def _():
+                send.start()
+
+        if qi == 0:
+            flows[3].go_one()
+            start_all(cot_sends())
+        if qi == nq - 2:
+            flows[1].go_three()
+            flows[2].go_three()
+    last = local(n + 9 + Y, oT, oT_out)
+    last.start()
+    flows[3].go_three()
+    for flow in flows[1:]:
+        arrive_all(flow.three())
+    for qi in range(nq):
+        for owner, keep, send in block_copies(qi):
+
+            @pl.when(owner == c)
+            def _():
+                keep.wait()
+
+            @pl.when(owner != c)
+            def _():
+                send.wait_send()
+
+            @pl.when(owner == c)
+            def _():
+                send.wait_recv()
+
+    arrive_all(cot_sends())
+    leave_all(cot_sends())
+    for what, src, dst in row_parts:
+        leave_all(along_y(what, src, dst))
+        to_sibling_own(what, src, dst).wait_send()
+        leave_all(to_sibling(what, dst))
+    for flow in flows:
+        flow.leave()
+    for copy in saves + [last, kept[-1]]:
+        copy.wait()
+
+
+def forward(place, shards, tok, cot, tag, vec_in):
+    n = len(shards) - 1
+    Z, X, Y, C = place.Z, place.X, place.Y, place.C
+    R, T, D = tok.shape
+    L = Y * C * T
+    H = D // C
+    W3 = 3 * H
+    BQ = 512
+    pairs = H // 128
+    inside = pl.BlockSpec(memory_space=pltpu.VMEM)
+    anywhere = pl.BlockSpec(memory_space=pl.ANY)
+    out_shape = [jax.ShapeDtypeStruct((Y, C, Z, X) + m.shape, bf16) for m in shards[1:]]
+    out_shape += [
+        jax.ShapeDtypeStruct((Y, T, D), bf16),
+        jax.ShapeDtypeStruct((Y, T, D), bf16),
+        jax.ShapeDtypeStruct((8, D), f32),
+        jax.ShapeDtypeStruct((1, L), jnp.int32),
+        jax.ShapeDtypeStruct((L, W3), bf16),
+        jax.ShapeDtypeStruct((D, W3), bf16),
+        jax.ShapeDtypeStruct((D, L), bf16),
+        jax.ShapeDtypeStruct((Y * T, D), bf16),
+        jax.ShapeDtypeStruct((H, L), f32),
+        jax.ShapeDtypeStruct((pairs, 2, L), f32),
+    ]
+    each = (Z - 1) + 2 * Y + 1
+    copies = (n + 1) * each + 3 * (2 * (Y - 1) + 1) + (Y - 1) + Y
+    scratch = [
+        pltpu.VMEM((Y, C, Z, X) + shards[0].shape, bf16),
+        pltpu.VMEM((Y, C, T, D), bf16),
+        pltpu.VMEM((Y, C) + tag.shape[1:], jnp.int32),
+        pltpu.VMEM((Y, C) + vec_in.shape, bf16),
+        pltpu.VMEM((L, D), bf16),
+        pltpu.VMEM((D, L), bf16),
+        pltpu.VMEM((D, W3), bf16),
+        pltpu.VMEM((L, W3), bf16),
+        pltpu.VMEM((H, L), bf16),
+        pltpu.VMEM((L, H), bf16),
+        pltpu.VMEM((H, L), f32),
+        pltpu.SemaphoreType.DMA((copies,)),
+        pltpu.SemaphoreType.DMA((copies,)),
+        pltpu.SemaphoreType.DMA((n + 10 + Y,)),
+    ]
+    return pl.pallas_call(
+        functools.partial(forward_kernel, place, n, BQ),
+        out_shape=out_shape,
+        in_specs=[anywhere] * (n + 5),
+        out_specs=[anywhere] * (n + 2) + [inside] * 2 + [anywhere] * 5 + [inside],
+        scratch_shapes=scratch,
+        compiler_params=pltpu.CompilerParams(
+            collective_id=0, has_side_effects=True, vmem_limit_bytes=60 << 20
+        ),
+        name="forward",
+    )(*shards, tok, cot, tag, vec_in)
 
 
 class Summing:
@@ -1205,10 +1371,6 @@
     return value.reshape((Y, C, Z, X) + value.shape[2:])
 
 
-def chosen(pair, c):
-    return jnp.where(c == 0, pair[0], pair[1])
-
-
 def body(
     place,
     tokens,
@@ -1225,17 +1387,17 @@
     cotangent,
 ):
     rows, block, width = tokens.shape
-    Y, C = place.Y, place.C
-    length = place.blk * block
+    Y = place.Y
     index = lax.axis_index("blk")
-    c = index % C
-    half = width // C
     query_pos = index * block + jnp.arange(block, dtype=jnp.int32)
     local_tags = jnp.where(present == 1, segments, -1 - query_pos[None, :])
     tag_in = jnp.broadcast_to(local_tags[:, None, :], (rows, 8, block))
     vec_in = jnp.stack([gain_one, bias_one, gain_two, bias_two])
     vec_in = jnp.pad(vec_in, ((0, 12), (0, 0)))
-    proj_g, out_g, up_g, down_g, tok_g, cot_g, tag_g, vec_g = gather_all(
+    (
+        out_g, up_g, down_g, tok_mine, cot_mine, vec, begin, projected, proj_own, normed_t,
+        attended_low, attended_t, log_total,
+    ) = forward(
         place,
         [proj_weight, out_weight, up_weight, down_weight.T],
         tokens,
@@ -1243,45 +1405,17 @@
         tag_in,
         vec_in,
     )
-    proj_full = joined(proj_g, 0)
-    vec = vec_g.reshape(place.blk, 16, -1)[:, :8].transpose(1, 0, 2).reshape(8, width).astype(f32)
-    gain_a, bias_a = vec[0], vec[1]
-    proj_own = lax.dynamic_index_in_dim(
-        proj_full.reshape(width, 3, C, half), c, 2, keepdims=False
-    ).reshape(width, 3 * half)
-    row_tags = tag_g[:, :, 0].reshape(length)
-    row_pos = jnp.arange(length, dtype=jnp.int32)
-    begin = sum(
-        jnp.where(row_tags > s, jnp.sum((row_tags == s).astype(jnp.int32)), 0) for s in range(4)
-    )
-    begin = jnp.where(row_tags < 0, row_pos, begin)[None]
-    inputs = tok_g.reshape(length, width).astype(f32)
-    unit, factor = normed(inputs)
-    normed_low = (unit * gain_a + bias_a).astype(bf16)
-    projected = dot(normed_low, proj_own, 1, 0).astype(bf16)
-    attended, attended_t, log_total = attention_forward(projected, begin)
-    by_core = attended.reshape(Y, C, block, half).transpose(1, 0, 2, 3)
-    other = swap(place, by_core, 2).reshape(Y * block, half)
-    mine = lax.dynamic_index_in_dim(by_core, c, 0, keepdims=False).reshape(Y * block, half)
-    attended_low = jnp.concatenate(
-        [chosen((mine, other), c), chosen((other, mine), c)], axis=1
-    )
-    inputs_mine = (
-        lax.dynamic_index_in_dim(tok_g, c, 1, keepdims=False)
-        .reshape(Y * block, width)
-        .astype(f32)
-    )
+    tok_mine = tok_mine.reshape(Y * block, width)
     output, grad_middle, grad_attended, up_p, down_p, out_p, vec_two = dense(
         place,
         attended_low,
-        lax.dynamic_index_in_dim(tok_g, c, 1, keepdims=False).reshape(Y * block, width),
-        cot_g.reshape(Y * block, width),
+        tok_mine,
+        cot_mine.reshape(Y * block, width),
         out_g,
         up_g,
         down_g,
         vec,
     )
-    inputs_mine = lax.dynamic_index_in_dim(tok_g, c, 1, keepdims=False)
     proj_sum, out_sum, up_sum, down_sum, vec_sum, output, token_grad = backward(
         place,
         [out_p, up_p, down_p],
@@ -1291,9 +1425,9 @@
         grad_attended,
         attended_t,
         log_total,
-        normed_low.T,
+        normed_t,
         proj_own,
-        inputs_mine.reshape(Y * block, width),
+        tok_mine,
         grad_middle,
         output,
         vec,

time: 437 us -> 322 us (0.74)
  Pallas kernels: 372 us -> 304 us
  local copies, waits for them, and re-layouts: 33.5 us -> 11.3 us
  other arithmetic: 18.9 us -> 1.41 us
  matrix products: 5.91 us -> 0 us
    pallas_call x3 -> x1, Pallas kernels: 167 us -> 112 us  [forward(): pl.pallas_call(functools.partial(forward_kernel, place, n, BQ), out_shape...]
    pallas_call x1, Pallas kernels: 70.4 us -> 55.6 us  [dense(): pl.pallas_call(functools.partial(dense_kernel, place, aligned), out_shape...]
    reshape x3 -> x0, local copies, waits for them, and re-layouts: 11.4 us -> none  [the longest x1 6.16 us: joined(): gathered.reshape(Y * C, Z * X * r, w).transpose(1, 0, 2)]
    convert_element_type x2 -> x0, local copies, waits for them, and re-layouts: 6.1 us -> none  [the longest x1 5.41 us: body(): inputs = tok_g.reshape(length, width).astype(f32)]
    dot_general x1 -> x0, matrix products: 5.91 us -> none  [dot(): lax.dot_general(left, right, (((left_dim,), (right_dim,)), ((), ())), pre...]
    transpose x1 -> x0, other arithmetic: 5.48 us -> none  [body(): proj_sum, out_sum, up_sum, down_sum, vec_sum, output, token_grad = backwa...]
where the time goes in v3:
time: 322 us; the launch traced here: 318 us
  Pallas kernels  304 us (94%)
  local copies, waits for them, and re-layouts  11.3 us (4%)
    pallas_call x1, Pallas kernels, backward(): pl.pallas_call(functools.partial(backward_kernel, place, n, BQ), out_shap...  137 us
    pallas_call x1, Pallas kernels, forward(): pl.pallas_call(functools.partial(forward_kernel, place, n, BQ), out_shape...  112 us
    pallas_call x1, Pallas kernels, dense(): pl.pallas_call(functools.partial(dense_kernel, place, aligned), out_shape...  55.6 us
    unnamed x16, local copies, waits for them, and re-layouts  6.69 us

profile of v3, /device:TPU:0, one launch (start us, length us, event | category | flops | bytes accessed | tf_op | source)
XLA Modules:
  0.0 318.0 jit_solution(1259076908514013605)
XLA Ops:
  0.6 0.7 stack.15
  1.3 0.7 stack.16
  2.0 0.7 stack.17
  2.6 0.7 stack.18
  3.3 0.7 compare_select_fusion
  4.0 0.6 fusion.6.refs_7_
  4.6 0.6 broadcast_in_dim.16.refs_6_
  5.2 111.6 %forward.1 = (bf16[2,2,4,2,96,192]{5,4,3,2,1,0:T(8,128)(2,1)}, bf16[2,2,4,2,96,768]{5,4,3,2,1,0:T(8,128)(2,1)}, bf16[2,2,4,2,192,384]{5,4,3,2,1,0:T(8,128)(2,1)}...) custom-call(bf16[96,576]{1,0:T(8,128)(2,1)} %refs_0_.1, ...), custom_call_target="tpu_custom_call" | custom-call | tf_op jit(solution)/shard_map/forward/pallas_call | solution.py:497
  116.8 55.6 %dense.1 = (bf16[1024,768]{1,0:T(8,128)(2,1)}, f32[1024,768]{1,0:T(8,128)}, bf16[1024,768]{1,0:T(8,128)(2,1)}, bf16[4,768,768]{2,1,0:T(8,128)(2,1)}, bf16[4,8,19...) custom-call(bf16[1024,768]{1,0:T(8,128)(2,1)} %get-tuple-element.39.att, ...), custom_call_target="tpu_custom_call" | custom-call | tf_op jit(solution)/shard_map/dense/pallas_call | solution.py:1295
  172.4 137.2 %backward.1 = (f32[96,576]{1,0:T(8,128)}, f32[96,192]{1,0:T(8,128)}, f32[96,768]{1,0:T(8,128)}, f32[192,384]{1,0:T(8,128)}, f32[8,384]{1,0:T(8,128)}, /*index=5*...) custom-call(s32[1,2048]{1,0:T(1,128)} %get-tuple-element.37.refs_0_, bf16[2048,1152]{1,0:T(8,128)(2,1)} %get-tuple-element.38.refs_1_, ...), custom_call_target="tpu_custom_call" | custom-call | tf_op jit(solution)/shard_map/backward/pallas_call | solution.py:1087
  309.7 0.8 fusion.8
  310.4 0.1 fusion.7
  310.5 0.6 fusion.9
  311.1 0.0 copy-start
  311.1 2.8 copy.28
  313.9 0.0 copy-done
  313.9 0.0 copy-start.3
  313.9 0.0 copy-start.4
  313.9 0.0 copy-start.2
  313.9 0.0 copy-start.1
  313.9 1.1 copy.29
  315.1 0.0 copy-done.3
  315.1 0.7 copy.30
  315.7 0.0 copy-done.4
  315.8 0.6 copy.31
  316.4 0.0 copy-done.2
  316.4 0.7 copy.32
  317.1 0.0 copy-done.1
  317.1 0.7 copy.33
  (1 shorter events, 0.0 us)
Async XLA Ops:
  311.1 2.8 copy-start
  313.9 1.2 copy-start.3
  313.9 1.9 copy-start.4
  313.9 2.5 copy-start.2
  313.9 3.2 %copy-start.1 = (f32[192,384]{1,0:T(8,128)S(1)}, f32[192,384]{1,0:T(8,128)}, u32[]{:S(2)}) copy-start(f32[192,384]{1,0:T(8,128)} %get-tuple-element.62) | copy-start | bytes 884740

commit v4 on v3

v4 whole, which is shorter than its diff:
```python
import functools

import jax
import jax.numpy as jnp
from jax import lax
from jax.experimental import pallas as pl
from jax.experimental.pallas import tpu as pltpu
from jax.sharding import PartitionSpec as P

HEADS = 12
HEAD_DIM = 64
CORES = 2
LANE_X = 2
MESH = pl.DeviceIdType.MESH
LOG2E = 1.4426950408889634
epsilon = 1e-05
masked = -1e30
bf16 = jnp.bfloat16
f32 = jnp.float32


def dot(left, right, left_dim, right_dim):
    return lax.dot_general(
        left, right, (((left_dim,), (right_dim,)), ((), ())), preferred_element_type=f32
    )


class Place:
    def __init__(self, sizes):
        self.batch, self.blk = sizes
        self.Z, self.X = self.batch // LANE_X, LANE_X
        self.Y, self.C = self.blk // CORES, CORES

    def here(self):
        b, d = lax.axis_index("batch"), lax.axis_index("blk")
        return b // self.X, b % self.X, d // self.C, d % self.C

    def device(self, z, x, p, c):
        return (z * self.X + x, p * self.C + c)


class Wire:
    def __init__(self, send_sem, recv_sem):
        self.send_sem, self.recv_sem, self.names = send_sem, recv_sem, {}

    def copy(self, name, src, dst, device):
        i = self.names.setdefault(name, len(self.names))
        return pltpu.make_async_remote_copy(
            src_ref=src,
            dst_ref=dst,
            send_sem=self.send_sem.at[i],
            recv_sem=self.recv_sem.at[i],
            device_id=device,
            device_id_type=MESH,
        )


def start_all(copies):
    for copy in copies:
        copy.start()


def arrive_all(copies):
    for copy in copies:
        copy.wait_recv()


def leave_all(copies):
    for copy in copies:
        copy.wait_send()


def first_rows(rows, sixths):
    return min(rows - 16, 16 * ((rows * sixths // 6) // 16)) if rows > 16 else 0


def greet(place, partners):
    barrier = pltpu.get_barrier_semaphore()
    for partner in partners:
        pl.semaphore_signal(barrier, inc=1, device_id=partner, device_id_type=MESH)
    pl.semaphore_wait(barrier, len(partners))


def partners_of(place):
    z, x, p, c = place.here()
    found = [place.device((z + k) % place.Z, x, p, c) for k in range(1, place.Z)]
    found += [place.device(z, 1 - x, p, c)]
    found += [place.device(z, x, (p + k) % place.Y, c) for k in range(1, place.Y)]
    found += [place.device(z, x, p, 1 - c)]
    return found


def head_masked(value, h, axis):
    index = lax.broadcasted_iota(jnp.int32, value.shape, axis)
    return jnp.where((index // HEAD_DIM) == h, value, jnp.zeros_like(value))


class Spreading:
    def __init__(self, place, wire, name, spots, shard, whole, sixths):
        self.place, self.wire, self.name, self.spots = place, wire, name, spots
        self.shard, self.whole = shard, whole
        self.rows = shard.shape[0]
        self.h = first_rows(self.rows, sixths)

    def zero(self):
        z, x, p, c = self.spots
        place = self.place
        found = []
        for k in range(1, place.Z):
            found.append(
                self.wire.copy(
                    (self.name, "z", k),
                    self.shard,
                    self.whole.at[p, c, z, x],
                    place.device((z + k) % place.Z, x, p, c),
                )
            )
        return found

    def one(self):
        z, x, p, c = self.spots
        place, h, r = self.place, self.h, self.rows
        low = self.whole.at[p, c, :, x, 0:h]
        found = [self.wire.copy((self.name, "xa"), low, low, place.device(z, 1 - x, p, c))]
        high = self.whole.at[p, c, :, x, h:r]
        for k in range(1, place.Y):
            found.append(
                self.wire.copy(
                    (self.name, "yb", k), high, high, place.device(z, x, (p + k) % place.Y, c)
                )
            )
        return found

    def two(self):
        z, x, p, c = self.spots
        place, h, r = self.place, self.h, self.rows
        low = self.whole.at[p, c, :, :, 0:h]
        found = [
            self.wire.copy(
                (self.name, "ya", k), low, low, place.device(z, x, (p + k) % place.Y, c)
            )
            for k in range(1, place.Y)
        ]
        high = self.whole.at[:, c, :, x, h:r]
        found.append(
            self.wire.copy((self.name, "xb"), high, high, place.device(z, 1 - x, p, c))
        )
        return found

    def three(self):
        z, x, p, c = self.spots
        plane = self.whole.at[:, c]
        return [self.wire.copy((self.name, "core"), plane, plane, self.place.device(z, x, p, 1 - c))]

    def go_one(self):
        arrive_all(self.zero())
        start_all(self.one())

    def go_two_low(self):
        arrive_all(self.one()[:1])
        start_all(self.two()[:-1])

    def go_two_high(self):
        arrive_all(self.one()[1:])
        start_all(self.two()[-1:])

    def go_three(self):
        arrive_all(self.two())
        start_all(self.three())

    def leave(self):
        for copies in (self.zero(), self.one(), self.two(), self.three()):
            leave_all(copies)


FORWARD_PLAN = (
    "O1", "P1", "V", "N0", "K", "O2b", "P2a", "P2b", "U1", "N2", "P3", "O2a", "N3", "D1",
    "U2b", "W", "U2a", "O3", "J", "S00", "S01", "S02", "S10", "S11", "D2a", "S12", "D2b",
    "S20", "S21", "S22", "S30", "U3", "S31", "D3", "S32",
)


def forward_kernel(place, n, BQ, *refs):
    shards, (tok, segments, present, vec_in) = refs[: n + 1], refs[n + 1 : n + 5]
    outs = refs[n + 5 :]
    wholes = outs[:n]
    (tok_out, vec_out, begin, proj_out, w_out, normedT_out, att_out, oT_out, lt) = outs[
        n : n + 9
    ]
    (
        proj_v, tok_v, tag, tag_v, vec_v, n_v, nT, wv, pv, vT, att, oT,
        send_sem, recv_sem, local_sem,
    ) = outs[n + 9 :]
    spots = place.here()
    z, x, p, c = spots
    Z, X, Y, C = place.Z, place.X, place.Y, place.C
    D, W3 = wv.shape
    H = W3 // 3
    L = pv.shape[0]
    T = L // (Y * C)
    U = BQ // T
    pairs = H // 128
    nq = L // BQ
    wire = Wire(send_sem, recv_sem)
    sibling = place.device(z, x, p, 1 - c)
    flows = [
        Spreading(place, wire, m, spots, shards[m], proj_v if m == 0 else wholes[m - 1], 3)
        for m in range(n + 1)
    ]

    def local(i, src, dst):
        return pltpu.make_async_copy(src, dst, local_sem.at[i])

    def lane(offset, size):
        return pl.ds(pl.multiple_of(offset, 128), size)

    def line(offset, size):
        return pl.ds(pl.multiple_of(offset, 16), size)

    row_parts = (("vec", vec_in, vec_v), ("tag", tag, tag_v), ("tok", tok, tok_v))

    def along_y(what, src, dst):
        found = []
        for k in range(1, Y):
            to = (p + k) % Y
            piece = src if what == "vec" else src.at[to]
            found.append(
                wire.copy((what, "y", k), piece, dst.at[p, c], place.device(z, x, to, c))
            )
        return found

    def to_sibling_own(what, src, dst):
        piece = src if what == "vec" else src.at[p]
        return wire.copy((what, "own"), piece, dst.at[p, c], sibling)

    def to_sibling(what, dst):
        found = []
        for k in range(1, Y):
            q = (p + k) % Y
            found.append(wire.copy((what, "pass", k), dst.at[q, c], dst.at[q, c], sibling))
        return found

    position = lax.broadcasted_iota(jnp.int32, (Y, T), 1) + (p * C + c) * T
    tags = jnp.where(present[...] == 1, segments[...], -1 - position)
    for q in range(Y):
        tag[q] = jnp.broadcast_to(tags[q : q + 1, :], tag.shape[1:])
    greet(place, partners_of(place))
    for part in row_parts:
        start_all(along_y(*part))
    for part in row_parts:
        to_sibling_own(*part).start()
    for flow in flows:
        start_all(flow.zero())
    kept = [local(m, shards[m], flows[m].whole.at[p, c, z, x]) for m in range(n + 1)]
    kept += [
        local(n + 1, vec_in, vec_v.at[p, c]),
        local(n + 2, tag.at[p], tag_v.at[p, c]),
        local(n + 3, tok.at[p], tok_v.at[p, c]),
    ]
    start_all(kept)
    saves = [
        local(n + 5, nT, normedT_out),
        local(n + 6, tok_v.at[:, c], tok_out),
        local(n + 7, pv, proj_out),
        local(n + 8, wv, w_out),
    ]

    def norm_block(q, i):
        unit, factor = normed(tok_v[q, i].astype(f32))
        low = (unit * vec_out[0:1, :] + vec_out[1:2, :]).astype(bf16)
        rows = line((q * C + i) * T, T)
        n_v[rows, :] = low
        nT[:, lane((q * C + i) * T, T)] = low.T

    def begin_one(m):
        kept[m].wait()
        flows[m].go_one()

    def vector_pass():
        arrive_all(along_y(*row_parts[0]))
        start_all(to_sibling("vec", vec_v))

    def norm_near():
        for copy in kept[n + 1 :]:
            copy.wait()
        to_sibling_own(*row_parts[0]).wait_recv()
        arrive_all(to_sibling("vec", vec_v))
        share = vec_v.shape[3]
        for q in range(Y):
            for i in range(C):
                lo = (q * C + i) * share
                vec_out[:, lo : lo + share] = vec_v[q, i, 0:8, :].astype(f32)
        norm_block(p, c)
        to_sibling_own(*row_parts[2]).wait_recv()
        norm_block(p, 1 - c)

    def row_pass():
        for what, src, dst in row_parts[1:]:
            arrive_all(along_y(what, src, dst))
            start_all(to_sibling(what, dst))

    def norm_far():
        for k in range(1, Y):
            norm_block((p + k) % Y, c)

    def norm_last():
        arrive_all(to_sibling("tok", tok_v))
        for k in range(1, Y):
            norm_block((p + k) % Y, 1 - c)
        start_all(saves[:2])
        to_sibling_own(*row_parts[1]).wait_recv()
        arrive_all(to_sibling("tag", tag_v))
        tags = [tag_v[q, i, 0:1, :] for q in range(Y) for i in range(C)]
        counts = []
        for s in range(4):
            hits = sum((t == s).astype(f32) for t in tags)
            counts.append(jnp.sum(hits, axis=1, keepdims=True).astype(jnp.int32))
        for b, t in enumerate(tags):
            first = sum(jnp.where(t > s, counts[s], 0) for s in range(4))
            position = lax.broadcasted_iota(jnp.int32, (1, T), 1) + b * T
            begin[:, b * T : (b + 1) * T] = jnp.where(t < 0, position, first)

    def weight_columns():
        arrive_all(flows[0].three())
        r, w = proj_v.shape[4:]
        for mine in range(C):

            @pl.when(c == mine)
            def _():
                for third in range(3):
                    base = third * D + mine * H
                    for d in range(Y * C):
                        a, b = max(base, d * w), min(base + H, (d + 1) * w)
                        if a >= b:
                            continue
                        to = third * H + a - base
                        for i in range(Z * X):
                            wv[i * r : (i + 1) * r, to : to + b - a] = proj_v[
                                d // C, d % C, i // X, i % X, :, a - d * w : b - d * w
                            ]

    def project_all():
        def project(i, nothing):
            rows = line(i * BQ, BQ)
            pv[rows, :] = dot(n_v[rows, :], wv[...], 1, 0).astype(bf16)
            return nothing

        lax.fori_loop(0, nq, project, 0)
        vT[...] = pv[:, 2 * H :].T
        start_all(saves[2:])

    scale = HEAD_DIM ** (-0.5) * LOG2E

    def block_copies(qi):
        found = []
        for u in range(U):
            b = qi * U + u
            q, owner = b // C, b % C
            src = att.at[b * T : (b + 1) * T, :]
            dst = att_out.at[q * T : (q + 1) * T, lane(c * H, H)]
            found.append(
                (owner, local(n + 9 + q, src, dst), wire.copy(("att", q), src, dst, sibling))
            )
        return found

    acts = {
        "V": vector_pass,
        "N0": norm_near,
        "K": row_pass,
        "N2": norm_far,
        "N3": norm_last,
        "W": weight_columns,
        "J": project_all,
    }
    for m, name in enumerate("POUD"):
        acts[name + "1"] = functools.partial(begin_one, m)
        acts[name + "2a"] = flows[m].go_two_low
        acts[name + "2b"] = flows[m].go_two_high
        acts[name + "3"] = flows[m].go_three
    events, spot = {}, None
    for name in FORWARD_PLAN:
        if name[0] == "S":
            spot = (int(name[1]), int(name[2]))
        else:
            events.setdefault(spot, []).append(name)
    for name in events[None]:
        acts[name]()
    for qi in range(nq):
        qs = slice(qi * BQ, (qi + 1) * BQ)
        d0 = qi * BQ
        if qi == nq - 1:
            cuts = [(0, d0, 1)] if d0 else []
        elif d0 > 256:
            cuts = [(0, 256, 1), (256, d0, 0)]
        else:
            cuts = [(0, d0, 1)] if d0 else []
        cuts.append((d0, d0 + BQ, 2))

        def one_pair(pair, nothing):
            cols = lane(pair * 128, 128)
            k_cols = lane(H + pair * 128, 128)
            qT = pv[qs, cols].T
            found = []
            for h in range(2):
                query = head_masked(qT, h, 0)
                rows = pl.ds(pl.multiple_of(pair * 128 + h * HEAD_DIM, HEAD_DIM), HEAD_DIM)
                parts = []
                for a, b, mode in cuts:
                    s = dot(pv[a:b, k_cols], query, 1, 0) * scale
                    if mode:
                        key_pos = lax.broadcasted_iota(jnp.int32, (b - a, BQ), 0) + a
                        visible = key_pos >= begin[:, qs]
                        if mode == 2:
                            query_pos = lax.broadcasted_iota(jnp.int32, (b - a, BQ), 1) + d0
                            visible = jnp.logical_and(visible, key_pos <= query_pos)
                        s = jnp.where(visible, s, masked)
                    parts.append(s)
                top = functools.reduce(
                    jnp.maximum, [jnp.max(s, axis=0, keepdims=True) for s in parts]
                )
                total, accum = 0.0, 0.0
                for (a, b, mode), s in zip(cuts, parts):
                    e = jnp.exp2(s - top)
                    total = total + jnp.sum(e, axis=0, keepdims=True)
                    accum = accum + dot(vT[rows, a:b], e.astype(bf16), 1, 0)
                result = accum / total
                oT[rows, qs] = result
                found.append(result)
                lt[pair, h : h + 1, qs] = top + jnp.log2(total)
            att[qs, cols] = jnp.concatenate(found, axis=0).astype(bf16).T
            for number in range(pairs):
                if (qi, number) in events:

                    @pl.when(pair == number)
                    def _():
                        for name in events[qi, number]:
                            acts[name]()

            return nothing

        lax.fori_loop(0, pairs, one_pair, 0)
        for owner, keep, send in block_copies(qi):

            @pl.when(owner == c)
            def _():
                keep.start()

            @pl.when(owner != c)
            def _():
                send.start()

    last = local(n + 9 + Y, oT, oT_out)
    last.start()
    for flow in flows[1:]:
        arrive_all(flow.three())
    for qi in range(nq):
        for owner, keep, send in block_copies(qi):

            @pl.when(owner == c)
            def _():
                keep.wait()

            @pl.when(owner != c)
            def _():
                send.wait_send()

            @pl.when(owner == c)
            def _():
                send.wait_recv()

    for what, src, dst in row_parts:
        leave_all(along_y(what, src, dst))
        to_sibling_own(what, src, dst).wait_send()
        leave_all(to_sibling(what, dst))
    for flow in flows:
        flow.leave()
    for copy in saves + [last]:
        copy.wait()


def forward(place, shards, tok, segments, present, vec_in):
    n = len(shards) - 1
    Z, X, Y, C = place.Z, place.X, place.Y, place.C
    R, T, D = tok.shape
    L = Y * C * T
    H = D // C
    W3 = 3 * H
    BQ = 512
    pairs = H // 128
    inside = pl.BlockSpec(memory_space=pltpu.VMEM)
    anywhere = pl.BlockSpec(memory_space=pl.ANY)
    out_shape = [jax.ShapeDtypeStruct((Y, C, Z, X) + m.shape, bf16) for m in shards[1:]]
    out_shape += [
        jax.ShapeDtypeStruct((Y, T, D), bf16),
        jax.ShapeDtypeStruct((8, D), f32),
        jax.ShapeDtypeStruct((1, L), jnp.int32),
        jax.ShapeDtypeStruct((L, W3), bf16),
        jax.ShapeDtypeStruct((D, W3), bf16),
        jax.ShapeDtypeStruct((D, L), bf16),
        jax.ShapeDtypeStruct((Y * T, D), bf16),
        jax.ShapeDtypeStruct((H, L), f32),
        jax.ShapeDtypeStruct((pairs, 2, L), f32),
    ]
    each = (Z - 1) + 2 * Y + 1
    copies = (n + 1) * each + 3 * (2 * (Y - 1) + 1) + Y
    scratch = [
        pltpu.VMEM((Y, C, Z, X) + shards[0].shape, bf16),
        pltpu.VMEM((Y, C, T, D), bf16),
        pltpu.VMEM((Y, 8, T), jnp.int32),
        pltpu.VMEM((Y, C, 8, T), jnp.int32),
        pltpu.VMEM((Y, C) + vec_in.shape, bf16),
        pltpu.VMEM((L, D), bf16),
        pltpu.VMEM((D, L), bf16),
        pltpu.VMEM((D, W3), bf16),
        pltpu.VMEM((L, W3), bf16),
        pltpu.VMEM((H, L), bf16),
        pltpu.VMEM((L, H), bf16),
        pltpu.VMEM((H, L), f32),
        pltpu.SemaphoreType.DMA((copies,)),
        pltpu.SemaphoreType.DMA((copies,)),
        pltpu.SemaphoreType.DMA((n + 10 + Y,)),
    ]
    return pl.pallas_call(
        functools.partial(forward_kernel, place, n, BQ),
        out_shape=out_shape,
        in_specs=[inside] * (n + 1) + [anywhere] + [inside] * 3,
        out_specs=[anywhere] * (n + 1) + [inside] * 2 + [anywhere] * 5 + [inside],
        scratch_shapes=scratch,
        compiler_params=pltpu.CompilerParams(
            collective_id=0, has_side_effects=True, vmem_limit_bytes=60 << 20
        ),
        name="forward",
    )(*shards, tok, segments, present, vec_in)


class Summing:
    def __init__(self, place, wire, name, spots, acc, xa, yb, ya, xb, zz):
        self.place, self.wire, self.name, self.spots = place, wire, name, spots
        self.acc, self.xa, self.yb, self.ya, self.xb, self.zz = acc, xa, yb, ya, xb, zz
        self.rows = acc.shape[3]
        self.h = xa.shape[2]

    def one(self):
        z, x, p, c = self.spots
        place, h, r = self.place, self.h, self.rows
        side = place.device(z, 1 - x, p, c)
        found = [
            self.wire.copy((self.name, "xa"), self.acc.at[:, :, 1 - x, 0:h], self.xa, side)
        ]
        for k in range(1, place.Y):
            to = (p + k) % place.Y
            found.append(
                self.wire.copy(
                    (self.name, "yb", k),
                    self.acc.at[to, :, :, h:r],
                    self.yb.at[k - 1],
                    place.device(z, x, to, c),
                )
            )
        return found

    def two(self):
        z, x, p, c = self.spots
        place, h, r = self.place, self.h, self.rows
        found = []
        for k in range(1, place.Y):
            to = (p + k) % place.Y
            found.append(
                self.wire.copy(
                    (self.name, "ya", k),
                    self.acc.at[to, :, x, 0:h],
                    self.ya.at[k - 1],
                    place.device(z, x, to, c),
                )
            )
        side = place.device(z, 1 - x, p, c)
        found.append(
            self.wire.copy((self.name, "xb"), self.acc.at[p, :, 1 - x, h:r], self.xb, side)
        )
        return found

    def three(self):
        z, x, p, c = self.spots
        place = self.place
        found = []
        for k in range(1, place.Z):
            to = (z + k) % place.Z
            found.append(
                self.wire.copy(
                    (self.name, "z", k),
                    self.acc.at[p, to, x],
                    self.zz.at[k - 1],
                    place.device(to, x, p, c),
                )
            )
        return found

    def add_one(self):
        z, x, p, c = self.spots
        place, h, r, acc = self.place, self.h, self.rows, self.acc
        ones = self.one()
        ones[0].wait_recv()

        def low(i, nothing):
            a, b = i // place.Z, i % place.Z
            total = acc[a, b, x, 0:h].astype(f32) + self.xa[a, b].astype(f32)
            acc[a, b, x, 0:h] = total.astype(bf16)
            return nothing

        lax.fori_loop(0, place.Y * place.Z, low, 0)
        twos = self.two()
        start_all(twos[:-1])
        arrive_all(ones[1:])

        def high(i, nothing):
            a, b = i // place.X, i % place.X
            total = acc[p, a, b, h:r].astype(f32)
            for k in range(place.Y - 1):
                total = total + self.yb[k, a, b].astype(f32)
            acc[p, a, b, h:r] = total.astype(bf16)
            return nothing

        lax.fori_loop(0, place.Z * place.X, high, 0)
        twos[-1].start()

    def add_two(self):
        z, x, p, c = self.spots
        place, h, r, acc = self.place, self.h, self.rows, self.acc
        arrive_all(self.two())

        def both(i, nothing):
            total = acc[p, i, x, 0:h].astype(f32)
            for k in range(place.Y - 1):
                total = total + self.ya[k, i].astype(f32)
            acc[p, i, x, 0:h] = total.astype(bf16)
            total = acc[p, i, x, h:r].astype(f32) + self.xb[i].astype(f32)
            acc[p, i, x, h:r] = total.astype(bf16)
            return nothing

        lax.fori_loop(0, place.Z, both, 0)
        start_all(self.three())

    def finish(self, target):
        z, x, p, c = self.spots
        arrive_all(self.three())
        total = self.acc[p, z, x].astype(f32)
        for k in range(self.place.Z - 1):
            total = total + self.zz[k].astype(f32)
        target[...] = total

    def leave(self):
        leave_all(self.one())
        leave_all(self.two())
        leave_all(self.three())


class DepthSum:
    def __init__(self, place, wire, name, spots, acc, zr, xr, yr):
        self.place, self.wire, self.name, self.spots = place, wire, name, spots
        self.acc, self.zr, self.xr, self.yr = acc, zr, xr, yr

    def one(self):
        z, x, p, c = self.spots
        place = self.place
        return [
            self.wire.copy(
                (self.name, "z", k),
                self.acc.at[:, (z + k) % place.Z],
                self.zr.at[k - 1],
                place.device((z + k) % place.Z, x, p, c),
            )
            for k in range(1, place.Z)
        ]

    def two(self):
        z, x, p, c = self.spots
        side = self.place.device(z, 1 - x, p, c)
        return [self.wire.copy((self.name, "x"), self.acc.at[:, z, 1 - x], self.xr, side)]

    def three(self):
        z, x, p, c = self.spots
        place = self.place
        return [
            self.wire.copy(
                (self.name, "y", k),
                self.acc.at[(p + k) % place.Y, z, x],
                self.yr.at[k - 1],
                place.device(z, x, (p + k) % place.Y, c),
            )
            for k in range(1, place.Y)
        ]

    def add_one(self):
        z, x, p, c = self.spots
        place, acc = self.place, self.acc
        arrive_all(self.one())

        def add(i, nothing):
            a, b = i // place.X, i % place.X
            total = acc[a, z, b].astype(f32)
            for k in range(place.Z - 1):
                total = total + self.zr[k, a, b].astype(f32)
            acc[a, z, b] = total.astype(bf16)
            return nothing

        lax.fori_loop(0, place.Y * place.X, add, 0)
        start_all(self.two())

    def add_two(self):
        z, x, p, c = self.spots
        place, acc = self.place, self.acc
        arrive_all(self.two())

        def add(i, nothing):
            total = acc[i, z, x].astype(f32) + self.xr[i].astype(f32)
            acc[i, z, x] = total.astype(bf16)
            return nothing

        lax.fori_loop(0, place.Y, add, 0)
        start_all(self.three())

    def finish(self, target):
        z, x, p, c = self.spots
        arrive_all(self.three())
        total = self.acc[p, z, x].astype(f32)
        for k in range(self.place.Y - 1):
            total = total + self.yr[k].astype(f32)
        target[...] = total

    def leave(self):
        leave_all(self.one())
        leave_all(self.two())
        leave_all(self.three())


class ChunkSum:
    def __init__(self, place, wire, name, spots, acc, xr, zr, total, far):
        self.place, self.wire, self.name, self.spots = place, wire, name, spots
        self.acc, self.xr, self.zr, self.total, self.far = acc, xr, zr, total, far

    def along_x(self):
        z, x, p, c = self.spots
        side = self.place.device(z, 1 - x, p, c)
        return [self.wire.copy((self.name, "x"), self.acc.at[:, 1 - x], self.xr, side)]

    def along_z(self):
        z, x, p, c = self.spots
        place = self.place
        return [
            self.wire.copy(
                (self.name, "z", k),
                self.acc.at[(z + k) % place.Z, x],
                self.zr.at[k - 1],
                place.device((z + k) % place.Z, x, p, c),
            )
            for k in range(1, place.Z)
        ]

    def along_y(self):
        z, x, p, c = self.spots
        place = self.place
        return [
            self.wire.copy(
                (self.name, "y", k),
                self.total.at[0],
                self.total.at[k],
                place.device(z, x, (p + k) % place.Y, c),
            )
            for k in range(1, place.Y)
        ]

    def to_core(self):
        z, x, p, c = self.spots
        return [
            self.wire.copy(
                (self.name, "core"), self.total, self.far, self.place.device(z, x, p, 1 - c)
            )
        ]

    def go_z(self):
        z, x, p, c = self.spots
        arrive_all(self.along_x())

        def one(i, nothing):
            total = self.acc[i, x].astype(f32) + self.xr[i].astype(f32)
            self.acc[i, x] = total.astype(bf16)
            return nothing

        lax.fori_loop(0, self.place.Z, one, 0)
        start_all(self.along_z())

    def go_y(self):
        z, x, p, c = self.spots
        arrive_all(self.along_z())
        total = self.acc[z, x].astype(f32)
        for k in range(self.place.Z - 1):
            total = total + self.zr[k].astype(f32)
        self.total[0] = total.astype(bf16)
        start_all(self.along_y())

    def go_core(self):
        arrive_all(self.along_y())
        start_all(self.to_core())

    def result(self):
        arrive_all(self.to_core())
        return [
            sum(part[k].astype(f32) for k in range(self.place.Y)) for part in (self.total, self.far)
        ]

    def leave(self):
        for copies in (self.along_x(), self.along_z(), self.along_y(), self.to_core()):
            leave_all(copies)


BACKWARD_PLAN = (
    "U0", "S00", "S01", "O0", "S02", "S03", "U1", "C0x", "S10", "D0", "U2", "S11", "S12",
    "C0z", "S13", "C1x", "S20", "B3", "D1", "S21", "C1z", "B2", "S22", "S23", "D2", "T3",
    "C2x", "B1", "C0y", "O1", "UF", "T2", "B0", "C1y", "T1", "C0c", "T0", "C2z", "C1c",
    "Vc", "Vx", "C2y", "Vz", "O2", "C0r", "Vy", "C1r", "DF", "C2c", "OF", "Vr", "C2r",
)


def backward_kernel(place, n, BQ, *refs):
    (begin, proj, grad_in, oT_in, lt, normedT, w_in, tok, gm, vec, vec_two) = refs[:11]
    parts, others = refs[11 : 11 + n], refs[11 + n : 11 + 2 * n]
    outs = refs[11 + 2 * n :]
    sums, (vec_out, tg_home) = outs[: n + 1], outs[n + 1 : n + 3]
    landing = outs[n + 3 : 2 * n + 3]
    rest = outs[2 * n + 3 :]
    (
        pv, do, oT, wv, kT, dk, dv, nT,
        keep, g_send, g_recv, tok_v, gm_v, grads, v0, v1, v2, v3, vc, vy, vx, vz, whole,
    ) = rest[:23]
    buffers = rest[23 : 23 + 6 * n - 2]
    chunk_buffers = rest[23 + 6 * n - 2 : -3]
    send_sem, recv_sem, local_sem = rest[-3:]
    tg_v = g_recv
    spots = place.here()
    z, x, p, c = spots
    Z, X, Y, C = place.Z, place.X, place.Y, place.C
    L, W3 = pv.shape
    H = W3 // 3
    D = wv.shape[0]
    T = L // (Y * C)
    pairs = H // 128
    nq = L // BQ
    scale = HEAD_DIM ** (-0.5) * LOG2E
    scale_back = HEAD_DIM ** (-0.5)
    wire = Wire(send_sem, recv_sem)
    sibling = place.device(z, x, p, 1 - c)
    beside = place.device(z, 1 - x, p, c)
    adds = [DepthSum(place, wire, 0, spots, *buffers[:4])]
    adds += [
        Summing(place, wire, m, spots, *buffers[6 * m - 2 : 6 * m + 4]) for m in range(1, n)
    ]
    chunks = [
        ChunkSum(place, wire, ("chunk", i), spots, *chunk_buffers[5 * i : 5 * i + 5])
        for i in range(pairs)
    ]

    def local(i, src, dst):
        return pltpu.make_async_copy(src, dst, local_sem.at[i])

    def lane(offset, size):
        return pl.ds(pl.multiple_of(offset, 128), size)

    def line(offset, size):
        return pl.ds(pl.multiple_of(offset, 16), size)

    def out_fetch(pair):
        return local(2, oT_in.at[line(pair * 128, 128), :], oT)

    loads = [local(0, proj, pv), local(1, grad_in, do), local(3, w_in, wv)]
    late = local(4 + 2 * n, normedT, nT)
    halves = [
        (local(4 + m, parts[m], adds[m].acc), local(4 + n + m, others[m], landing[m]))
        for m in range(n)
    ]
    for m in (1, 2, 0):
        start_all(halves[m])
    start_all(loads + [late])
    out_fetch(0).start()
    greet(place, partners_of(place))
    row_sem = 5 + 2 * n

    def core_add(m):
        for copy in halves[m]:
            copy.wait()
        acc, other = adds[m].acc, landing[m]

        def one(i, nothing):
            a, b, d = i // (Z * X), (i // X) % Z, i % X
            total = acc[a, b, d].astype(f32) + other[a, b, d].astype(f32)
            acc[a, b, d] = total.astype(bf16)
            return nothing

        lax.fori_loop(0, Y * Z * X, one, 0)

    for copy in loads:
        copy.wait()
    kT[...] = pv[:, H : 2 * H].T
    grads[...] = jnp.zeros_like(grads)

    U = BQ // T
    gain = vec[0:1, :]

    def sub_blocks(qi):
        found = []
        for u in range(U):
            block = qi * U + u
            found.append((u, block // C, block % C))
        return found

    reserved = send_sem.shape[0] - 3 * Y

    def g_wire(q):
        return pltpu.make_async_remote_copy(
            src_ref=g_send.at[q],
            dst_ref=g_recv.at[q],
            send_sem=send_sem.at[reserved + q],
            recv_sem=recv_sem.at[reserved + q],
            device_id=sibling,
            device_id_type=MESH,
        )

    def home_from(k):
        q = (p + k) % Y
        return pltpu.make_async_remote_copy(
            src_ref=tg_v.at[p],
            dst_ref=tg_home.at[q],
            send_sem=send_sem.at[reserved + Y + q],
            recv_sem=recv_sem.at[reserved + 2 * Y + q],
            device_id=place.device(z, x, q, c),
            device_id_type=MESH,
        )

    def home_to(q):
        return pltpu.make_async_remote_copy(
            src_ref=tg_v.at[q],
            dst_ref=tg_home.at[p],
            send_sem=send_sem.at[reserved + Y + q],
            recv_sem=recv_sem.at[reserved + 2 * Y + p],
            device_id=place.device(z, x, q, c),
            device_id_type=MESH,
        )

    def block_done(qi):
        g = dot(pv[line(qi * BQ, BQ), :], wv[...], 1, 1)
        for u, q, owner in sub_blocks(qi):
            rows = slice(u * T, (u + 1) * T)

            @pl.when(owner == c)
            def _():
                keep[(qi % 2 * U + u) // C] = g[rows, :]

            @pl.when(owner != c)
            def _():
                g_send[q] = g[rows, :].astype(bf16)
                g_wire(q).start()

    def pair_done(i):
        wide = [pv[:, t * H + i * 128 : t * H + (i + 1) * 128] for t in range(3)]
        value = dot(nT[...], jnp.concatenate(wide, axis=1), 1, 0).astype(bf16)
        chunk = chunks[i]
        r = chunk.acc.shape[2]
        for b in range(Z * X):
            chunk.acc[b // X, b % X] = value[b * r : (b + 1) * r, :]
        start_all(chunk.along_x())

    def token_rows(qi):
        for u, q, owner in sub_blocks(qi):

            @pl.when(owner == c)
            def _():
                a = local(row_sem, tok.at[line(q * T, T)], tok_v)
                b = local(row_sem + 1, gm.at[line(q * T, T)], gm_v)
                a.start()
                b.start()
                g_wire(q).wait_recv()
                grad = keep[(qi % 2 * U + u) // C] + g_recv[q].astype(f32)
                a.wait()
                unit, factor = normed(tok_v[...].astype(f32))
                grads[0:1, :] += jnp.sum(grad * unit, axis=0, keepdims=True)
                grads[1:2, :] += jnp.sum(grad, axis=0, keepdims=True)
                b.wait()
                tg_v[q] = (gm_v[...] + norm_back(grad, gain, unit, factor)).astype(bf16)

                @pl.when(q == p)
                def _():
                    local(row_sem + 2, tg_v.at[q], tg_home.at[p]).start()

                @pl.when(q != p)
                def _():
                    home_to(q).start()

    def one_query(pair, qi):
        d0 = qi * BQ
        qs = slice(d0, d0 + BQ)
        cols = lane(pair * 128, 128)
        k_cols, v_cols = lane(H + pair * 128, 128), lane(2 * H + pair * 128, 128)
        q_val, do_val = pv[qs, cols], do[qs, cols]
        qT, doT = q_val.T, do_val.T
        part = BQ // 2
        cuts = []
        if d0 and qi < nq - 1:
            cuts = [(0, part, 1, 0), (part, min(BQ, d0), 0, 0)]
            cuts += [(a, a + BQ, 0, 0) for a in range(BQ, d0, BQ)]
        elif d0:
            cuts = [(a, a + BQ, 1, 0) for a in range(0, d0, BQ)]
        cuts += [(d0, d0 + part, 2, 0), (d0 + part, d0 + BQ, 2, part)]
        dqs = []
        for h in range(2):
            rows = slice(h * HEAD_DIM, (h + 1) * HEAD_DIM)
            kT_rows = pl.ds(pl.multiple_of(pair * 128 + h * HEAD_DIM, HEAD_DIM), HEAD_DIM)
            query, grad = head_masked(qT, h, 0), head_masked(doT, h, 0)
            q_nat, do_nat = head_masked(q_val, h, 1), head_masked(do_val, h, 1)
            delta = jnp.sum(doT[rows, :].astype(f32) * oT[rows, qs], axis=0, keepdims=True)
            log_total = lt[pair, h : h + 1, qs]
            dq = jnp.zeros((HEAD_DIM, BQ), f32)
            for a, b, mode, qa in cuts:
                sc = dot(pv[a:b, k_cols], query[:, qa:], 1, 0) * scale
                prob = jnp.exp2(sc - log_total[:, qa:])
                if mode:
                    shape = (b - a, BQ - qa)
                    key_pos = lax.broadcasted_iota(jnp.int32, shape, 0) + a
                    visible = key_pos >= begin[:, d0 + qa : d0 + BQ]
                    if mode == 2:
                        query_pos = lax.broadcasted_iota(jnp.int32, shape, 1) + d0 + qa
                        visible = jnp.logical_and(visible, key_pos <= query_pos)
                    prob = jnp.where(visible, prob, 0.0)
                dp = dot(pv[a:b, v_cols], grad[:, qa:], 1, 0)
                ds = (prob * (dp - delta[:, qa:])).astype(bf16)
                dv[a:b, :] += dot(prob.astype(bf16), do_nat[qa:], 1, 0)
                dk[a:b, :] += dot(ds, q_nat[qa:], 1, 0)
                more = dot(kT[kT_rows, a:b], ds, 1, 0)
                if qa:
                    more = jnp.concatenate([jnp.zeros((HEAD_DIM, qa), f32), more], axis=1)
                dq = dq + more
            dqs.append(dq)
        pv[qs, cols] = (jnp.concatenate(dqs, axis=0) * scale_back).astype(bf16).T
        pv[qs, k_cols] = (dk[qs, :] * scale_back).astype(bf16)
        pv[qs, v_cols] = dv[qs, :].astype(bf16)

    out_m, up_m, down_m = adds
    v_core = wire.copy("vc", v0, vc, sibling)
    v_x = wire.copy("vx", v1, vx, beside)
    v_z = [
        wire.copy(("vz", k), v2, vz.at[k - 1], place.device((z + k) % Z, x, p, c))
        for k in range(1, Z)
    ]
    v_y = [
        wire.copy(("vy", k), v3, vy.at[k - 1], place.device(z, x, (p + k) % Y, c))
        for k in range(1, Y)
    ]

    def vector_core():
        grads[2:4, :] = vec_two[...]
        v0[0:4, :] = grads[0:4, 0:H]
        v0[4:8, :] = grads[0:4, H:]
        v_core.start()

    def vector_x():
        v_core.wait_recv()
        v1[...] = v0[...] + vc[...]
        v_x.start()

    def vector_z():
        v_x.wait_recv()
        v2[...] = v1[...] + vx[...]
        start_all(v_z)

    def vector_y():
        arrive_all(v_z)
        v3[...] = v2[...] + sum(vz[k] for k in range(Z - 1))
        start_all(v_y)

    def vector_end():
        arrive_all(v_y)
        vec_out[...] = v3[...] + sum(vy[k] for k in range(Y - 1))

    def chunk_end(i):
        mine, far = chunks[i].result()
        for half in range(C):

            @pl.when(c == half)
            def _():
                for value, core in ((mine, half), (far, 1 - half)):
                    for t in range(3):
                        lo = t * D + core * H + i * 128
                        whole[:, lo : lo + 128] = value[:, t * 128 : (t + 1) * 128]

    def out_start():
        core_add(0)
        start_all(out_m.one())

    def up_start():
        core_add(1)
        start_all(up_m.one())

    def down_start():
        core_add(2)
        start_all(down_m.one())

    acts = {
        "U0": up_start,
        "U1": up_m.add_one,
        "U2": up_m.add_two,
        "UF": lambda: up_m.finish(sums[2]),
        "D0": down_start,
        "D1": down_m.add_one,
        "D2": down_m.add_two,
        "DF": lambda: down_m.finish(sums[3]),
        "O0": out_start,
        "O1": out_m.add_one,
        "O2": out_m.add_two,
        "OF": lambda: out_m.finish(sums[1]),
        "Vc": vector_core,
        "Vx": vector_x,
        "Vz": vector_z,
        "Vy": vector_y,
        "Vr": vector_end,
    }
    for i, chunk in enumerate(chunks):
        acts[f"C{i}x"] = functools.partial(pair_done, i)
        acts[f"C{i}z"] = chunk.go_z
        acts[f"C{i}y"] = chunk.go_y
        acts[f"C{i}c"] = chunk.go_core
        acts[f"C{i}r"] = functools.partial(chunk_end, i)
    for qi in range(nq):
        acts[f"B{qi}"] = functools.partial(block_done, qi)
        acts[f"T{qi}"] = functools.partial(token_rows, qi)
    events, spot = {}, None
    for name in BACKWARD_PLAN:
        if name[0] == "S":
            spot = (int(name[1]), int(name[2]))
        else:
            events.setdefault(spot, []).append(name)

    def one_pair(pair, nothing):
        out_fetch(pair).wait()
        dk[...] = jnp.zeros_like(dk)
        dv[...] = jnp.zeros_like(dv)
        for i in range(nq):
            one_query(pair, nq - 1 - i)
            if i == nq - 1:

                @pl.when(pair < pairs - 1)
                def _():
                    out_fetch(pair + 1).start()

            for number in range(pairs):
                if (number, i) in events and (number, i) != (pairs - 1, nq - 1):

                    @pl.when(pair == number)
                    def _():
                        for name in events[number, i]:
                            acts[name]()

        return nothing

    for name in events.get(None, ()):
        acts[name]()
    late.wait()
    lax.fori_loop(0, pairs, one_pair, 0)
    for name in events[pairs - 1, nq - 1]:
        acts[name]()
    w = sums[0].shape[1]
    for d in range(Y * C):

        @pl.when(p * C + c == d)
        def _():
            sums[0][...] = whole[:, d * w : (d + 1) * w]

    for k in range(1, Y):
        home_from(k).wait_recv()
        home_to((p + k) % Y).wait_send()
    local(row_sem + 2, tg_v.at[p], tg_home.at[p]).wait()
    for q in range(Y):
        g_wire(q).wait_send()
    v_core.wait_send()
    leave_all(v_y)
    v_x.wait_send()
    leave_all(v_z)
    for summing in adds + chunks:
        summing.leave()


def backward(place, parts, others, proj_shape, begin, proj, heads, oT, lt, normedT, w_own, tok, gm, vec, vec_two):
    n = len(parts)
    Z, X, Y, C = place.Z, place.X, place.Y, place.C
    L, W3 = proj.shape
    H = W3 // 3
    D = w_own.shape[0]
    T = L // (Y * C)
    BQ = 512
    inside = pl.BlockSpec(memory_space=pltpu.VMEM)
    anywhere = pl.BlockSpec(memory_space=pl.ANY)
    shapes = [proj_shape] + [part.shape[3:] for part in parts]
    sixths = [3, 3]
    out_shape = [jax.ShapeDtypeStruct(shape, f32) for shape in shapes]
    out_shape += [
        jax.ShapeDtypeStruct((8, H), f32),
        jax.ShapeDtypeStruct((Y, T, D), bf16),
    ]
    scratch = [pltpu.VMEM((Y, Z, X) + shape, bf16) for shape in shapes[1:]]
    scratch += [
        pltpu.VMEM((L, W3), bf16),
        pltpu.VMEM((L, H), bf16),
        pltpu.VMEM((128, L), f32),
        pltpu.VMEM((D, W3), bf16),
        pltpu.VMEM((H, L), bf16),
        pltpu.VMEM((L, 128), f32),
        pltpu.VMEM((L, 128), f32),
        pltpu.VMEM((D, L), bf16),
        pltpu.VMEM((max(1, 2 * (BQ // T) // C), T, D), f32),
        pltpu.VMEM((Y, T, D), bf16),
        pltpu.VMEM((Y, T, D), bf16),
        pltpu.VMEM((T, D), bf16),
        pltpu.VMEM((T, D), f32),
    ]
    scratch += [pltpu.VMEM((8, D), f32)] + [pltpu.VMEM((8, H), f32)] * 5
    scratch += [
        pltpu.VMEM((Y - 1, 8, H), f32),
        pltpu.VMEM((8, H), f32),
        pltpu.VMEM((Z - 1, 8, H), f32),
        pltpu.VMEM((proj_shape[0], 3 * D), f32),
    ]
    r, w = shapes[1]
    scratch += [
        pltpu.VMEM((Y, Z, X, r, w), bf16),
        pltpu.VMEM((Z - 1, Y, X, r, w), bf16),
        pltpu.VMEM((Y, r, w), bf16),
        pltpu.VMEM((Y - 1, r, w), bf16),
    ]
    for shape, part in zip(shapes[2:], sixths):
        r, w = shape
        h = first_rows(r, part)
        scratch += [
            pltpu.VMEM((Y, Z, X, r, w), bf16),
            pltpu.VMEM((Y, Z, h, w), bf16),
            pltpu.VMEM((Y - 1, Z, X, r - h, w), bf16),
            pltpu.VMEM((Y - 1, Z, h, w), bf16),
            pltpu.VMEM((Z, r - h, w), bf16),
            pltpu.VMEM((Z - 1, r, w), bf16),
        ]
    r = proj_shape[0]
    for pair in range(H // 128):
        scratch += [
            pltpu.VMEM((Z, X, r, 384), bf16),
            pltpu.VMEM((Z, r, 384), bf16),
            pltpu.VMEM((Z - 1, r, 384), bf16),
            pltpu.VMEM((Y, r, 384), bf16),
            pltpu.VMEM((Y, r, 384), bf16),
        ]
    each = 1 + (Y - 1) + (Y - 1) + 1 + (Z - 1)
    chunk_copies = 1 + (Z - 1) + (Y - 1) + 1
    copies = n * each + (H // 128) * chunk_copies + 2 + (Y - 1) + 1 + (Z - 1) + 3 * Y
    scratch += [
        pltpu.SemaphoreType.DMA((copies,)),
        pltpu.SemaphoreType.DMA((copies,)),
        pltpu.SemaphoreType.DMA((5 + 2 * n + 3,)),
    ]
    return pl.pallas_call(
        functools.partial(backward_kernel, place, n, BQ),
        out_shape=out_shape,
        in_specs=[inside] + [anywhere] * 3 + [inside] + [anywhere] * 4 + [inside] * 2 + [anywhere] * (2 * n),
        out_specs=[inside] * (n + 2) + [anywhere],
        scratch_shapes=scratch,
        compiler_params=pltpu.CompilerParams(
            collective_id=1, has_side_effects=True, vmem_limit_bytes=63 << 20
        ),
        name="backward",
    )(begin, proj, heads, oT, lt, normedT, w_own, tok, gm, vec, vec_two, *parts, *others)


def gelu_both(u):
    k = 0.7978845608028654
    square = u * u
    t = jnp.tanh(k * u * (1.0 + 0.044715 * square))
    half = 0.5 * (1.0 + t)
    slope = half + 0.5 * k * u * (1.0 - t * t) * (1.0 + 3 * 0.044715 * square)
    return u * half, slope


class Task:
    def __init__(self, copy, far):
        self.copy, self.far, self.left, self.here = copy, far, False, False
        copy.start()

    def gone(self):
        if not self.left:
            if self.far:
                self.copy.wait_send()
            else:
                self.copy.wait()
            self.left = True

    def came(self):
        if self.far and not self.here:
            self.copy.wait_recv()
            self.here = True


def dense_kernel(
    place, aligned, att, tok, cot, out_w, up_w, down_w, vec,
    home, gm_out, heads, up_own, down_own, out_own, up_other, down_other, out_other, vec_out,
    att_v, tok_v, cot_v, out_v, up_v, down_v, out_full, mid, n2, act, gh, n2T, cotT, oacc, g2,
    h_buf, g_buf, stage, up_cut, down_cut, load_sem, store_sem, send_sem, recv_sem,
):
    S, nb, Y, C = place.blk, place.batch, place.Y, place.C
    z, x, p, c = place.here()
    M, D = att_v.shape
    J = up_v.shape[1] // D
    T = M // Y
    H = D // C
    half = M // 2
    sibling = place.device(z, x, p, 1 - c)
    others = [place.device(z, x, (p + k) % Y, c) for k in range(1, Y)]
    wire = Wire(send_sem, recv_sem)
    loads, tasks = [], []

    def line(offset, size):
        return pl.ds(pl.multiple_of(offset, 16), size)

    def lane(offset, size):
        return pl.ds(pl.multiple_of(offset, 128), size)

    def load(src, dst):
        task = Task(pltpu.make_async_copy(src, dst, load_sem.at[len(loads)]), False)
        loads.append(task)
        return task

    def store(src, dst):
        count = sum(not task.far for task in tasks)
        tasks.append(Task(pltpu.make_async_copy(src, dst, store_sem.at[count]), False))
        return tasks[-1]

    def send(name, src, dst, device):
        tasks.append(Task(wire.copy(name, src, dst, device), True))
        return tasks[-1]

    first = [load(att, att_v), load(tok, tok_v), load(out_w, out_v)]
    first.append(load(cot.at[p], cot_v.at[line(p * T, T), :]))
    if aligned:
        w = up_w.shape[2]
        weights = [load(up_w.at[d], up_v.at[:, d * w : (d + 1) * w]) for d in range(S)]
        r, w = down_w.shape[2:]
        weights += [
            load(down_w.at[d, b], down_v.at[d * r : (d + 1) * r, b * w : (b + 1) * w])
            for d in range(S)
            for b in range(nb)
        ]
    else:
        weights = [load(up_w, up_v), load(down_w, down_v)]
    greet(place, others + [sibling])
    cots = []
    for k in range(1, Y):
        to = (p + k) % Y
        cots.append(send(("cot", k), cot.at[to], cot_v.at[line(p * T, T), :], others[k - 1]))
    for task in first:
        task.gone()
    w = out_v.shape[2]
    for d in range(S):
        out_full[:, d * w : (d + 1) * w] = out_v[d]
    gain, shift = vec[2:3, :], vec[3:4, :]
    near = (p * T) // half
    halves = [1 - near, near]
    rows_of = [line(t * half, half) for t in halves]
    for t in (0, 1):
        ts = rows_of[t]
        middle = tok_v[ts, :].astype(f32) + dot(att_v[ts, :], out_full[...], 1, 0)
        unit, factor = normed(middle)
        mid[ts, :] = middle
        low = (unit * gain + shift).astype(bf16)
        n2[ts, :] = low
        n2T[:, lane(halves[t] * half, half)] = low.T
    for task in weights:
        task.gone()
    w_up = up_own.shape[2]
    in_chunk = D // w_up
    chunks = []
    for s in range(J):
        if in_chunk == 1:
            chunks.append((s // C) * C + (1 - c if s % C == 0 else c))
        else:
            chunks.append(s)

    def cols(s):
        return lane(chunks[s] * D, D)

    busy = {}

    def staged(key, value, width, cut):
        for task in busy.get(key, []):
            task.gone()
        busy[key] = []
        if cut is not None:
            for i in range(value.shape[1] // width):
                cut[i] = value[:, i * width : (i + 1) * width]
            return lambda rows, i: cut.at[i, rows, :]
        stage[key] = value
        if value.shape[1] == width:
            return lambda rows, i: stage.at[key, rows, :]
        return lambda rows, i: stage.at[key, rows, i * width : (i + 1) * width]

    def up_gradient(s):
        value = dot(n2T[...], gh[:, cols(s)], 1, 0).astype(bf16)
        piece = staged(0, value, w_up, None if aligned else up_cut)
        every = slice(0, D)
        if in_chunk == 1:
            q = s // C
            if s % C == 0:
                busy[0].append(send(("up", s), piece(every, 0), up_other.at[q], sibling))
            else:
                busy[0].append(store(piece(every, 0), up_own.at[q]))
            return
        for i in range(in_chunk // C):
            q = s * in_chunk // C + i
            busy[0].append(store(piece(every, C * i + c), up_own.at[q]))
            busy[0].append(send(("up", q), piece(every, C * i + 1 - c), up_other.at[q], sibling))

    def down_gradient(s):
        value = dot(cotT[...], act[:, cols(s)], 1, 0).astype(bf16)
        r, w = down_own.shape[2:]
        piece = staged(1, value, w, None if aligned else down_cut)
        for q in range(Y):
            for i in range(D // w):
                b = chunks[s] * (D // w) + i
                busy[1].append(store(piece(line((C * q + c) * r, r), i), down_own.at[q, b]))
                busy[1].append(
                    send(
                        ("down", s, q, i),
                        piece(line((C * q + 1 - c) * r, r), i),
                        down_other.at[q, b],
                        sibling,
                    )
                )

    units = [(0, "f", s) for s in range(J)] + [(1, "fb", s) for s in range(J)]
    units += [(0, "b", s) for s in range(J)]

    def ahead(number):
        t, kind, s = units[number]
        slot = number % 2
        if "f" in kind:
            h_buf[slot] = dot(n2[rows_of[t], :], up_v[:, cols(s)], 1, 0)
        if "b" in kind:
            g_buf[slot] = dot(cot_v[rows_of[t], :], down_v[:, cols(s)], 1, 0)

    def output_rows(t):
        ts = rows_of[t]
        tok_v[ts, :] = (mid[ts, :] + oacc[...]).astype(bf16)
        for i in range(half // T):
            q = halves[t] * (half // T) + i
            if Y == 2 and t == 1:
                store(tok_v.at[ts, :], home.at[q])
            elif Y == 2:
                send("home", tok_v.at[ts, :], home.at[p], others[0])

    sums = [jnp.zeros((1, D), f32), jnp.zeros((1, D), f32)]

    def norm_rows(t):
        ts = rows_of[t]
        unit, factor = normed(mid[ts, :])
        grad = g2[...]
        sums[0] = sums[0] + jnp.sum(grad * unit, axis=0, keepdims=True)
        sums[1] = sums[1] + jnp.sum(grad, axis=0, keepdims=True)
        gm = cot_v[ts, :].astype(f32) + norm_back(grad, gain, unit, factor)
        mid[ts, :] = gm
        low = gm.astype(bf16)
        n2[ts, :] = low
        cot_v[ts, :] = dot(low, out_full[...], 1, 1).astype(bf16)
        store(mid.at[ts, :], gm_out.at[ts, :])
        for i in range(half // T):
            q = halves[t] * (half // T) + i
            rows = line(q * T, T)
            spot = line((C * q + c) * T, T)
            store(cot_v.at[rows, lane(c * H, H)], heads.at[spot, :])
            send(("ga", t, i), cot_v.at[rows, lane((1 - c) * H, H)], heads.at[spot, :], sibling)

    ahead(0)
    for number, (t, kind, s) in enumerate(units):
        ts, slot = rows_of[t], number % 2
        if number + 1 < len(units):
            if units[number + 1] == ((0, "b", 0) if Y == 2 else (1, "fb", 0)):
                for task in cots:
                    task.came()
            ahead(number + 1)
        if "f" in kind:
            a, slope = gelu_both(h_buf[slot])
            a = a.astype(bf16)
            act[ts, cols(s)] = a
            more = dot(a, down_v[:, cols(s)], 1, 1)
            if s == 0:
                oacc[...] = more
            else:
                oacc[...] += more
            if kind == "f":
                gh[ts, cols(s)] = slope.astype(bf16)
        else:
            slope = gh[ts, cols(s)].astype(f32)
        if "b" in kind:
            b = (g_buf[slot] * slope).astype(bf16)
            gh[ts, cols(s)] = b
            more = dot(b, up_v[:, cols(s)], 1, 1)
            if s == 0:
                g2[...] = more
            else:
                g2[...] += more
        if kind == "b":
            up_gradient(s)
            down_gradient(s)
        if s == J - 1:
            if kind == "f":
                output_rows(t)
            elif kind == "fb":
                output_rows(t)
                cotT[:, lane(halves[t] * half, half)] = cot_v[ts, :].T
                norm_rows(t)
                cotT[:, lane(halves[0] * half, half)] = cot_v[rows_of[0], :].T
            else:
                norm_rows(t)
    if Y > 2:
        store(tok_v.at[line(p * T, T), :], home.at[p])
        for k in range(1, Y):
            to = (p + k) % Y
            send(("home", k), tok_v.at[line(to * T, T), :], home.at[p], others[k - 1])
    vec_out[0:1, :] = sums[0]
    vec_out[1:2, :] = sums[1]
    value = dot(att_v[...], n2[...], 0, 0).astype(bf16)
    w = out_own.shape[2]
    for d in range(S):
        out_v[d] = value[:, d * w : (d + 1) * w]
    for q in range(Y):
        store(out_v.at[C * q + c], out_own.at[q])
        send(("out", q), out_v.at[C * q + 1 - c], out_other.at[q], sibling)
    for task in tasks:
        task.came()
    for task in tasks:
        task.gone()


def dense(place, att, tok, cot, out_g, up_g, down_g, vec):
    M, D = att.shape
    S, nb, Y, C = place.blk, place.batch, place.Y, place.C
    T = M // Y
    H = D // C
    aligned = up_g.shape[-1] % 128 == 0 and down_g.shape[-1] % 128 == 0
    out_w = out_g.reshape(S, D, -1)
    FF = S * up_g.shape[-1]
    if aligned:
        up_w = up_g.reshape(S, D, -1)
        down_w = down_g.reshape((S, nb) + down_g.shape[-2:])
    else:
        up_w, down_w = joined(up_g, 0), joined(down_g, 1)
    anywhere = pl.BlockSpec(memory_space=pl.ANY)
    inside = pl.BlockSpec(memory_space=pltpu.VMEM)
    pieces = [
        jax.ShapeDtypeStruct((Y, D, up_g.shape[-1]), bf16),
        jax.ShapeDtypeStruct((Y, nb) + down_g.shape[-2:], bf16),
        jax.ShapeDtypeStruct((Y, D, out_g.shape[-1]), bf16),
    ]
    none = (1, 16, 128)
    up_cut = none if aligned else (D // up_g.shape[-1], D, up_g.shape[-1])
    down_cut = none if aligned else (D // down_g.shape[-1], D, down_g.shape[-1])
    loads = 8 + S + S * nb
    J = FF // D
    down_count = J * Y * (D // down_g.shape[-1])
    copies = 2 * (Y - 1) + 2 * Y + S + down_count + 4 * Y + 8
    results = pl.pallas_call(
        functools.partial(dense_kernel, place, aligned),
        out_shape=[
            jax.ShapeDtypeStruct((Y, T, D), bf16),
            jax.ShapeDtypeStruct((M, D), f32),
            jax.ShapeDtypeStruct((S * T, H), bf16),
        ]
        + pieces
        + pieces
        + [jax.ShapeDtypeStruct((2, D), f32)],
        in_specs=[anywhere] * 6 + [inside],
        out_specs=[anywhere] * 9 + [inside],
        scratch_shapes=[
            pltpu.VMEM((M, D), bf16),
            pltpu.VMEM((M, D), bf16),
            pltpu.VMEM((M, D), bf16),
            pltpu.VMEM(out_w.shape, bf16),
            pltpu.VMEM((D, FF), bf16),
            pltpu.VMEM((D, FF), bf16),
            pltpu.VMEM((D, D), bf16),
            pltpu.VMEM((M, D), f32),
            pltpu.VMEM((M, D), bf16),
            pltpu.VMEM((M, FF), bf16),
            pltpu.VMEM((M, FF), bf16),
            pltpu.VMEM((D, M), bf16),
            pltpu.VMEM((D, M), bf16),
            pltpu.VMEM((M // 2, D), f32),
            pltpu.VMEM((M // 2, D), f32),
            pltpu.VMEM((2, M // 2, D), f32),
            pltpu.VMEM((2, M // 2, D), f32),
            pltpu.VMEM((2, D, D), bf16) if aligned else pltpu.VMEM((1, 16, 128), bf16),
            pltpu.VMEM(up_cut, bf16),
            pltpu.VMEM(down_cut, bf16),
            pltpu.SemaphoreType.DMA((loads,)),
            pltpu.SemaphoreType.DMA((copies,)),
            pltpu.SemaphoreType.DMA((copies,)),
            pltpu.SemaphoreType.DMA((copies,)),
        ],
        compiler_params=pltpu.CompilerParams(
            collective_id=2, has_side_effects=True, vmem_limit_bytes=62 << 20
        ),
        name="dense",
    )(att, tok, cot, out_w, up_w, down_w, vec)
    home, gm, heads = results[:3]
    shapes = [(Y,) + up_g.shape[2:], (Y,) + down_g.shape[2:], (Y,) + out_g.shape[2:]]
    own = [value.reshape(shape) for value, shape in zip(results[3:6], shapes)]
    other = [value.reshape(shape) for value, shape in zip(results[6:9], shapes)]
    return home, gm, heads, own, other, results[9]


def hand_over_kernel(place, n, *refs):
    given, vec, out, vec_out = refs[:n], refs[n], refs[n + 1 : 2 * n + 1], refs[2 * n + 1]
    whole, between, sem = refs[2 * n + 2], refs[2 * n + 3 : 3 * n + 3], refs[3 * n + 3]
    here = [pltpu.make_async_copy(given[i], between[i], sem.at[0, i]) for i in range(n)]
    away = [pltpu.make_async_copy(between[i], out[i], sem.at[1, i]) for i in range(n)]
    start_all(here)
    H = vec.shape[1]
    whole[0:4, 0:H] = vec[0:4, :]
    whole[0:4, H:] = vec[4:8, :]
    me = lax.axis_index("blk")
    w = vec_out.shape[1]
    for d in range(place.blk):

        @pl.when(me == d)
        def _():
            vec_out[...] = whole[0:4, d * w : (d + 1) * w]

    for i in range(n):
        here[i].wait()
        away[i].start()
    for copy in away:
        copy.wait()


def hand_over(place, given, vec):
    n = len(given)
    anywhere = pl.BlockSpec(memory_space=pl.ANY)
    inside = pl.BlockSpec(memory_space=pltpu.VMEM)
    H = vec.shape[1]
    return pl.pallas_call(
        functools.partial(hand_over_kernel, place, n),
        out_shape=[jax.ShapeDtypeStruct(v.shape, v.dtype) for v in given]
        + [jax.ShapeDtypeStruct((4, 2 * H // place.blk), f32)],
        in_specs=[anywhere] * n + [inside],
        out_specs=[anywhere] * n + [inside],
        scratch_shapes=[pltpu.VMEM((8, 2 * H), f32)]
        + [pltpu.VMEM(v.shape, v.dtype) for v in given]
        + [pltpu.SemaphoreType.DMA((2, n))],
        compiler_params=pltpu.CompilerParams(vmem_limit_bytes=62 << 20),
        name="hand_over",
    )(*given, vec)


def normed(values):
    average = jnp.mean(values, axis=-1, keepdims=True)
    centered = values - average
    variance = jnp.mean(centered * centered, axis=-1, keepdims=True)
    factor = lax.rsqrt(variance + epsilon)
    return centered * factor, factor


def norm_back(grad, gain, unit, factor):
    e = grad * gain
    return factor * (
        e - jnp.mean(e, axis=-1, keepdims=True) - unit * jnp.mean(e * unit, axis=-1, keepdims=True)
    )


def joined(gathered, axis):
    Y, C, Z, X, r, w = gathered.shape
    if axis == 0:
        return gathered.reshape(Y * C, Z * X * r, w).transpose(1, 0, 2).reshape(Z * X * r, -1)
    return gathered.reshape(Y * C, Z * X, r, w).transpose(0, 2, 1, 3).reshape(Y * C * r, -1)


def parted(whole, place, axis):
    Y, C, Z, X = place.Y, place.C, place.Z, place.X
    rows, columns = whole.shape
    if axis == 0:
        value = whole.reshape(Z * X, rows // (Z * X), Y * C, columns // (Y * C))
        value = value.transpose(2, 0, 1, 3)
    else:
        value = whole.reshape(Y * C, rows // (Y * C), Z * X, columns // (Z * X))
        value = value.transpose(0, 2, 1, 3)
    return value.reshape((Y, C, Z, X) + value.shape[2:])


def body(
    place,
    tokens,
    proj_weight,
    out_weight,
    up_weight,
    down_weight,
    gain_one,
    bias_one,
    gain_two,
    bias_two,
    segments,
    present,
    cotangent,
):
    rows, block, width = tokens.shape
    Y = place.Y
    row = lax.broadcasted_iota(jnp.int32, (16, width // place.blk), 0)
    vec_in = jnp.zeros(row.shape, bf16)
    for i, vector in enumerate((gain_one, bias_one, gain_two, bias_two)):
        vec_in = jnp.where(row == i, vector[None, :], vec_in)
    (
        out_g, up_g, down_g, tok_mine, vec, begin, projected, proj_own, normed_t,
        attended_low, attended_t, log_total,
    ) = forward(
        place,
        [proj_weight, out_weight, up_weight, down_weight.T],
        tokens,
        segments,
        present,
        vec_in,
    )
    tok_mine = tok_mine.reshape(Y * block, width)
    output, grad_middle, grad_heads, own, other, vec_two = dense(
        place, attended_low, tok_mine, cotangent, out_g, up_g, down_g, vec
    )
    order = (2, 0, 1)
    proj_sum, out_sum, up_sum, down_sum, vec_sum, token_grad = backward(
        place,
        [own[i] for i in order],
        [other[i] for i in order],
        proj_weight.shape,
        begin,
        projected,
        grad_heads,
        attended_t,
        log_total,
        normed_t,
        proj_own,
        tok_mine,
        grad_middle,
        vec,
        vec_two,
    )
    output, token_grad, proj_sum, out_sum, up_sum, down_sum, vectors = hand_over(
        place, (output, token_grad, proj_sum, out_sum, up_sum, down_sum), vec_sum
    )
    return (
        output,
        token_grad,
        proj_sum,
        out_sum,
        up_sum,
        down_sum.T,
        vectors[0],
        vectors[1],
        vectors[2],
        vectors[3],
    )


def solution(mesh):
    place = Place((mesh.shape["batch"], mesh.shape["blk"]))
    weight, vector = P("batch", "blk"), P("blk")
    row = P("batch", "blk", None)
    in_specs = (row,) + (weight,) * 4 + (vector,) * 4 + (weight,) * 2 + (row,)
    out_specs = (row, row) + (weight,) * 4 + (vector,) * 4
    return jax.shard_map(
        functools.partial(body, place),
        mesh=mesh,
        in_specs=in_specs,
        out_specs=out_specs,
        check_vma=False,
    )
```

time: 322 us -> 269 us (0.84)
  Pallas kernels: 304 us -> 262 us
  local copies, waits for them, and re-layouts: 11.3 us -> 1.41 us
    pallas_call x1, Pallas kernels: 137 us -> 104 us  [backward(): pl.pallas_call(functools.partial(backward_kernel, place, n, BQ), out_shap...]
    pallas_call x1, Pallas kernels: 112 us -> 98.5 us  [forward(): pl.pallas_call(functools.partial(forward_kernel, place, n, BQ), out_shape...]
    unnamed x16 -> x0, local copies, waits for them, and re-layouts: 6.69 us -> none
    pallas_call x0 -> x1, Pallas kernels: none -> 4.77 us  [hand_over(): pl.pallas_call(functools.partial(hand_over_kernel, place, n), out_shape=[...]
where the time goes in v4:
time: 269 us; the launch traced here: 266 us
  Pallas kernels  262 us (97%)
    pallas_call x1, Pallas kernels, backward(): pl.pallas_call(functools.partial(backward_kernel, place, n, BQ), out_shap...  104 us
    pallas_call x1, Pallas kernels, forward(): pl.pallas_call(functools.partial(forward_kernel, place, n, BQ), out_shape...  98.5 us
    pallas_call x1, Pallas kernels, dense(): pl.pallas_call(functools.partial(dense_kernel, place, aligned), out_shape...  54.9 us

profile of v4, /device:TPU:0, one launch (start us, length us, event | category | flops | bytes accessed | tf_op | source)
XLA Modules:
  0.0 265.8 jit_solution(16063322287508267579)
XLA Ops:
  0.7 1.4 select_select_fusion.refs_7_
  2.1 98.5 %forward.1 = (bf16[2,2,4,2,96,192]{5,4,3,2,1,0:T(8,128)(2,1)}, bf16[2,2,4,2,96,768]{5,4,3,2,1,0:T(8,128)(2,1)}, bf16[2,2,4,2,192,384]{5,4,3,2,1,0:T(8,128)(2,1)}...) custom-call(bf16[96,576]{1,0:T(8,128)(2,1)} %refs_0_.1, ...), custom_call_target="tpu_custom_call" | custom-call | tf_op jit(solution)/shard_map/forward/pallas_call | solution.py:523
  100.6 54.9 %dense.1 = (bf16[2,512,768]{2,1,0:T(8,128)(2,1)}, f32[1024,768]{1,0:T(8,128)}, bf16[2048,384]{1,0:T(8,128)(2,1)}, bf16[2,768,768]{2,1,0:T(8,128)(2,1)}, bf16[2,8...) custom-call(bf16[1024,768]{1,0:T(8,128)(2,1)} %get-tuple-element.45., ...), custom_call_target="tpu_custom_call" | custom-call | tf_op jit(solution)/shard_map/dense/pallas_call | solution.py:1571
  155.5 103.9 %backward.1 = (f32[96,576]{1,0:T(8,128)}, f32[96,192]{1,0:T(8,128)}, f32[96,768]{1,0:T(8,128)}, f32[192,384]{1,0:T(8,128)}, f32[8,384]{1,0:T(8,128)}, /*index=5*/bf16[2,512,768]{2,1,0:T(8,128)(2,1)}) custom-call(s32[1,2048]{1,0:T(1,128)} %get-tuple-element.52.refs_0_, bf16[2048,1152]{1,0:T(8,128)(2,1)} %get-tuple-element.53.refs_1_, ...), custom_call_target="tpu_custom_call" | custom-call | tf_op jit(solution)/shard_map/backward/pallas_call | solution.py:1264
  259.4 4.8 %hand_over.1 = (bf16[2,512,768]{2,1,0:T(8,128)(2,1)}, bf16[2,512,768]{2,1,0:T(8,128)(2,1)}, f32[96,576]{1,0:T(8,128)}, f32[96,192]{1,0:T(8,128)}, f32[96,768]{1,...) custom-call(bf16[2,512,768]{2,1,0:T(8,128)(2,1)} %get-tuple-element.51.refs_0_, ...), custom_call_target="tpu_custom_call" | custom-call | tf_op jit(solution)/shard_map/hand_over/pallas_call | solution.py:1650
  264.2 1.4 fusion
  (2 shorter events, 0.0 us)

commit v5 on v4

--- a/solution.py
+++ b/solution.py
@@ -38,6 +38,15 @@
     def device(self, z, x, p, c):
         return (z * self.X + x, p * self.C + c)
 
+    def across_z(self):
+        return [k for k in range(2, self.Z)] + [1]
+
+    def mirror(self, z, k):
+        for bit in range(self.Z.bit_length()):
+            if k >> bit & 1:
+                z = z + (1 << bit) - (2 << bit) * (z // (1 << bit) % 2)
+        return z
+
 
 class Wire:
     def __init__(self, send_sem, recv_sem):
@@ -83,7 +92,7 @@
 
 def partners_of(place):
     z, x, p, c = place.here()
-    found = [place.device((z + k) % place.Z, x, p, c) for k in range(1, place.Z)]
+    found = [place.device(place.mirror(z, k), x, p, c) for k in place.across_z()]
     found += [place.device(z, 1 - x, p, c)]
     found += [place.device(z, x, (p + k) % place.Y, c) for k in range(1, place.Y)]
     found += [place.device(z, x, p, 1 - c)]
@@ -96,88 +105,123 @@
 
 
 class Spreading:
-    def __init__(self, place, wire, name, spots, shard, whole, sixths):
+    def __init__(self, place, wire, name, spots, shard, whole, deep, low):
         self.place, self.wire, self.name, self.spots = place, wire, name, spots
         self.shard, self.whole = shard, whole
-        self.rows = shard.shape[0]
-        self.h = first_rows(self.rows, sixths)
-
-    def zero(self):
+        self.r = shard.shape[0]
+        self.g = sixths(self.r, deep)
+        self.h = self.g + sixths(self.r, low)
+
+    def copy(self, what, src, dst, device):
+        return self.wire.copy((self.name, what), src, dst, device)
+
+    def sides(self):
         z, x, p, c = self.spots
         place = self.place
+        along_y = [(k, place.device(z, x, (p + k) % place.Y, c)) for k in range(1, place.Y)]
+        along_z = [(k, place.device(place.mirror(z, k), x, p, c)) for k in place.across_z()]
+        return place.device(z, 1 - x, p, c), along_y, along_z
+
+    def deep_one(self):
+        z, x, p, c = self.spots
+        src, dst = self.shard.at[0 : self.g], self.whole.at[p, c, z, x, 0 : self.g]
+        return [self.copy(("dy", k), src, dst, side) for k, side in self.sides()[1]]
+
+    def deep_two(self):
+        z, x, p, c = self.spots
+        part = self.whole.at[:, c, z, x, 0 : self.g]
+        return [self.copy("dx", part, part, self.sides()[0])]
+
+    def deep_three(self):
+        z, x, p, c = self.spots
+        part = self.whole.at[:, c, z, :, 0 : self.g]
+        return [self.copy(("dz", k), part, part, side) for k, side in self.sides()[2]]
+
+    def along_z(self, what, rows):
+        z, x, p, c = self.spots
+        src, dst = self.shard.at[rows], self.whole.at[p, c, z, x, rows]
+        return [self.copy((what, k), src, dst, side) for k, side in self.sides()[2]]
+
+    def low_zero(self):
+        return self.along_z("za", slice(self.g, self.h))
+
+    def high_zero(self):
+        return self.along_z("zb", slice(self.h, self.r))
+
+    def low_one(self):
+        z, x, p, c = self.spots
+        part = self.whole.at[p, c, :, x, self.g : self.h]
+        return [self.copy("xa", part, part, self.sides()[0])]
+
+    def high_one(self):
+        z, x, p, c = self.spots
+        part = self.whole.at[p, c, :, x, self.h : self.r]
+        return [self.copy(("yb", k), part, part, side) for k, side in self.sides()[1]]
+
+    def low_two(self):
+        z, x, p, c = self.spots
+        part = self.whole.at[p, c, :, :, self.g : self.h]
+        return [self.copy(("ya", k), part, part, side) for k, side in self.sides()[1]]
+
+    def high_two(self):
+        z, x, p, c = self.spots
+        part = self.whole.at[:, c, :, x, self.h : self.r]
+        return [self.copy("xb", part, part, self.sides()[0])]
+
+    def to_core(self, what, rows):
+        z, x, p, c = self.spots
+        part = self.whole.at[:, c, :, :, rows]
+        return [self.copy(what, part, part, self.place.device(z, x, p, 1 - c))]
+
+    def low_three(self):
+        return self.to_core("ca", slice(self.g, self.h))
+
+    def high_three(self):
+        return self.to_core("cb", slice(self.h, self.r))
+
+    def deep_four(self):
+        return self.to_core("cd", slice(0, self.g))
+
+    def chains(self):
         found = []
-        for k in range(1, place.Z):
-            found.append(
-                self.wire.copy(
-                    (self.name, "z", k),
-                    self.shard,
-                    self.whole.at[p, c, z, x],
-                    place.device((z + k) % place.Z, x, p, c),
-                )
-            )
+        if self.g:
+            found.append([self.deep_one, self.deep_two, self.deep_three, self.deep_four])
+        if self.g < self.h:
+            found.append([self.low_zero, self.low_one, self.low_two, self.low_three])
+        if self.h < self.r:
+            found.append([self.high_zero, self.high_one, self.high_two, self.high_three])
         return found
 
-    def one(self):
-        z, x, p, c = self.spots
-        place, h, r = self.place, self.h, self.rows
-        low = self.whole.at[p, c, :, x, 0:h]
-        found = [self.wire.copy((self.name, "xa"), low, low, place.device(z, 1 - x, p, c))]
-        high = self.whole.at[p, c, :, x, h:r]
-        for k in range(1, place.Y):
-            found.append(
-                self.wire.copy(
-                    (self.name, "yb", k), high, high, place.device(z, x, (p + k) % place.Y, c)
-                )
-            )
-        return found
-
-    def two(self):
-        z, x, p, c = self.spots
-        place, h, r = self.place, self.h, self.rows
-        low = self.whole.at[p, c, :, :, 0:h]
-        found = [
-            self.wire.copy(
-                (self.name, "ya", k), low, low, place.device(z, x, (p + k) % place.Y, c)
-            )
-            for k in range(1, place.Y)
-        ]
-        high = self.whole.at[:, c, :, x, h:r]
-        found.append(
-            self.wire.copy((self.name, "xb"), high, high, place.device(z, 1 - x, p, c))
-        )
-        return found
-
-    def three(self):
-        z, x, p, c = self.spots
-        plane = self.whole.at[:, c]
-        return [self.wire.copy((self.name, "core"), plane, plane, self.place.device(z, x, p, 1 - c))]
-
-    def go_one(self):
-        arrive_all(self.zero())
-        start_all(self.one())
-
-    def go_two_low(self):
-        arrive_all(self.one()[:1])
-        start_all(self.two()[:-1])
-
-    def go_two_high(self):
-        arrive_all(self.one()[1:])
-        start_all(self.two()[-1:])
-
-    def go_three(self):
-        arrive_all(self.two())
-        start_all(self.three())
+    def begin(self):
+        for chain in self.chains():
+            start_all(chain[0]())
+
+    def step(self, group, number):
+        chain = (
+            [self.deep_one, self.deep_two, self.deep_three, self.deep_four],
+            [self.low_zero, self.low_one, self.low_two, self.low_three],
+            [self.high_zero, self.high_one, self.high_two, self.high_three],
+        )[group]
+        arrive_all(chain[number - 1]())
+        start_all(chain[number]())
+
+    def arrive(self):
+        for chain in self.chains():
+            arrive_all(chain[3]())
 
     def leave(self):
-        for copies in (self.zero(), self.one(), self.two(), self.three()):
-            leave_all(copies)
+        for chain in self.chains():
+            for stage in chain:
+                leave_all(stage())
 
 
 FORWARD_PLAN = (
-    "O1", "P1", "V", "N0", "K", "O2b", "P2a", "P2b", "U1", "N2", "P3", "O2a", "N3", "D1",
-    "U2b", "W", "U2a", "O3", "J", "S00", "S01", "S02", "S10", "S11", "D2a", "S12", "D2b",
-    "S20", "S21", "S22", "S30", "U3", "S31", "D3", "S32",
+    "t1", "O1d", "V", "D1d", "O2d", "t2", "U1d", "N0", "P1a", "P1b", "t3", "P2b", "P2a",
+    "U1b", "K", "U1a", "D1b", "P3b", "D1a", "P3a", "N2", "N3", "W", "U2b", "U2a", "D2d",
+    "J", "S00", "S01", "D2b", "D2a", "S02", "S10", "O3d", "S11", "S12", "U2d", "S20",
+    "S21", "S22", "U3a", "S30", "U3b", "D3b", "U3d", "S31", "D3a", "D3d", "S32",
 )
+ROW_PARTS = 4
 
 
 def forward_kernel(place, n, BQ, *refs):
@@ -204,8 +248,8 @@
     wire = Wire(send_sem, recv_sem)
     sibling = place.device(z, x, p, 1 - c)
     flows = [
-        Spreading(place, wire, m, spots, shards[m], proj_v if m == 0 else wholes[m - 1], 3)
-        for m in range(n + 1)
+        Spreading(place, wire, m, spots, shards[m], proj_v if m == 0 else wholes[m - 1], *way)
+        for m, way in enumerate(((0, 3), (6, 0), (1, 3), (1, 3)))
     ]
 
     def local(i, src, dst):
@@ -223,11 +267,22 @@
         found = []
         for k in range(1, Y):
             to = (p + k) % Y
-            piece = src if what == "vec" else src.at[to]
-            found.append(
-                wire.copy((what, "y", k), piece, dst.at[p, c], place.device(z, x, to, c))
-            )
+            device = place.device(z, x, to, c)
+            if what == "tok":
+                for i in range(ROW_PARTS):
+                    rows = slice(i * T // ROW_PARTS, (i + 1) * T // ROW_PARTS)
+                    found.append(
+                        wire.copy(
+                            (what, "y", k, i), src.at[to, rows], dst.at[p, c, rows], device
+                        )
+                    )
+            else:
+                piece = src if what == "vec" else src.at[to]
+                found.append(wire.copy((what, "y", k), piece, dst.at[p, c], device))
         return found
+
+    def send_tokens(i):
+        start_all(along_y(*row_parts[2])[i::ROW_PARTS])
 
     def to_sibling_own(what, src, dst):
         piece = src if what == "vec" else src.at[p]
@@ -245,12 +300,13 @@
     for q in range(Y):
         tag[q] = jnp.broadcast_to(tags[q : q + 1, :], tag.shape[1:])
     greet(place, partners_of(place))
-    for part in row_parts:
-        start_all(along_y(*part))
+    start_all(along_y(*row_parts[0]))
     for part in row_parts:
         to_sibling_own(*part).start()
     for flow in flows:
-        start_all(flow.zero())
+        flow.begin()
+    start_all(along_y(*row_parts[1]))
+    send_tokens(0)
     kept = [local(m, shards[m], flows[m].whole.at[p, c, z, x]) for m in range(n + 1)]
     kept += [
         local(n + 1, vec_in, vec_v.at[p, c]),
@@ -272,9 +328,16 @@
         n_v[rows, :] = low
         nT[:, lane((q * C + i) * T, T)] = low.T
 
-    def begin_one(m):
-        kept[m].wait()
-        flows[m].go_one()
+    waited = set()
+
+    def own_shard(m):
+        if m not in waited:
+            kept[m].wait()
+            waited.add(m)
+
+    def advance(m, group, number):
+        own_shard(m)
+        flows[m].step(group, number)
 
     def vector_pass():
         arrive_all(along_y(*row_parts[0]))
@@ -321,7 +384,7 @@
             begin[:, b * T : (b + 1) * T] = jnp.where(t < 0, position, first)
 
     def weight_columns():
-        arrive_all(flows[0].three())
+        flows[0].arrive()
         r, w = proj_v.shape[4:]
         for mine in range(C):
 
@@ -346,7 +409,10 @@
             return nothing
 
         lax.fori_loop(0, nq, project, 0)
-        vT[...] = pv[:, 2 * H :].T
+        values = pv[:, 2 * H :].T
+        for h in range(2 * pairs):
+            vT[h, 0:HEAD_DIM, :] = values[h * HEAD_DIM : (h + 1) * HEAD_DIM, :]
+            vT[h, HEAD_DIM:, :] = jnp.ones((16, L), bf16)
         start_all(saves[2:])
 
     scale = HEAD_DIM ** (-0.5) * LOG2E
@@ -373,10 +439,11 @@
         "J": project_all,
     }
     for m, name in enumerate("POUD"):
-        acts[name + "1"] = functools.partial(begin_one, m)
-        acts[name + "2a"] = flows[m].go_two_low
-        acts[name + "2b"] = flows[m].go_two_high
-        acts[name + "3"] = flows[m].go_three
+        for group, letter in enumerate("dab"):
+            for number in (1, 2, 3):
+                acts[f"{name}{number}{letter}"] = functools.partial(advance, m, group, number)
+    for i in range(1, ROW_PARTS):
+        acts[f"t{i}"] = functools.partial(send_tokens, i)
     events, spot = {}, None
     for name in FORWARD_PLAN:
         if name[0] == "S":
@@ -388,42 +455,53 @@
     for qi in range(nq):
         qs = slice(qi * BQ, (qi + 1) * BQ)
         d0 = qi * BQ
-        if qi == nq - 1:
-            cuts = [(0, d0, 1)] if d0 else []
-        elif d0 > 256:
-            cuts = [(0, 256, 1), (256, d0, 0)]
-        else:
-            cuts = [(0, d0, 1)] if d0 else []
-        cuts.append((d0, d0 + BQ, 2))
+        part = BQ // 2
+        cuts = []
+        if d0 and qi < nq - 1:
+            cuts = [(0, part, 1, 0), (part, min(BQ, d0), 0, 0)]
+            cuts += [(a, a + BQ, 0, 0) for a in range(BQ, d0, BQ)]
+        elif d0:
+            cuts = [(a, a + BQ, 1, 0) for a in range(0, d0, BQ)]
+        cuts += [(d0, d0 + part, 2, 0), (d0 + part, d0 + BQ, 2, part)]
+
+        def widened(value, qa, blank):
+            if not qa:
+                return value
+            return jnp.concatenate([jnp.full((value.shape[0], qa), blank, f32), value], axis=1)
 
         def one_pair(pair, nothing):
             cols = lane(pair * 128, 128)
             k_cols = lane(H + pair * 128, 128)
             qT = pv[qs, cols].T
-            found = []
+            found, scores = [], []
             for h in range(2):
                 query = head_masked(qT, h, 0)
-                rows = pl.ds(pl.multiple_of(pair * 128 + h * HEAD_DIM, HEAD_DIM), HEAD_DIM)
                 parts = []
-                for a, b, mode in cuts:
-                    s = dot(pv[a:b, k_cols], query, 1, 0) * scale
+                for a, b, mode, qa in cuts:
+                    s = dot(pv[a:b, k_cols], query[:, qa:], 1, 0)
                     if mode:
-                        key_pos = lax.broadcasted_iota(jnp.int32, (b - a, BQ), 0) + a
-                        visible = key_pos >= begin[:, qs]
+                        shape = (b - a, BQ - qa)
+                        key_pos = lax.broadcasted_iota(jnp.int32, shape, 0) + a
+                        visible = key_pos >= begin[:, d0 + qa : d0 + BQ]
                         if mode == 2:
-                            query_pos = lax.broadcasted_iota(jnp.int32, (b - a, BQ), 1) + d0
+                            query_pos = lax.broadcasted_iota(jnp.int32, shape, 1) + d0 + qa
                             visible = jnp.logical_and(visible, key_pos <= query_pos)
                         s = jnp.where(visible, s, masked)
                     parts.append(s)
-                top = functools.reduce(
-                    jnp.maximum, [jnp.max(s, axis=0, keepdims=True) for s in parts]
-                )
-                total, accum = 0.0, 0.0
-                for (a, b, mode), s in zip(cuts, parts):
-                    e = jnp.exp2(s - top)
-                    total = total + jnp.sum(e, axis=0, keepdims=True)
-                    accum = accum + dot(vT[rows, a:b], e.astype(bf16), 1, 0)
-                result = accum / total
+                scores.append(parts)
+            for h in range(2):
+                tops = [
+                    widened(jnp.max(s, axis=0, keepdims=True), cut[3], masked)
+                    for cut, s in zip(cuts, scores[h])
+                ]
+                top = functools.reduce(jnp.maximum, tops) * scale
+                accum = jnp.zeros((vT.shape[1], BQ), f32)
+                for (a, b, mode, qa), s in zip(cuts, scores[h]):
+                    e = jnp.exp2(s * scale - top[:, qa:]).astype(bf16)
+                    accum = accum + widened(dot(vT[pair * 2 + h, :, a:b], e, 1, 0), qa, 0.0)
+                total = accum[HEAD_DIM : HEAD_DIM + 1]
+                result = accum[:HEAD_DIM] / total
+                rows = pl.ds(pl.multiple_of(pair * 128 + h * HEAD_DIM, HEAD_DIM), HEAD_DIM)
                 oT[rows, qs] = result
                 found.append(result)
                 lt[pair, h : h + 1, qs] = top + jnp.log2(total)
@@ -439,6 +517,9 @@
             return nothing
 
         lax.fori_loop(0, pairs, one_pair, 0)
+        save = local(n + 9 + Y + qi, oT.at[:, qs], oT_out.at[:, qs])
+        save.start()
+        saves.append(save)
         for owner, keep, send in block_copies(qi):
 
             @pl.when(owner == c)
@@ -449,10 +530,8 @@
             def _():
                 send.start()
 
-    last = local(n + 9 + Y, oT, oT_out)
-    last.start()
     for flow in flows[1:]:
-        arrive_all(flow.three())
+        flow.arrive()
     for qi in range(nq):
         for owner, keep, send in block_copies(qi):
 
@@ -474,7 +553,7 @@
         leave_all(to_sibling(what, dst))
     for flow in flows:
         flow.leave()
-    for copy in saves + [last]:
+    for copy in saves:
         copy.wait()
 
 
@@ -501,8 +580,8 @@
         jax.ShapeDtypeStruct((H, L), f32),
         jax.ShapeDtypeStruct((pairs, 2, L), f32),
     ]
-    each = (Z - 1) + 2 * Y + 1
-    copies = (n + 1) * each + 3 * (2 * (Y - 1) + 1) + Y
+    each = 3 * (Z - 1) + 3 * (Y - 1) + 6
+    copies = (n + 1) * each + 3 * (2 * (Y - 1) + 1) + ROW_PARTS * (Y - 1) + Y
     scratch = [
         pltpu.VMEM((Y, C, Z, X) + shards[0].shape, bf16),
         pltpu.VMEM((Y, C, T, D), bf16),
@@ -513,12 +592,12 @@
         pltpu.VMEM((D, L), bf16),
         pltpu.VMEM((D, W3), bf16),
         pltpu.VMEM((L, W3), bf16),
-        pltpu.VMEM((H, L), bf16),
+        pltpu.VMEM((H // HEAD_DIM, HEAD_DIM + 16, L), bf16),
         pltpu.VMEM((L, H), bf16),
         pltpu.VMEM((H, L), f32),
         pltpu.SemaphoreType.DMA((copies,)),
         pltpu.SemaphoreType.DMA((copies,)),
-        pltpu.SemaphoreType.DMA((n + 10 + Y,)),
+        pltpu.SemaphoreType.DMA((n + 9 + Y + L // BQ,)),
     ]
     return pl.pallas_call(
         functools.partial(forward_kernel, place, n, BQ),
@@ -531,6 +610,10 @@
         ),
         name="forward",
     )(*shards, tok, segments, present, vec_in)
+
+
+def sixths(rows, count):
+    return rows if count == 6 else 0 if count == 0 else max(16, 16 * (rows * count // 96))
 
 
 class Summing:
@@ -583,8 +666,8 @@
         z, x, p, c = self.spots
         place = self.place
         found = []
-        for k in range(1, place.Z):
-            to = (z + k) % place.Z
+        for k in place.across_z():
+            to = place.mirror(z, k)
             found.append(
                 self.wire.copy(
                     (self.name, "z", k),
@@ -665,11 +748,11 @@
         return [
             self.wire.copy(
                 (self.name, "z", k),
-                self.acc.at[:, (z + k) % place.Z],
+                self.acc.at[:, place.mirror(z, k)],
                 self.zr.at[k - 1],
-                place.device((z + k) % place.Z, x, p, c),
+                place.device(place.mirror(z, k), x, p, c),
             )
-            for k in range(1, place.Z)
+            for k in place.across_z()
         ]
 
     def two(self):
@@ -749,11 +832,11 @@
         return [
             self.wire.copy(
                 (self.name, "z", k),
-                self.acc.at[(z + k) % place.Z, x],
+                self.acc.at[place.mirror(z, k), x],
                 self.zr.at[k - 1],
-                place.device((z + k) % place.Z, x, p, c),
+                place.device(place.mirror(z, k), x, p, c),
             )
-            for k in range(1, place.Z)
+            for k in place.across_z()
         ]
 
     def along_y(self):
@@ -871,16 +954,19 @@
     def out_fetch(pair):
         return local(2, oT_in.at[line(pair * 128, 128), :], oT)
 
-    loads = [local(0, proj, pv), local(1, grad_in, do), local(3, w_in, wv)]
+    loads = [local(0, proj, pv), local(1, grad_in, do)]
+    columns = local(3, w_in, wv)
     late = local(4 + 2 * n, normedT, nT)
     halves = [
         (local(4 + m, parts[m], adds[m].acc), local(4 + n + m, others[m], landing[m]))
         for m in range(n)
     ]
-    for m in (1, 2, 0):
+    start_all(halves[1])
+    start_all(loads)
+    out_fetch(0).start()
+    for m in (2, 0):
         start_all(halves[m])
-    start_all(loads + [late])
-    out_fetch(0).start()
+    start_all([late, columns])
     greet(place, partners_of(place))
     row_sem = 5 + 2 * n
 
@@ -946,6 +1032,8 @@
         )
 
     def block_done(qi):
+        if qi == nq - 1:
+            columns.wait()
         g = dot(pv[line(qi * BQ, BQ), :], wv[...], 1, 1)
         for u, q, owner in sub_blocks(qi):
             rows = slice(u * T, (u + 1) * T)
@@ -960,6 +1048,8 @@
                 g_wire(q).start()
 
     def pair_done(i):
+        if i == 0:
+            late.wait()
         wide = [pv[:, t * H + i * 128 : t * H + (i + 1) * 128] for t in range(3)]
         value = dot(nT[...], jnp.concatenate(wide, axis=1), 1, 0).astype(bf16)
         chunk = chunks[i]
@@ -1046,8 +1136,8 @@
     v_core = wire.copy("vc", v0, vc, sibling)
     v_x = wire.copy("vx", v1, vx, beside)
     v_z = [
-        wire.copy(("vz", k), v2, vz.at[k - 1], place.device((z + k) % Z, x, p, c))
-        for k in range(1, Z)
+        wire.copy(("vz", k), v2, vz.at[k - 1], place.device(place.mirror(z, k), x, p, c))
+        for k in place.across_z()
     ]
     v_y = [
         wire.copy(("vy", k), v3, vy.at[k - 1], place.device(z, x, (p + k) % Y, c))
@@ -1161,7 +1251,6 @@
 
     for name in events.get(None, ()):
         acts[name]()
-    late.wait()
     lax.fori_loop(0, pairs, one_pair, 0)
     for name in events[pairs - 1, nq - 1]:
         acts[name]()

time: 269 us -> 251 us (0.933)
  Pallas kernels: 262 us -> 243 us
    pallas_call x1, Pallas kernels: 98.5 us -> 86.4 us  [forward(): pl.pallas_call(functools.partial(forward_kernel, place, n, BQ), out_shape...]
    pallas_call x1, Pallas kernels: 104 us -> 96.9 us  [backward(): pl.pallas_call(functools.partial(backward_kernel, place, n, BQ), out_shap...]
where the time goes in v5:
time: 251 us; the launch traced here: 247 us
  Pallas kernels  243 us (97%)
    pallas_call x1, Pallas kernels, backward(): pl.pallas_call(functools.partial(backward_kernel, place, n, BQ), out_shap...  96.9 us
    pallas_call x1, Pallas kernels, forward(): pl.pallas_call(functools.partial(forward_kernel, place, n, BQ), out_shape...  86.4 us
    pallas_call x1, Pallas kernels, dense(): pl.pallas_call(functools.partial(dense_kernel, place, aligned), out_shape...  55.1 us

profile of v5, /device:TPU:0, one launch (start us, length us, event | category | flops | bytes accessed | tf_op | source)
XLA Modules:
  0.0 246.8 jit_solution(4511690837862630419)
XLA Ops:
  0.7 1.4 select_select_fusion.refs_7_
  2.1 86.4 %forward.1 = (bf16[2,2,4,2,96,192]{5,4,3,2,1,0:T(8,128)(2,1)}, bf16[2,2,4,2,96,768]{5,4,3,2,1,0:T(8,128)(2,1)}, bf16[2,2,4,2,192,384]{5,4,3,2,1,0:T(8,128)(2,1)}...) custom-call(bf16[96,576]{1,0:T(8,128)(2,1)} %refs_0_.1, ...), custom_call_target="tpu_custom_call" | custom-call | tf_op jit(solution)/shard_map/forward/pallas_call | solution.py:602
  88.4 55.1 %dense.1 = (bf16[2,512,768]{2,1,0:T(8,128)(2,1)}, f32[1024,768]{1,0:T(8,128)}, bf16[2048,384]{1,0:T(8,128)(2,1)}, bf16[2,768,768]{2,1,0:T(8,128)(2,1)}, bf16[2,8...) custom-call(bf16[1024,768]{1,0:T(8,128)(2,1)} %get-tuple-element.45., ...), custom_call_target="tpu_custom_call" | custom-call | tf_op jit(solution)/shard_map/dense/pallas_call | solution.py:1660
  143.5 96.9 %backward.1 = (f32[96,576]{1,0:T(8,128)}, f32[96,192]{1,0:T(8,128)}, f32[96,768]{1,0:T(8,128)}, f32[192,384]{1,0:T(8,128)}, f32[8,384]{1,0:T(8,128)}, /*index=5*/bf16[2,512,768]{2,1,0:T(8,128)(2,1)}) custom-call(s32[1,2048]{1,0:T(1,128)} %get-tuple-element.52.refs_0_, bf16[2048,1152]{1,0:T(8,128)(2,1)} %get-tuple-element.53.refs_1_, ...), custom_call_target="tpu_custom_call" | custom-call | tf_op jit(solution)/shard_map/backward/pallas_call | solution.py:1353
  240.4 4.8 %hand_over.1 = (bf16[2,512,768]{2,1,0:T(8,128)(2,1)}, bf16[2,512,768]{2,1,0:T(8,128)(2,1)}, f32[96,576]{1,0:T(8,128)}, f32[96,192]{1,0:T(8,128)}, f32[96,768]{1,...) custom-call(bf16[2,512,768]{2,1,0:T(8,128)(2,1)} %get-tuple-element.51.refs_0_, ...), custom_call_target="tpu_custom_call" | custom-call | tf_op jit(solution)/shard_map/hand_over/pallas_call | solution.py:1739
  245.2 1.4 fusion
  (2 shorter events, 0.0 us)

commit v6 on v5

--- a/solution.py
+++ b/solution.py
@@ -957,6 +957,7 @@
     loads = [local(0, proj, pv), local(1, grad_in, do)]
     columns = local(3, w_in, wv)
     late = local(4 + 2 * n, normedT, nT)
+    columns_here = []
     halves = [
         (local(4 + m, parts[m], adds[m].acc), local(4 + n + m, others[m], landing[m]))
         for m in range(n)
@@ -1032,8 +1033,9 @@
         )
 
     def block_done(qi):
-        if qi == nq - 1:
+        if not columns_here:
             columns.wait()
+            columns_here.append(True)
         g = dot(pv[line(qi * BQ, BQ), :], wv[...], 1, 1)
         for u, q, owner in sub_blocks(qi):
             rows = slice(u * T, (u + 1) * T)
@@ -1429,43 +1431,15 @@
         tasks.append(Task(wire.copy(name, src, dst, device), True))
         return tasks[-1]
 
-    first = [load(att, att_v), load(tok, tok_v), load(out_w, out_v)]
-    first.append(load(cot.at[p], cot_v.at[line(p * T, T), :]))
-    if aligned:
-        w = up_w.shape[2]
-        weights = [load(up_w.at[d], up_v.at[:, d * w : (d + 1) * w]) for d in range(S)]
-        r, w = down_w.shape[2:]
-        weights += [
-            load(down_w.at[d, b], down_v.at[d * r : (d + 1) * r, b * w : (b + 1) * w])
-            for d in range(S)
-            for b in range(nb)
-        ]
-    else:
-        weights = [load(up_w, up_v), load(down_w, down_v)]
-    greet(place, others + [sibling])
-    cots = []
-    for k in range(1, Y):
-        to = (p + k) % Y
-        cots.append(send(("cot", k), cot.at[to], cot_v.at[line(p * T, T), :], others[k - 1]))
-    for task in first:
-        task.gone()
-    w = out_v.shape[2]
-    for d in range(S):
-        out_full[:, d * w : (d + 1) * w] = out_v[d]
-    gain, shift = vec[2:3, :], vec[3:4, :]
-    near = (p * T) // half
+    per_half = half // T
+    near = p // per_half
     halves = [1 - near, near]
-    rows_of = [line(t * half, half) for t in halves]
-    for t in (0, 1):
-        ts = rows_of[t]
-        middle = tok_v[ts, :].astype(f32) + dot(att_v[ts, :], out_full[...], 1, 0)
-        unit, factor = normed(middle)
-        mid[ts, :] = middle
-        low = (unit * gain + shift).astype(bf16)
-        n2[ts, :] = low
-        n2T[:, lane(halves[t] * half, half)] = low.T
-    for task in weights:
-        task.gone()
+    rows_of = [slice(0, half), slice(half, M)]
+
+    def spot_of(q, chip):
+        apart = q // per_half - chip // per_half
+        return (1 - apart * apart) * half + q % per_half * T
+
     w_up = up_own.shape[2]
     in_chunk = D // w_up
     chunks = []
@@ -1475,8 +1449,53 @@
         else:
             chunks.append(s)
 
+    first = [load(out_w, out_v)]
+    for t in (0, 1):
+        there = line(halves[t] * half, half)
+        first += [load(att.at[there], att_v.at[rows_of[t]]), load(tok.at[there], tok_v.at[rows_of[t]])]
+    first.append(load(cot.at[p], cot_v.at[line(spot_of(p, p), T), :]))
+    if aligned:
+        weights = []
+        r, w = down_w.shape[2:]
+        for s in range(J):
+            for i in range(in_chunk):
+                at = s * D + i * w_up
+                weights.append(load(up_w.at[chunks[s] * in_chunk + i], up_v.at[:, at : at + w_up]))
+            for i in range(D // w):
+                at = s * D + i * w
+                weights += [
+                    load(
+                        down_w.at[d, chunks[s] * (D // w) + i],
+                        down_v.at[d * r : (d + 1) * r, at : at + w],
+                    )
+                    for d in range(S)
+                ]
+    else:
+        weights = [load(up_w, up_v), load(down_w, down_v)]
+    greet(place, others + [sibling])
+    cots = []
+    for k in range(1, Y):
+        to = (p + k) % Y
+        dst = cot_v.at[line(spot_of(p, to), T), :]
+        cots.append(send(("cot", k), cot.at[to], dst, others[k - 1]))
+    for task in first:
+        task.gone()
+    w = out_v.shape[2]
+    for d in range(S):
+        out_full[:, d * w : (d + 1) * w] = out_v[d]
+    gain, shift = vec[2:3, :], vec[3:4, :]
+    for t in (0, 1):
+        ts = rows_of[t]
+        middle = tok_v[ts, :].astype(f32) + dot(att_v[ts, :], out_full[...], 1, 0)
+        unit, factor = normed(middle)
+        mid[ts, :] = middle
+        low = (unit * gain + shift).astype(bf16)
+        n2[ts, :] = low
+        n2T[:, ts] = low.T
+    for task in weights:
+        task.gone()
     def cols(s):
-        return lane(chunks[s] * D, D)
+        return slice(s * D, (s + 1) * D)
 
     busy = {}
 
@@ -1529,23 +1548,54 @@
     units = [(0, "f", s) for s in range(J)] + [(1, "fb", s) for s in range(J)]
     units += [(0, "b", s) for s in range(J)]
 
-    def ahead(number):
+    W = D
+
+    def part_of(s, i):
+        return slice(s * D + i * W, s * D + (i + 1) * W)
+
+    def enter(number, i):
         t, kind, s = units[number]
-        slot = number % 2
+        mine = slice(i * W, (i + 1) * W)
         if "f" in kind:
-            h_buf[slot] = dot(n2[rows_of[t], :], up_v[:, cols(s)], 1, 0)
+            h_buf[number % 2, :, mine] = dot(n2[rows_of[t], :], up_v[:, part_of(s, i)], 1, 0)
         if "b" in kind:
-            g_buf[slot] = dot(cot_v[rows_of[t], :], down_v[:, cols(s)], 1, 0)
+            g_buf[number % 2, :, mine] = dot(cot_v[rows_of[t], :], down_v[:, part_of(s, i)], 1, 0)
+
+    def activate(number, i):
+        t, kind, s = units[number]
+        ts, mine, place_here = rows_of[t], slice(i * W, (i + 1) * W), part_of(s, i)
+        if "f" in kind:
+            a, slope = gelu_both(h_buf[number % 2, :, mine])
+            act[ts, place_here] = a.astype(bf16)
+            if kind == "f":
+                gh[ts, place_here] = slope.astype(bf16)
+        else:
+            slope = gh[ts, place_here].astype(f32)
+        if "b" in kind:
+            gh[ts, place_here] = (g_buf[number % 2, :, mine] * slope).astype(bf16)
+
+    def leave(number, i):
+        t, kind, s = units[number]
+        ts, mine = rows_of[t], slice(i * W, (i + 1) * W)
+        wanted = []
+        if "f" in kind:
+            wanted.append((oacc, act, down_v))
+        if "b" in kind:
+            wanted.append((g2, gh, up_v))
+        for total, left, right in wanted:
+            more = dot(left[ts, cols(s)], right[mine, cols(s)], 1, 1)
+            if s == 0:
+                total[:, mine] = more
+            else:
+                total[:, mine] += more
 
     def output_rows(t):
         ts = rows_of[t]
         tok_v[ts, :] = (mid[ts, :] + oacc[...]).astype(bf16)
-        for i in range(half // T):
-            q = halves[t] * (half // T) + i
-            if Y == 2 and t == 1:
-                store(tok_v.at[ts, :], home.at[q])
-            elif Y == 2:
-                send("home", tok_v.at[ts, :], home.at[p], others[0])
+        if Y == 2 and t == 1:
+            store(tok_v.at[ts, :], home.at[near])
+        elif Y == 2:
+            send("home", tok_v.at[ts, :], home.at[p], others[0])
 
     sums = [jnp.zeros((1, D), f32), jnp.zeros((1, D), f32)]
 
@@ -1560,61 +1610,49 @@
         low = gm.astype(bf16)
         n2[ts, :] = low
         cot_v[ts, :] = dot(low, out_full[...], 1, 1).astype(bf16)
-        store(mid.at[ts, :], gm_out.at[ts, :])
-        for i in range(half // T):
-            q = halves[t] * (half // T) + i
-            rows = line(q * T, T)
+        store(mid.at[ts, :], gm_out.at[line(halves[t] * half, half), :])
+        for i in range(per_half):
+            q = halves[t] * per_half + i
+            rows = slice(t * half + i * T, t * half + (i + 1) * T)
             spot = line((C * q + c) * T, T)
             store(cot_v.at[rows, lane(c * H, H)], heads.at[spot, :])
             send(("ga", t, i), cot_v.at[rows, lane((1 - c) * H, H)], heads.at[spot, :], sibling)
 
-    ahead(0)
-    for number, (t, kind, s) in enumerate(units):
-        ts, slot = rows_of[t], number % 2
-        if number + 1 < len(units):
-            if units[number + 1] == ((0, "b", 0) if Y == 2 else (1, "fb", 0)):
+    count = len(units)
+    for number in range(count + 2):
+        if number < count:
+            t, kind, s = units[number]
+            if units[number] == ((0, "b", 0) if Y == 2 else (1, "fb", 0)):
                 for task in cots:
                     task.came()
-            ahead(number + 1)
-        if "f" in kind:
-            a, slope = gelu_both(h_buf[slot])
-            a = a.astype(bf16)
-            act[ts, cols(s)] = a
-            more = dot(a, down_v[:, cols(s)], 1, 1)
-            if s == 0:
-                oacc[...] = more
-            else:
-                oacc[...] += more
-            if kind == "f":
-                gh[ts, cols(s)] = slope.astype(bf16)
-        else:
-            slope = gh[ts, cols(s)].astype(f32)
-        if "b" in kind:
-            b = (g_buf[slot] * slope).astype(bf16)
-            gh[ts, cols(s)] = b
-            more = dot(b, up_v[:, cols(s)], 1, 1)
-            if s == 0:
-                g2[...] = more
-            else:
-                g2[...] += more
-        if kind == "b":
-            up_gradient(s)
-            down_gradient(s)
+        for i in range(D // W):
+            if number < count:
+                enter(number, i)
+            if 0 <= number - 1 < count:
+                activate(number - 1, i)
+            if 0 <= number - 2:
+                leave(number - 2, i)
+        if number < 2:
+            continue
+        t, kind, s = units[number - 2]
         if s == J - 1:
             if kind == "f":
                 output_rows(t)
             elif kind == "fb":
                 output_rows(t)
-                cotT[:, lane(halves[t] * half, half)] = cot_v[ts, :].T
+                cotT[:, rows_of[t]] = cot_v[rows_of[t], :].T
                 norm_rows(t)
-                cotT[:, lane(halves[0] * half, half)] = cot_v[rows_of[0], :].T
+                cotT[:, rows_of[0]] = cot_v[rows_of[0], :].T
             else:
                 norm_rows(t)
+        if kind == "b":
+            up_gradient(s)
+            down_gradient(s)
     if Y > 2:
-        store(tok_v.at[line(p * T, T), :], home.at[p])
+        store(tok_v.at[line(spot_of(p, p), T), :], home.at[p])
         for k in range(1, Y):
             to = (p + k) % Y
-            send(("home", k), tok_v.at[line(to * T, T), :], home.at[p], others[k - 1])
+            send(("home", k), tok_v.at[line(spot_of(to, p), T), :], home.at[p], others[k - 1])
     vec_out[0:1, :] = sums[0]
     vec_out[1:2, :] = sums[1]
     value = dot(att_v[...], n2[...], 0, 0).astype(bf16)
@@ -1708,25 +1746,38 @@
 
 
 def hand_over_kernel(place, n, *refs):
-    given, vec, out, vec_out = refs[:n], refs[n], refs[n + 1 : 2 * n + 1], refs[2 * n + 1]
-    whole, between, sem = refs[2 * n + 2], refs[2 * n + 3 : 3 * n + 3], refs[3 * n + 3]
-    here = [pltpu.make_async_copy(given[i], between[i], sem.at[0, i]) for i in range(n)]
-    away = [pltpu.make_async_copy(between[i], out[i], sem.at[1, i]) for i in range(n)]
+    given, vec, out, vec_out = refs[:n], refs[n], refs[n + 1 : 2 * n + 1], refs[2 * n + 1 : 2 * n + 5]
+    whole, between, sem = refs[2 * n + 5], refs[2 * n + 6 : 3 * n + 6], refs[3 * n + 6]
+    pieces = []
+    for i in range(n):
+        if len(given[i].shape) == 3:
+            R, T, _ = given[i].shape
+            cut = [(r, slice(h * T // 2, (h + 1) * T // 2)) for r in range(R) for h in range(2)]
+        else:
+            cut = [slice(None)]
+        pieces += [(given[i].at[k], between[i].at[k], out[i].at[k]) for k in cut]
+    here = [
+        pltpu.make_async_copy(src, mid, sem.at[0, j]) for j, (src, mid, dst) in enumerate(pieces)
+    ]
+    away = [
+        pltpu.make_async_copy(mid, dst, sem.at[1, j]) for j, (src, mid, dst) in enumerate(pieces)
+    ]
     start_all(here)
     H = vec.shape[1]
     whole[0:4, 0:H] = vec[0:4, :]
     whole[0:4, H:] = vec[4:8, :]
     me = lax.axis_index("blk")
-    w = vec_out.shape[1]
+    w = vec_out[0].shape[1]
     for d in range(place.blk):
 
         @pl.when(me == d)
         def _():
-            vec_out[...] = whole[0:4, d * w : (d + 1) * w]
-
-    for i in range(n):
-        here[i].wait()
-        away[i].start()
+            for i in range(4):
+                vec_out[i][...] = whole[i : i + 1, d * w : (d + 1) * w]
+
+    for come, go in zip(here, away):
+        come.wait()
+        go.start()
     for copy in away:
         copy.wait()
 
@@ -1736,15 +1787,16 @@
     anywhere = pl.BlockSpec(memory_space=pl.ANY)
     inside = pl.BlockSpec(memory_space=pltpu.VMEM)
     H = vec.shape[1]
+    count = sum(2 * v.shape[0] if len(v.shape) == 3 else 1 for v in given)
     return pl.pallas_call(
         functools.partial(hand_over_kernel, place, n),
         out_shape=[jax.ShapeDtypeStruct(v.shape, v.dtype) for v in given]
-        + [jax.ShapeDtypeStruct((4, 2 * H // place.blk), f32)],
+        + [jax.ShapeDtypeStruct((1, 2 * H // place.blk), f32)] * 4,
         in_specs=[anywhere] * n + [inside],
-        out_specs=[anywhere] * n + [inside],
+        out_specs=[anywhere] * n + [inside] * 4,
         scratch_shapes=[pltpu.VMEM((8, 2 * H), f32)]
         + [pltpu.VMEM(v.shape, v.dtype) for v in given]
-        + [pltpu.SemaphoreType.DMA((2, n))],
+        + [pltpu.SemaphoreType.DMA((2, count))],
         compiler_params=pltpu.CompilerParams(vmem_limit_bytes=62 << 20),
         name="hand_over",
     )(*given, vec)
@@ -1838,7 +1890,7 @@
         vec,
         vec_two,
     )
-    output, token_grad, proj_sum, out_sum, up_sum, down_sum, vectors = hand_over(
+    output, token_grad, proj_sum, out_sum, up_sum, down_sum, *vectors = hand_over(
         place, (output, token_grad, proj_sum, out_sum, up_sum, down_sum), vec_sum
     )
     return (
@@ -1848,10 +1900,10 @@
         out_sum,
         up_sum,
         down_sum.T,
-        vectors[0],
-        vectors[1],
-        vectors[2],
-        vectors[3],
+        vectors[0].reshape(-1),
+        vectors[1].reshape(-1),
+        vectors[2].reshape(-1),
+        vectors[3].reshape(-1),
     )
 
 

time: 251 us -> 248 us (0.988)
  no operation moved by 1% of the time
where the time goes in v6:
time: 248 us; the launch traced here: 244 us
  Pallas kernels  242 us (98%)
    pallas_call x1, Pallas kernels, backward(): pl.pallas_call(functools.partial(backward_kernel, place, n, BQ), out_shap...  97.4 us
    pallas_call x1, Pallas kernels, forward(): pl.pallas_call(functools.partial(forward_kernel, place, n, BQ), out_shape...  86.4 us
    pallas_call x1, Pallas kernels, dense(): pl.pallas_call(functools.partial(dense_kernel, place, aligned), out_shape...  53.3 us

profile of v6, /device:TPU:0, one launch (start us, length us, event | category | flops | bytes accessed | tf_op | source)
XLA Modules:
  0.0 244.3 jit_solution(10930725298675407994)
XLA Ops:
  0.7 1.4 select_select_fusion.refs_7_
  2.1 86.4 %forward.1 = (bf16[2,2,4,2,96,192]{5,4,3,2,1,0:T(8,128)(2,1)}, bf16[2,2,4,2,96,768]{5,4,3,2,1,0:T(8,128)(2,1)}, bf16[2,2,4,2,192,384]{5,4,3,2,1,0:T(8,128)(2,1)}...) custom-call(bf16[96,576]{1,0:T(8,128)(2,1)} %refs_0_.1, ...), custom_call_target="tpu_custom_call" | custom-call | tf_op jit(solution)/shard_map/forward/pallas_call | solution.py:602
  88.4 53.3 %dense.1 = (bf16[2,512,768]{2,1,0:T(8,128)(2,1)}, f32[1024,768]{1,0:T(8,128)}, bf16[2048,384]{1,0:T(8,128)(2,1)}, bf16[2,768,768]{2,1,0:T(8,128)(2,1)}, bf16[2,8...) custom-call(bf16[1024,768]{1,0:T(8,128)(2,1)} %get-tuple-element.48., ...), custom_call_target="tpu_custom_call" | custom-call | tf_op jit(solution)/shard_map/dense/pallas_call | solution.py:1698
  141.8 97.4 %backward.1 = (f32[96,576]{1,0:T(8,128)}, f32[96,192]{1,0:T(8,128)}, f32[96,768]{1,0:T(8,128)}, f32[192,384]{1,0:T(8,128)}, f32[8,384]{1,0:T(8,128)}, /*index=5*/bf16[2,512,768]{2,1,0:T(8,128)(2,1)}) custom-call(s32[1,2048]{1,0:T(1,128)} %get-tuple-element.55.refs_0_, bf16[2048,1152]{1,0:T(8,128)(2,1)} %get-tuple-element.56.refs_1_, ...), custom_call_target="tpu_custom_call" | custom-call | tf_op jit(solution)/shard_map/backward/pallas_call | solution.py:1355
  239.2 4.8 %hand_over.1 = (bf16[2,512,768]{2,1,0:T(8,128)(2,1)}, bf16[2,512,768]{2,1,0:T(8,128)(2,1)}, f32[96,576]{1,0:T(8,128)}, f32[96,192]{1,0:T(8,128)}, f32[96,768]{1,...) custom-call(bf16[2,512,768]{2,1,0:T(8,128)(2,1)} %get-tuple-element., ...), custom_call_target="tpu_custom_call" | custom-call | tf_op jit(solution)/shard_map/hand_over/pallas_call | solution.py:1791
  (2 shorter events, 0.0 us)

commit v7 on v6

--- a/solution.py
+++ b/solution.py
@@ -225,14 +225,14 @@
 
 
 def forward_kernel(place, n, BQ, *refs):
-    shards, (tok, segments, present, vec_in) = refs[: n + 1], refs[n + 1 : n + 5]
-    outs = refs[n + 5 :]
+    shards, (tok, segments, present) = refs[: n + 1], refs[n + 1 : n + 4]
+    vectors, outs = refs[n + 4 : n + 8], refs[n + 8 :]
     wholes = outs[:n]
     (tok_out, vec_out, begin, proj_out, w_out, normedT_out, att_out, oT_out, lt) = outs[
         n : n + 9
     ]
     (
-        proj_v, tok_v, tag, tag_v, vec_v, n_v, nT, wv, pv, vT, att, oT,
+        vec_in, proj_v, tok_v, tag, tag_v, vec_v, n_v, nT, wv, pv, vT, att, oT,
         send_sem, recv_sem, local_sem,
     ) = outs[n + 9 :]
     spots = place.here()
@@ -295,6 +295,9 @@
             found.append(wire.copy((what, "pass", k), dst.at[q, c], dst.at[q, c], sibling))
         return found
 
+    vec_in[...] = jnp.zeros_like(vec_in)
+    for i, vector in enumerate(vectors):
+        vec_in[i : i + 1, :] = vector[...].astype(f32).reshape(1, -1).astype(bf16)
     position = lax.broadcasted_iota(jnp.int32, (Y, T), 1) + (p * C + c) * T
     tags = jnp.where(present[...] == 1, segments[...], -1 - position)
     for q in range(Y):
@@ -557,7 +560,7 @@
         copy.wait()
 
 
-def forward(place, shards, tok, segments, present, vec_in):
+def forward(place, shards, tok, segments, present, vectors):
     n = len(shards) - 1
     Z, X, Y, C = place.Z, place.X, place.Y, place.C
     R, T, D = tok.shape
@@ -582,12 +585,14 @@
     ]
     each = 3 * (Z - 1) + 3 * (Y - 1) + 6
     copies = (n + 1) * each + 3 * (2 * (Y - 1) + 1) + ROW_PARTS * (Y - 1) + Y
+    vec_shape = (16, vectors[0].shape[0])
     scratch = [
+        pltpu.VMEM(vec_shape, bf16),
         pltpu.VMEM((Y, C, Z, X) + shards[0].shape, bf16),
         pltpu.VMEM((Y, C, T, D), bf16),
         pltpu.VMEM((Y, 8, T), jnp.int32),
         pltpu.VMEM((Y, C, 8, T), jnp.int32),
-        pltpu.VMEM((Y, C) + vec_in.shape, bf16),
+        pltpu.VMEM((Y, C) + vec_shape, bf16),
         pltpu.VMEM((L, D), bf16),
         pltpu.VMEM((D, L), bf16),
         pltpu.VMEM((D, W3), bf16),
@@ -602,14 +607,14 @@
     return pl.pallas_call(
         functools.partial(forward_kernel, place, n, BQ),
         out_shape=out_shape,
-        in_specs=[inside] * (n + 1) + [anywhere] + [inside] * 3,
+        in_specs=[inside] * (n + 1) + [anywhere] + [inside] * 6,
         out_specs=[anywhere] * (n + 1) + [inside] * 2 + [anywhere] * 5 + [inside],
         scratch_shapes=scratch,
         compiler_params=pltpu.CompilerParams(
             collective_id=0, has_side_effects=True, vmem_limit_bytes=60 << 20
         ),
         name="forward",
-    )(*shards, tok, segments, present, vec_in)
+    )(*shards, tok, segments, present, *vectors)
 
 
 def sixths(rows, count):
@@ -1853,10 +1858,6 @@
 ):
     rows, block, width = tokens.shape
     Y = place.Y
-    row = lax.broadcasted_iota(jnp.int32, (16, width // place.blk), 0)
-    vec_in = jnp.zeros(row.shape, bf16)
-    for i, vector in enumerate((gain_one, bias_one, gain_two, bias_two)):
-        vec_in = jnp.where(row == i, vector[None, :], vec_in)
     (
         out_g, up_g, down_g, tok_mine, vec, begin, projected, proj_own, normed_t,
         attended_low, attended_t, log_total,
@@ -1866,7 +1867,7 @@
         tokens,
         segments,
         present,
-        vec_in,
+        (gain_one, bias_one, gain_two, bias_two),
     )
     tok_mine = tok_mine.reshape(Y * block, width)
     output, grad_middle, grad_heads, own, other, vec_two = dense(

time: 248 us -> 247 us (level)
  no operation moved by 1% of the time
where the time goes in v7:
time: 247 us; the launch traced here: 243 us
  Pallas kernels  242 us (98%)
    pallas_call x1, Pallas kernels, backward(): pl.pallas_call(functools.partial(backward_kernel, place, n, BQ), out_shap...  97.6 us
    pallas_call x1, Pallas kernels, forward(): pl.pallas_call(functools.partial(forward_kernel, place, n, BQ), out_shape...  86.5 us
    pallas_call x1, Pallas kernels, dense(): pl.pallas_call(functools.partial(dense_kernel, place, aligned), out_shape...  53.4 us

profile of v7, /device:TPU:0, one launch (start us, length us, event | category | flops | bytes accessed | tf_op | source)
XLA Modules:
  0.0 243.2 jit_solution(15786364932718137619)
XLA Ops:
  0.6 86.5 %forward.1 = (bf16[2,2,4,2,96,192]{5,4,3,2,1,0:T(8,128)(2,1)}, bf16[2,2,4,2,96,768]{5,4,3,2,1,0:T(8,128)(2,1)}, bf16[2,2,4,2,192,384]{5,4,3,2,1,0:T(8,128)(2,1)}...) custom-call(bf16[96,576]{1,0:T(8,128)(2,1)} %refs_0_.1, ...), custom_call_target="tpu_custom_call" | custom-call | tf_op jit(solution)/shard_map/forward/pallas_call | solution.py:607
  87.1 53.4 %dense.1 = (bf16[2,512,768]{2,1,0:T(8,128)(2,1)}, f32[1024,768]{1,0:T(8,128)}, bf16[2048,384]{1,0:T(8,128)(2,1)}, bf16[2,768,768]{2,1,0:T(8,128)(2,1)}, bf16[2,8...) custom-call(bf16[1024,768]{1,0:T(8,128)(2,1)} %get-tuple-element.48., ...), custom_call_target="tpu_custom_call" | custom-call | tf_op jit(solution)/shard_map/dense/pallas_call | solution.py:1703
  140.5 97.6 %backward.1 = (f32[96,576]{1,0:T(8,128)}, f32[96,192]{1,0:T(8,128)}, f32[96,768]{1,0:T(8,128)}, f32[192,384]{1,0:T(8,128)}, f32[8,384]{1,0:T(8,128)}, /*index=5*/bf16[2,512,768]{2,1,0:T(8,128)(2,1)}) custom-call(s32[1,2048]{1,0:T(1,128)} %get-tuple-element.55.refs_0_, bf16[2048,1152]{1,0:T(8,128)(2,1)} %get-tuple-element.56.refs_1_, ...), custom_call_target="tpu_custom_call" | custom-call | tf_op jit(solution)/shard_map/backward/pallas_call | solution.py:1360
  238.1 4.8 %hand_over.1 = (bf16[2,512,768]{2,1,0:T(8,128)(2,1)}, bf16[2,512,768]{2,1,0:T(8,128)(2,1)}, f32[96,576]{1,0:T(8,128)}, f32[96,192]{1,0:T(8,128)}, f32[96,768]{1,...) custom-call(bf16[2,512,768]{2,1,0:T(8,128)(2,1)} %get-tuple-element., ...), custom_call_target="tpu_custom_call" | custom-call | tf_op jit(solution)/shard_map/hand_over/pallas_call | solution.py:1796
